TPU v7x, 32 devices: a whole 2x2x4 slice. The times are simulated.
32 devices in a mesh: branch: 2 (over x), mp: 2 (over y), dp: 8 (over z, core).
Axes of the slice: x: 2, y: 2, z: 4, core: 2. Of those that a mesh axis runs over, the one named last changes fastest.
Arguments:
- block_input: bfloat16 [16, 512, 2048], P('dp'), may hold values from -6 to 6
- cotangent: bfloat16 [16, 512, 2048], P('dp', None, ('branch', 'mp')), may hold values from -6 to 6
- segments: int32 [16, 512], P('dp'), may hold values from 0 to 3, never falling along the last dimension, each value on 1 to 256 neighbouring positions
- attend_gain: float32 [2048], replicated, may hold values from 0.5 to 1.5
- attend_shift: float32 [2048], replicated, may hold values from -0.8 to 0.8
- joined_weight: bfloat16 [2048, 6144], P('dp', 'mp'), may hold values from -0.125 to 0.125
- joined_bias: float32 [6144], replicated, may hold values from -0.5 to 0.5
- dense_weight: bfloat16 [2048, 2048], P(('mp', 'dp')), may hold values from -0.5 to 0.5
- dense_bias: float32 [2048], replicated, may hold values from -1.2 to 1.2
- expand_gain: float32 [2048], replicated, may hold values from 0.5 to 1.5
- expand_shift: float32 [2048], replicated, may hold values from -0.8 to 0.8
- up_weight: bfloat16 [2048, 8192], P('dp', 'mp'), may hold values from -0.125 to 0.125
- up_bias: float32 [8192], replicated, may hold values from -1.2 to 1.2
- down_weight: bfloat16 [8192, 2048], P(('mp', 'dp')), may hold values from -0.0625 to 0.0625
- down_bias: float32 [2048], replicated, may hold values from -1.2 to 1.2
Outputs:
- block_output: bfloat16 [16, 512, 2048], P('dp', None, ('branch', 'mp'))
- input_gradient: bfloat16 [16, 512, 2048], P('dp', None, ('branch', 'mp'))
- attend_gain_gradient: float32 [2048], replicated
- attend_shift_gradient: float32 [2048], replicated
- joined_weight_gradient: float32 [2048, 6144], P(('branch', 'dp'), 'mp')
- joined_bias_gradient: float32 [6144], replicated
- dense_weight_gradient: float32 [2048, 2048], P('mp', ('branch', 'dp'))
- dense_bias_gradient: float32 [2048], replicated
- expand_gain_gradient: float32 [2048], replicated
- expand_shift_gradient: float32 [2048], replicated
- up_weight_gradient: float32 [2048, 8192], P(('branch', 'dp'), 'mp')
- up_bias_gradient: float32 [8192], replicated
- down_weight_gradient: float32 [8192, 2048], P('mp', ('branch', 'dp'))
- down_bias_gradient: float32 [2048], replicated
Inputs may be any that keep to these rules, and one draw needn't show every extreme that they name: `segments`: along a row the ids never fall and each id holds 1 to 256 of the row's tokens.
All inputs are finite; a program needn't handle non-finite values.
Results may differ from a plain program's by a relative error of at most 0.0092.
Values may be sent and summed in bfloat16 or wider, within the bound.
No kernel may reach another device: no remote copies, remote signals or barrier semaphores. Data moves between devices by JAX's collectives and lax.ppermute only.
A program may use at most 576 MiB of HBM per device.

v0:
```python
import math

import jax
import jax.numpy as jnp
from jax import lax
from jax.sharding import PartitionSpec as P

HEAD = 256
ROT = 64


NEGATIVE = -1e30


def layer_norm(values, gain_vector, shift_vector):
    center = values - jnp.mean(values, axis=-1, keepdims=True)
    spread = jnp.mean(center * center, axis=-1, keepdims=True)
    return center * lax.rsqrt(spread + 1e-05) * gain_vector + shift_vector


def rotary_tables(segment_row):
    length = segment_row.shape[0]
    before = jnp.sum((segment_row[None, :] < segment_row[:, None]).astype(jnp.int32), axis=1)
    places = (jnp.arange(length, dtype=jnp.int32) - before).astype(jnp.float32)
    frequency = 10000.0 ** (-jnp.arange(0, ROT, 2).astype(jnp.float32) / ROT)
    angles = places[:, None] * frequency[None, :]
    return (jnp.cos(angles)[:, None, :], jnp.sin(angles)[:, None, :])


def allowed_pairs(segment_row):
    token_index = jnp.arange(segment_row.shape[0], dtype=jnp.int32)
    return (segment_row[:, None] == segment_row[None, :]) & (
        token_index[None, :] <= token_index[:, None]
    )


def rotate(values, cosine_table, sine_table):
    half_width = ROT // 2
    first_half = values[..., :half_width]
    second = values[..., half_width:ROT]
    return jnp.concatenate(
        [
            first_half * cosine_table - second * sine_table,
            second * cosine_table + first_half * sine_table,
            values[..., ROT:],
        ],
        axis=-1,
    )


def exact_gelu(values):
    return jax.nn.gelu(values, approximate=False)


def product(left_side, right_side):
    return jnp.dot(left_side, right_side, preferred_element_type=jnp.float32)


def contract_last(left_side, right_side):
    return lax.dot_general(
        left_side, right_side, (((1,), (1,)), ((), ())), preferred_element_type=jnp.float32
    )


def contract_first(left_side, right_side):
    return lax.dot_general(
        left_side, right_side, (((0,), (0,)), ((), ())), preferred_element_type=jnp.float32
    )


def blanks(shape_list, number_type):
    return tuple((jnp.zeros(each_shape, number_type) for each_shape in shape_list))


def fetch_attention(joined_weight, dense_weight):
    return tuple(
        (
            lax.all_gather(joined_weight, "dp", axis=0, tiled=True),
            lax.all_gather(dense_weight, "dp", axis=0, tiled=True),
        )
    )


def fetch_expand(up_weight, down_weight):
    return tuple(
        (
            lax.all_gather(up_weight, "dp", axis=0, tiled=True),
            lax.all_gather(down_weight, "dp", axis=0, tiled=True),
        )
    )


def reduce_all(grad_tuple):
    return tuple(
        (
            lax.psum_scatter(grad_tuple[0], ("branch", "dp"), scatter_dimension=0, tiled=True),
            lax.psum_scatter(grad_tuple[1], ("branch", "dp"), scatter_dimension=1, tiled=True),
            lax.psum_scatter(grad_tuple[2], ("branch", "dp"), scatter_dimension=0, tiled=True),
            lax.psum_scatter(grad_tuple[3], ("branch", "dp"), scatter_dimension=1, tiled=True),
        )
    )


def on_device(
    block_input,
    cotangent,
    segments,
    attend_gain,
    attend_shift,
    joined_weight,
    joined_bias,
    dense_weight,
    dense_bias,
    expand_gain,
    expand_shift,
    up_weight,
    up_bias,
    down_weight,
    down_bias,
):
    batches, length, model_width = block_input.shape
    column_count = model_width // (lax.axis_size("branch") * lax.axis_size("mp"))
    column_start = (
        lax.axis_index("branch") * lax.axis_size("mp") + lax.axis_index("mp")
    ) * column_count
    attention_side = lax.axis_index("branch") == 0
    model_index = lax.axis_index("mp")
    joined_columns = joined_weight.shape[1]
    hidden_columns = up_weight.shape[1]
    local_heads = joined_columns // (3 * HEAD)
    query_scale = 1.0 / math.sqrt(HEAD)
    data_count = lax.axis_size("dp")
    share_count = data_count * lax.axis_size("branch")
    joined_span = joined_bias.shape[0]
    hidden_span = up_bias.shape[0]
    slot_expand = 2 * model_width + joined_span
    slot_hidden = 4 * model_width + joined_span
    slot_output = 4 * model_width + joined_span + hidden_span
    total_span = 5 * model_width + joined_span + hidden_span
    joined_rows = joined_weight.shape[0] * data_count
    dense_rows = dense_weight.shape[0] * data_count
    up_rows = up_weight.shape[0] * data_count
    down_rows = down_weight.shape[0] * data_count
    attention_full = ((joined_rows, joined_columns), (dense_rows, model_width))
    expand_full = ((up_rows, hidden_columns), (down_rows, model_width))
    share_shapes = (
        (joined_rows // share_count, joined_columns),
        (dense_rows, model_width // share_count),
        (up_rows // share_count, hidden_columns),
        (down_rows, model_width // share_count),
    )

    def attention_pass(block_row, cotangent_full, cosine_table, sine_table, allowed):
        joined_full, dense_full = fetch_attention(joined_weight, dense_weight)
        block_float = block_row.astype(jnp.float32)
        normed_float, norm_back = jax.vjp(layer_norm, block_float, attend_gain, attend_shift)
        normed = normed_float.astype(jnp.bfloat16)
        bias_here = lax.dynamic_slice_in_dim(
            joined_bias, model_index * joined_columns, joined_columns
        )
        joined_raw = (product(normed, joined_full) + bias_here).reshape(
            length, local_heads, 3, HEAD
        )

        def turned(query_raw, key_raw):
            return (
                rotate(query_raw, cosine_table, sine_table) * query_scale,
                rotate(key_raw, cosine_table, sine_table),
            )

        (query_float, key_float), turn_back = jax.vjp(
            turned, joined_raw[:, :, 0], joined_raw[:, :, 1]
        )
        queries = query_float.astype(jnp.bfloat16)
        keyset = key_float.astype(jnp.bfloat16)
        valueset = joined_raw[:, :, 2].astype(jnp.bfloat16)
        scores = jnp.where(
            allowed[None],
            jnp.einsum("qhd,khd->hqk", queries, keyset, preferred_element_type=jnp.float32),
            NEGATIVE,
        )
        highest = jnp.max(scores, axis=-1, keepdims=True)
        shifted = jnp.exp(scores - highest)
        totals = jnp.sum(shifted, axis=-1, keepdims=True)
        log_total = highest + jnp.log(totals)
        probs_low = (shifted / totals).astype(jnp.bfloat16)
        mixed_heads = jnp.einsum(
            "hqk,khd->qhd", probs_low, valueset, preferred_element_type=jnp.float32
        )
        mixed_heads = mixed_heads.reshape(length, local_heads * HEAD).astype(jnp.bfloat16)
        branch_part = product(mixed_heads, dense_full)
        joined_full, dense_full = fetch_attention(joined_weight, dense_weight)
        mixed_grad = (
            contract_last(cotangent_full, dense_full)
            .astype(jnp.bfloat16)
            .reshape(length, local_heads, HEAD)
        )
        dense_total = contract_first(mixed_heads, cotangent_full)
        scores_again = jnp.where(
            allowed[None],
            jnp.einsum("qhd,khd->hqk", queries, keyset, preferred_element_type=jnp.float32),
            NEGATIVE,
        )
        probs_again = jnp.exp(scores_again - log_total)
        probs_grad = jnp.einsum(
            "qhd,khd->hqk", mixed_grad, valueset, preferred_element_type=jnp.float32
        )
        value_grad = jnp.einsum(
            "hqk,qhd->khd",
            probs_again.astype(jnp.bfloat16),
            mixed_grad,
            preferred_element_type=jnp.float32,
        )
        inner_sum = jnp.sum(probs_grad * probs_again, axis=-1, keepdims=True)
        score_grad = (probs_again * (probs_grad - inner_sum)).astype(jnp.bfloat16)
        query_grad = jnp.einsum(
            "hqk,khd->qhd", score_grad, keyset, preferred_element_type=jnp.float32
        )
        key_grad = jnp.einsum(
            "hqk,qhd->khd", score_grad, queries, preferred_element_type=jnp.float32
        )
        query_raw_grad, key_raw_grad = turn_back((query_grad, key_grad))
        joined_grad = (
            jnp.stack([query_raw_grad, key_raw_grad, value_grad], axis=2)
            .reshape(length, joined_columns)
            .astype(jnp.bfloat16)
        )
        joined_total = contract_first(normed, joined_grad)
        joined_bias_grad = jnp.sum(joined_grad.astype(jnp.float32), axis=0)
        normed_grad = contract_last(joined_grad, joined_full)
        input_part, gain_grad, shift_grad = norm_back(normed_grad)
        small_terms = jnp.concatenate(
            [gain_grad, shift_grad, jnp.zeros((total_span - 2 * model_width,), jnp.float32)]
        )
        small_terms = lax.dynamic_update_slice(
            small_terms, joined_bias_grad, (2 * model_width + model_index * joined_columns,)
        )
        weight_grads = (joined_total, dense_total) + blanks(expand_full, jnp.float32)
        return (branch_part, input_part, small_terms, weight_grads)

    def expand_pass(block_row, cotangent_full):
        up_full, down_full = fetch_expand(up_weight, down_weight)
        block_float = block_row.astype(jnp.float32)
        expanded_float, norm_back = jax.vjp(layer_norm, block_float, expand_gain, expand_shift)
        expanded = expanded_float.astype(jnp.bfloat16)
        bias_here = lax.dynamic_slice_in_dim(up_bias, model_index * hidden_columns, hidden_columns)
        hidden = product(expanded, up_full) + bias_here
        activated_float, gelu_back = jax.vjp(exact_gelu, hidden)
        activated = activated_float.astype(jnp.bfloat16)
        branch_part = product(activated, down_full)
        up_full, down_full = fetch_expand(up_weight, down_weight)
        activated_grad = contract_last(cotangent_full, down_full)
        hidden_grad = gelu_back(activated_grad)[0].astype(jnp.bfloat16)
        down_total = contract_first(activated, cotangent_full)
        up_total = contract_first(expanded, hidden_grad)
        up_bias_grad = jnp.sum(hidden_grad.astype(jnp.float32), axis=0)
        expanded_grad = contract_last(hidden_grad, up_full)
        input_part, gain_grad, shift_grad = norm_back(expanded_grad)
        small_terms = jnp.concatenate(
            [
                jnp.zeros((slot_expand,), jnp.float32),
                gain_grad,
                shift_grad,
                jnp.zeros((hidden_span + model_width,), jnp.float32),
            ]
        )
        small_terms = lax.dynamic_update_slice(
            small_terms, up_bias_grad, (slot_hidden + model_index * hidden_columns,)
        )
        weight_grads = blanks(attention_full, jnp.float32) + (up_total, down_total)
        return (branch_part, input_part, small_terms, weight_grads)

    small_sum = jnp.zeros((total_span,), jnp.float32)
    grad_acc = blanks(share_shapes, jnp.float32)
    column_bias = lax.dynamic_slice_in_dim(dense_bias + down_bias, column_start, column_count)
    cotangent_colsum = jnp.zeros((column_count,), jnp.float32)
    output_rows = []
    input_rows = []
    for micro_index in range(batches):
        block_row = block_input[micro_index]
        cotangent_row = cotangent[micro_index]
        cosine_table, sine_table = rotary_tables(segments[micro_index])
        allowed = allowed_pairs(segments[micro_index])
        cotangent_full = lax.all_gather(cotangent_row, ("branch", "mp"), axis=1, tiled=True)
        branch_part, input_part, small_terms, weight_grads = lax.cond(
            attention_side,
            lambda: attention_pass(block_row, cotangent_full, cosine_table, sine_table, allowed),
            lambda: expand_pass(block_row, cotangent_full),
        )
        forward_sum = lax.psum_scatter(
            branch_part, ("branch", "mp"), scatter_dimension=1, tiled=True
        )
        residual = lax.dynamic_slice_in_dim(block_row, column_start, column_count, 1).astype(
            jnp.float32
        )
        output_rows.append((residual + forward_sum + column_bias).astype(jnp.bfloat16))
        input_sum = lax.psum_scatter(input_part, ("branch", "mp"), scatter_dimension=1, tiled=True)
        cotangent_float = cotangent_row.astype(jnp.float32)
        input_rows.append((cotangent_float + input_sum).astype(jnp.bfloat16))
        cotangent_colsum = cotangent_colsum + jnp.sum(cotangent_float, axis=0)
        small_sum = small_sum + small_terms
        grad_acc = jax.tree.map(jnp.add, grad_acc, reduce_all(tuple(weight_grads)))
    small_sum = lax.dynamic_update_slice(small_sum, cotangent_colsum, (slot_output + column_start,))
    summed = lax.psum(small_sum, ("branch", "mp", "dp"))
    out_bias_grad = summed[slot_output : slot_output + model_width]
    return (
        jnp.stack(output_rows),
        jnp.stack(input_rows),
        summed[0:model_width],
        summed[model_width : 2 * model_width],
        grad_acc[0],
        summed[2 * model_width : slot_expand],
        grad_acc[1],
        out_bias_grad,
        summed[slot_expand : slot_expand + model_width],
        summed[slot_expand + model_width : slot_hidden],
        grad_acc[2],
        summed[slot_hidden:slot_output],
        grad_acc[3],
        out_bias_grad,
    )


def solution(mesh):
    in_specs = (
        P("dp", None, None),
        P("dp", None, ("branch", "mp")),
        P("dp", None),
        P(),
        P(),
        P("dp", "mp"),
        P(),
        P(("mp", "dp"), None),
        P(),
        P(),
        P(),
        P("dp", "mp"),
        P(),
        P(("mp", "dp"), None),
        P(),
    )
    out_specs = (
        P("dp", None, ("branch", "mp")),
        P("dp", None, ("branch", "mp")),
        P(),
        P(),
        P(("branch", "dp"), "mp"),
        P(),
        P("mp", ("branch", "dp")),
        P(),
        P(),
        P(),
        P(("branch", "dp"), "mp"),
        P(),
        P("mp", ("branch", "dp")),
        P(),
    )
    return jax.shard_map(
        on_device, mesh=mesh, in_specs=in_specs, out_specs=out_specs, check_vma=False
    )
```

profile of v0, /device:TPU:0, one launch (start us, length us, event | category | flops | bytes accessed | tf_op | source)
XLA Modules:
  0.0 2375.8 jit_solution(8899884487170086518)
XLA Ops:
  20.4 28.0 %all-gather.29.cloned.1.call-done = bf16[1,512,2048]{2,1,0:T(8,128)(2,1)} async-done(((bf16[1,512,512]{2,1,0:T(8,128)(2,1)}), bf16[1,512,2048]{2,1,0:T(8,128)(2,1)}) %all-gather.29.cloned.1.call-update) | async-done | bytes 2097168 | tf_op jit(solution)/shard_map/all_gather | solution.py:284
  48.3 37.6 %all-gather.31.cloned.1.call-done = bf16[1,512,2048]{2,1,0:T(8,128)(2,1)} async-done(((bf16[1,512,512]{2,1,0:T(8,128)(2,1)}), bf16[1,512,2048]{2,1,0:T(8,128)(2,1)}) %all-gather.31.cloned.1.call-update) | async-done | bytes 2097168 | tf_op jit(solution)/shard_map/all_gather | solution.py:284
  89.8 399.6 %conditional.3 = (f32[512,2048]{1,0:T(8,128)S(1)}, f32[24576]{0:T(1024)S(1)}, f32[2048,3072]{1,0:T(8,128)}, f32[1024,2048]{1,0:T(8,128)}, f32[2048,4096]{1,0:T(8...) conditional(s32[]{:T(128)} %convert_element_type.188, ...), branch_computations={%region_20.27_spmd, %region_27.37_spmd} | conditional | flops 51741003776 | bytes 471417632 | solution.py:285
  103.9 41.9 %all-gather.27.cloned.1.call-done = bf16[1024,2048]{1,0:T(8,128)(2,1)} async-done(((bf16[128,2048]{1,0:T(8,128)(2,1)}), bf16[1024,2048]{1,0:T(8,128)(2,1)}) %all-gather.27.cloned.1.call-update) | async-done | bytes 4194320 | tf_op jit(solution)/shard_map/cond/branch_1_fun/all_gather | solution.py:79
  153.5 212.7 %all-gather.25.cloned.1.call-done = bf16[2048,3072]{1,0:T(8,128)(2,1)} async-done(((bf16[256,3072]{1,0:T(8,128)(2,1)}), bf16[2048,3072]{1,0:T(8,128)(2,1)}) %all-gather.25.cloned.1.call-update) | async-done | bytes 12582928 | tf_op jit(solution)/shard_map/cond/branch_1_fun/all_gather | solution.py:78
  366.2 12.1 convolution_add_fusion.1
  427.3 14.3 fusion.113
  441.6 11.2 fusion.90
  464.4 11.2 broadcast.577
  475.6 11.3 broadcast.578
  492.7 447.4 %conditional.2 = (f32[512,2048]{1,0:T(8,128)}, f32[24576]{0:T(1024)S(1)}, f32[2048,3072]{1,0:T(8,128)}, f32[1024,2048]{1,0:T(8,128)}, f32[2048,4096]{1,0:T(8,128...) conditional(s32[]{:T(128)} %convert_element_type.188, ...), branch_computations={%region_1.8_spmd, %region_8.18_spmd} | conditional | flops 51741003776 | bytes 463282944 | solution.py:285
  507.3 85.4 %all-gather.19.cloned.1.call-done = bf16[1024,2048]{1,0:T(8,128)(2,1)} async-done(((bf16[128,2048]{1,0:T(8,128)(2,1)}), bf16[1024,2048]{1,0:T(8,128)(2,1)}) %all-gather.19.cloned.1.call-update) | async-done | bytes 4194320 | tf_op jit(solution)/shard_map/cond/branch_1_fun/all_gather | solution.py:79
  600.4 212.7 %all-gather.17.cloned.1.call-done = bf16[2048,3072]{1,0:T(8,128)(2,1)} async-done(((bf16[256,3072]{1,0:T(8,128)(2,1)}), bf16[2048,3072]{1,0:T(8,128)(2,1)}) %all-gather.17.cloned.1.call-update) | async-done | bytes 12582928 | tf_op jit(solution)/shard_map/cond/branch_1_fun/all_gather | solution.py:78
  813.1 11.5 convolution_add_fusion
  824.6 6.6 copy.93
  873.5 14.2 fusion.55
  887.7 11.2 fusion.32
  912.5 11.3 broadcast.520
  923.8 11.2 broadcast.521
  958.2 11.7 add.304
  970.0 25.1 %add.303 = f32[2048,3072]{1,0:T(8,128)} add(f32[2048,3072]{1,0:T(8,128)} %get-tuple-element.180, f32[2048,3072]{1,0:T(8,128)} %get-tuple-element.181) | non-fusion elementwise | flops 6291456 | bytes 75497472 | tf_op jit(solution)/shard_map/add | solution.py:302
  995.2 33.6 %add.305 = f32[2048,4096]{1,0:T(8,128)} add(f32[2048,4096]{1,0:T(8,128)} %get-tuple-element.184, f32[2048,4096]{1,0:T(8,128)} %get-tuple-element.185) | non-fusion elementwise | flops 8388608 | bytes 100663296 | tf_op jit(solution)/shard_map/add | solution.py:302
  1028.9 33.0 %add.306 = f32[4096,2048]{1,0:T(8,128)} add(f32[4096,2048]{1,0:T(8,128)} %get-tuple-element.186, f32[4096,2048]{1,0:T(8,128)} %get-tuple-element.187) | non-fusion elementwise | flops 8388608 | bytes 100663296 | tf_op jit(solution)/shard_map/add | solution.py:302
  1062.8 51.0 %all-reduce.14.cloned.1.call-done = f32[24576]{0:T(1024)} async-done(((f32[24576]{0:T(1024)}), f32[24576]{0:T(1024)}) %all-reduce.14.cloned.1.call-update) | async-done | bytes 98320 | tf_op jit(solution)/shard_map/psum | solution.py:304
  1118.0 52.4 %reduce-scatter.11.cloned.1.call-done = f32[512,512]{1,0:T(8,128)} async-done(((f32[512,2048]{1,0:T(8,128)}), f32[512,512]{1,0:T(8,128)}) %reduce-scatter.11.cloned.1.call-update) | async-done | bytes 1048592 | tf_op jit(solution)/shard_map/reduce_scatter | solution.py:290
  1170.4 55.9 %reduce-scatter.9.cloned.1.call-done = f32[512,512]{1,0:T(8,128)} async-done(((f32[512,2048]{1,0:T(8,128)}), f32[512,512]{1,0:T(8,128)}) %reduce-scatter.9.cloned.1.call-update) | async-done | bytes 1048592 | tf_op jit(solution)/shard_map/reduce_scatter | solution.py:290
  1229.5 52.3 %reduce-scatter.15.cloned.1.call-done = f32[512,512]{1,0:T(8,128)} async-done(((f32[512,2048]{1,0:T(8,128)}), f32[512,512]{1,0:T(8,128)}) %reduce-scatter.15.cloned.1.call-update) | async-done | bytes 1048592 | tf_op jit(solution)/shard_map/reduce_scatter | solution.py:297
  1281.8 55.9 %reduce-scatter.13.cloned.1.call-done = f32[512,512]{1,0:T(8,128)} async-done(((f32[512,2048]{1,0:T(8,128)}), f32[512,512]{1,0:T(8,128)}) %reduce-scatter.13.cloned.1.call-update) | async-done | bytes 1048592 | tf_op jit(solution)/shard_map/reduce_scatter | solution.py:297
  1340.7 106.4 %reduce-scatter.19.cloned.1.call-done = f32[1024,128]{1,0:T(8,128)} async-done(((f32[1024,2048]{1,0:T(8,128)}), f32[1024,128]{1,0:T(8,128)}) %reduce-scatter.19.cloned.1.call-update) | async-done | bytes 524304 | tf_op jit(solution)/shard_map/reduce_scatter | solution.py:97
  1447.1 248.3 %reduce-scatter.17.cloned.1.call-done = f32[128,3072]{1,0:T(8,128)} async-done(((f32[2048,3072]{1,0:T(8,128)}), f32[128,3072]{1,0:T(8,128)}) %reduce-scatter.17.cloned.1.call-update) | async-done | bytes 1572880 | tf_op jit(solution)/shard_map/reduce_scatter | solution.py:96
  1695.3 336.4 %reduce-scatter.21.cloned.1.call-done = f32[128,4096]{1,0:T(8,128)} async-done(((f32[2048,4096]{1,0:T(8,128)}), f32[128,4096]{1,0:T(8,128)}) %reduce-scatter.21.cloned.1.call-update) | async-done | bytes 2097168 | tf_op jit(solution)/shard_map/reduce_scatter | solution.py:98
  2031.8 336.5 %reduce-scatter.23.cloned.1.call-done = f32[4096,128]{1,0:T(8,128)} async-done(((f32[4096,2048]{1,0:T(8,128)}), f32[4096,128]{1,0:T(8,128)}) %reduce-scatter.23.cloned.1.call-update) | async-done | bytes 2097168 | tf_op jit(solution)/shard_map/reduce_scatter | solution.py:99
  (267 shorter events, 200.6 us)
Async XLA Ops:
  7.2 41.1 %all-gather.29.cloned.1.call-start = ((), (), s32[]{:S(2)}) async-start(), calls=%async_computation.21 | async-start | bytes 2621440 | tf_op jit(solution)/shard_map/all_gather | solution.py:284
  9.6 76.4 %all-gather.31.cloned.1.call-start = ((), (), s32[]{:S(2)}) async-start(), calls=%async_computation.22 | async-start | bytes 2621440 | tf_op jit(solution)/shard_map/all_gather | solution.py:284
  11.9 74.1 %copy-start.37 = (s32[1,512]{1,0:T(1,128)}, s32[1,512]{1,0:T(1,128)S(1)}, u32[]{:S(2)}) copy-start(s32[1,512]{1,0:T(1,128)S(1)} %get-tuple-element.293) | copy-start | bytes 6148
  11.9 75.2 %copy-start.39 = (s32[1,512]{1,0:T(1,128)}, s32[1,512]{1,0:T(1,128)S(1)}, u32[]{:S(2)}) copy-start(s32[1,512]{1,0:T(1,128)S(1)} %get-tuple-element.294) | copy-start | bytes 6148
  14.2 74.0 %copy-start.41 = (f32[2048]{0:T(1024)S(1)}, f32[2048]{0:T(1024)}, u32[]{:S(2)}) copy-start(f32[2048]{0:T(1024)} %param.28) | copy-start | bytes 24580
  14.2 74.0 %copy-start.43 = (f32[2048]{0:T(1024)S(1)}, f32[2048]{0:T(1024)}, u32[]{:S(2)}) copy-start(f32[2048]{0:T(1024)} %param.22) | copy-start | bytes 24580
  14.2 74.0 %copy-start.45 = (f32[8192]{0:T(1024)S(1)}, f32[8192]{0:T(1024)}, u32[]{:S(2)}) copy-start(f32[8192]{0:T(1024)} %param.31) | copy-start | bytes 98308
  14.2 74.0 %copy-start.47 = (f32[6144]{0:T(1024)S(1)}, f32[6144]{0:T(1024)}, u32[]{:S(2)}) copy-start(f32[6144]{0:T(1024)} %param.25) | copy-start | bytes 73732
  14.2 74.0 %copy-start.62 = (f32[2048]{0:T(1024)S(1)}, f32[2048]{0:T(1024)}, u32[]{:S(2)}) copy-start(f32[2048]{0:T(1024)} %param.29) | copy-start | bytes 24580
  96.1 7.5 copy-start.14
  96.2 7.5 copy-start.40
  96.2 49.6 %all-gather.27.cloned.1.call-start = ((), (), s32[]{:S(2)}) async-start(), calls=%async_computation.15 | async-start | bytes 4718592 | tf_op jit(solution)/shard_map/cond/branch_1_fun/all_gather | solution.py:79
  96.9 269.3 %all-gather.25.cloned.1.call-start = ((), (), s32[]{:S(2)}) async-start(), calls=%async_computation.14 | async-start | bytes 14155776 | tf_op jit(solution)/shard_map/cond/branch_1_fun/all_gather | solution.py:78
  97.5 6.2 copy-start.27
  145.8 220.4 %copy-start.64 = (f32[2048]{0:T(1024)S(1)}, f32[2048]{0:T(1024)}, u32[]{:S(2)}) copy-start(f32[2048]{0:T(1024)} %get-tuple-element.129) | copy-start | bytes 24580 | tf_op jit(solution)/shard_map/cond
  427.3 14.3 copy-start.2
  427.3 14.3 copy-start.19
  502.9 89.8 %all-gather.19.cloned.1.call-start = ((), (), s32[]{:S(2)}) async-start(), calls=%async_computation.11 | async-start | bytes 4718592 | tf_op jit(solution)/shard_map/cond/branch_1_fun/all_gather | solution.py:79
  503.5 309.6 %all-gather.17.cloned.1.call-start = ((), (), s32[]{:S(2)}) async-start(), calls=%async_computation.10 | async-start | bytes 14155776 | tf_op jit(solution)/shard_map/cond/branch_1_fun/all_gather | solution.py:78
  592.7 220.4 %copy-start.65 = (f32[2048]{0:T(1024)S(1)}, f32[2048]{0:T(1024)}, u32[]{:S(2)}) copy-start(f32[2048]{0:T(1024)} %get-tuple-element.110) | copy-start | bytes 24580 | tf_op jit(solution)/shard_map/cond
  873.5 14.2 copy-start.20
  940.1 173.7 %all-reduce.14.cloned.1.call-start = ((), (), s32[]{:S(2)}) async-start(), calls=%async_computation.20 | async-start | bytes 196608 | tf_op jit(solution)/shard_map/psum | solution.py:304
  942.6 227.8 %reduce-scatter.11.cloned.1.call-start = ((), (), s32[]{:S(2)}) async-start(), calls=%async_computation.17 | async-start | bytes 5242880 | tf_op jit(solution)/shard_map/reduce_scatter | solution.py:290
  943.3 283.0 %reduce-scatter.9.cloned.1.call-start = ((), (), s32[]{:S(2)}) async-start(), calls=%async_computation.16 | async-start | bytes 5242880 | tf_op jit(solution)/shard_map/reduce_scatter | solution.py:290
  944.1 337.7 %reduce-scatter.15.cloned.1.call-start = ((), (), s32[]{:S(2)}) async-start(), calls=%async_computation.19 | async-start | bytes 5242880 | tf_op jit(solution)/shard_map/reduce_scatter | solution.py:297
  951.1 386.6 %reduce-scatter.13.cloned.1.call-start = ((), (), s32[]{:S(2)}) async-start(), calls=%async_computation.18 | async-start | bytes 5242880 | tf_op jit(solution)/shard_map/reduce_scatter | solution.py:297
  958.2 488.9 %reduce-scatter.19.cloned.1.call-start = ((), (), s32[]{:S(2)}) async-start(), calls=%async_computation.24 | async-start | bytes 8912896 | tf_op jit(solution)/shard_map/reduce_scatter | solution.py:97
  970.0 725.4 %reduce-scatter.17.cloned.1.call-start = ((), (), s32[]{:S(2)}) async-start(), calls=%async_computation.23 | async-start | bytes 26738688 | tf_op jit(solution)/shard_map/reduce_scatter | solution.py:96
  995.1 1036.7 %reduce-scatter.21.cloned.1.call-start = ((), (), s32[]{:S(2)}) async-start(), calls=%async_computation.25 | async-start | bytes 35651584 | tf_op jit(solution)/shard_map/reduce_scatter | solution.py:98
  1028.8 1339.4 %reduce-scatter.23.cloned.1.call-start = ((), (), s32[]{:S(2)}) async-start(), calls=%async_computation.26 | async-start | bytes 35651584 | tf_op jit(solution)/shard_map/reduce_scatter | solution.py:99
  1061.9 275.8 %copy-start.11 = (bf16[2,512,512]{2,1,0:T(8,128)(2,1)S(1)}, bf16[2,512,512]{2,1,0:T(8,128)(2,1)}, u32[]{:S(2)}) copy-start(bf16[2,512,512]{2,1,0:T(8,128)(2,1)} %param.20) | copy-start | bytes 3145732
  1115.2 1253.0 %copy-start.44 = (f32[2048]{0:T(1024)}, f32[2048]{0:T(1024)S(1)}, u32[]{:S(2)}) copy-start(f32[2048]{0:T(1024)S(1)} %get-tuple-element.468) | copy-start | bytes 24580
  (42 other events, 119.2 us)
Sparse Core Ops, SparseCore 0:
  10.4 37.8 all-gather.28
  50.7 35.1 all-gather.30
  98.6 47.1 all-gather.26
  147.3 218.8 all-gather.24
  505.1 87.5 all-gather.18
  594.2 218.8 all-gather.16
  947.1 166.7 all-reduce.13
  1116.8 53.5 reduce-scatter.10
  1173.6 52.6 reduce-scatter.8
  1229.1 52.6 reduce-scatter.14
  1285.0 52.6 reduce-scatter.12
  1342.2 104.8 reduce-scatter.18
  1451.8 243.5 reduce-scatter.16
  1700.0 331.7 reduce-scatter.20
  2036.5 331.7 reduce-scatter.22
where the time goes:
time: 2390 us; the launch traced here: 2380 us
  waiting for transfers between devices  1920 us (80%)
  other arithmetic  166 us (7%)
  local copies, waits for them, and re-layouts  137 us (6%)
  matrix products  122 us (5%)
    all_gather x2, waiting for transfers between devices, fetch_attention(): lax.all_gather(joined_weight, 'dp', axis=0, tiled=True)  425 us
    reduce_scatter x1, waiting for transfers between devices, reduce_all(): lax.psum_scatter(grad_tuple[3], ('branch', 'dp'), scatter_dimension=1, ti...  336 us
    reduce_scatter x1, waiting for transfers between devices, reduce_all(): lax.psum_scatter(grad_tuple[2], ('branch', 'dp'), scatter_dimension=0, ti...  336 us
    reduce_scatter x1, waiting for transfers between devices, reduce_all(): lax.psum_scatter(grad_tuple[0], ('branch', 'dp'), scatter_dimension=0, ti...  248 us
    all_gather x2, waiting for transfers between devices, fetch_attention(): lax.all_gather(dense_weight, 'dp', axis=0, tiled=True)  127 us
    reduce_scatter x2, waiting for transfers between devices, on_device(): lax.psum_scatter(branch_part, ('branch', 'mp'), scatter_dimension=1, tile...  108 us
    reduce_scatter x2, waiting for transfers between devices, on_device(): lax.psum_scatter(input_part, ('branch', 'mp'), scatter_dimension=1, tiled...  108 us
    reduce_scatter x1, waiting for transfers between devices, reduce_all(): lax.psum_scatter(grad_tuple[1], ('branch', 'dp'), scatter_dimension=1, ti...  106 us
  transfers between devices with their start and end apart: 15, of which 15 were waited for; matrix products, arithmetic and copies ran while one was open for 7% of the time, Pallas kernels for 0%

commit v1 on v0

v1 whole, which is shorter than its diff:
```python
import math

import jax
import jax.numpy as jnp
from jax import lax
from jax.sharding import Mesh, PartitionSpec as P

HEAD = 256
ROT = 64
NEGATIVE = -1e30
F32 = jnp.float32
BF16 = jnp.bfloat16


def rotary_tables(segment_rows):
    length = segment_rows.shape[1]
    before = jnp.sum(
        (segment_rows[:, None, :] < segment_rows[:, :, None]).astype(jnp.int32), axis=2
    )
    places = (jnp.arange(length, dtype=jnp.int32)[None] - before).astype(F32)
    frequency = 10000.0 ** (-jnp.arange(0, ROT, 2).astype(F32) / ROT)
    angles = places[:, :, None] * frequency
    return jnp.cos(angles), jnp.sin(angles)


def allowed_pairs(segment_rows):
    token_index = jnp.arange(segment_rows.shape[1], dtype=jnp.int32)
    return (segment_rows[:, :, None] == segment_rows[:, None, :]) & (
        token_index[None, :] <= token_index[:, None]
    )


def rotate(values, cosine_table, sine_table):
    half = ROT // 2
    first, second = values[..., :half], values[..., half:ROT]
    return jnp.concatenate(
        [
            first * cosine_table - second * sine_table,
            second * cosine_table + first * sine_table,
            values[..., ROT:],
        ],
        axis=-1,
    )


def dot(left, right, left_dim, right_dim):
    return lax.dot_general(
        left, right, (((left_dim,), (right_dim,)), ((), ())), preferred_element_type=F32
    )


def pick(array, index, axis):
    return lax.dynamic_index_in_dim(array, index, axis, keepdims=False)


def add_low(left, right):
    return (left.astype(F32) + right.astype(F32)).astype(BF16)


SWAP = [(0, 1), (1, 0)]


def chain_sum(parts, index, count):
    from_left = from_right = None
    for step in range(1, count):
        to_right = parts(jnp.clip(index + count - step, 0, count - 1))
        to_left = parts(jnp.clip(index - count + step, 0, count - 1))
        if from_left is not None:
            to_right = add_low(to_right, from_left)
            to_left = add_low(to_left, from_right)
        from_left = lax.ppermute(to_right, "z", [(i, i + 1) for i in range(step)])
        from_right = lax.ppermute(to_left, "z", [(count - 1 - i, count - 2 - i) for i in range(step)])
    total = parts(index).astype(F32)
    if from_left is not None:
        total = total + from_left.astype(F32) + from_right.astype(F32)
    return total


def solution(mesh):
    branches, models, datas = (mesh.shape[name] for name in ("branch", "mp", "dp"))
    cores = 2
    chips = datas // cores
    fine = Mesh(
        mesh.devices.reshape(branches, models, chips, cores), ("branch", "mp", "z", "core")
    )

    def on_device(
        block_input,
        cotangent,
        segments,
        attend_gain,
        attend_shift,
        joined_weight,
        joined_bias,
        dense_weight,
        dense_bias,
        expand_gain,
        expand_shift,
        up_weight,
        up_bias,
        down_weight,
        down_bias,
    ):
        rows, length, width = block_input.shape
        b, m, z, c = (lax.axis_index(name) for name in ("branch", "mp", "z", "core"))
        tokens = rows * length
        span = width // (branches * models)
        column_start = (b * models + m) * span
        heads = branches * cores
        head_columns = joined_weight.shape[1] // heads
        hidden_columns = up_weight.shape[1]
        part = down_weight.shape[0] // branches
        head_slot = b * cores + c

        def swap_core(array):
            return lax.ppermute(array, "core", SWAP)

        def both_cores_columns(mine, theirs):
            other = swap_core(theirs)
            return jnp.where(c == 0, jnp.concatenate([mine, other]), jnp.concatenate([other, mine]))

        by_head = joined_weight.reshape(-1, heads, head_columns)
        joined_piece = both_cores_columns(
            pick(by_head, head_slot, 1), pick(by_head, b * cores + 1 - c, 1)
        )
        by_unit = up_weight.reshape(-1, chips, cores, branches, part)
        mine = pick(pick(by_unit, b, 3), c, 2).reshape(-1, chips * part)
        theirs = pick(pick(by_unit, b, 3), 1 - c, 2).reshape(-1, chips * part)
        up_piece = both_cores_columns(mine, theirs)
        joined_full = lax.all_gather(joined_piece, "z", axis=0, tiled=True)
        dense_full = lax.all_gather(dense_weight, ("z", "core"), axis=0, tiled=True)
        dense_full = lax.dynamic_slice_in_dim(dense_full, head_slot * HEAD, HEAD, 0)
        up_full = lax.all_gather(up_piece, "z", axis=0, tiled=True)
        down_piece = lax.dynamic_slice_in_dim(down_weight, b * part, part, 0)
        down_full = lax.all_gather(down_piece, "z", axis=0, tiled=True)

        joined_bias_here = lax.dynamic_slice_in_dim(
            joined_bias, (m * heads + head_slot) * head_columns, head_columns
        )
        bias_units = up_bias.reshape(models, chips, cores, branches, part)
        up_bias_here = pick(pick(pick(bias_units, b, 3), c, 2), m, 0).reshape(-1)

        x_own = block_input.reshape(tokens, width)
        x = jnp.concatenate([x_own, swap_core(x_own)])
        segment_rows = jnp.concatenate([segments, swap_core(segments)])
        g_piece = cotangent.reshape(tokens, span)
        g_own = jnp.zeros((tokens, width), BF16)
        for db in range(branches):
            for dm in range(models):
                axes = ([("branch", branches)] if db else []) + ([("mp", models)] if dm else [])
                piece = g_piece
                if axes:
                    count = math.prod(size for _, size in axes)
                    piece = lax.ppermute(
                        piece,
                        tuple(name for name, _ in axes),
                        [(i, count - 1 - i) for i in range(count)],
                    )
                start = ((b ^ db) * models + (m ^ dm)) * span
                g_own = lax.dynamic_update_slice(g_own, piece, (0, start))
        g = jnp.concatenate([g_own, swap_core(g_own)])

        xf = x.astype(F32)
        mean = jnp.mean(xf, axis=-1, keepdims=True)
        center = xf - mean
        inverse = lax.rsqrt(jnp.mean(center * center, axis=-1, keepdims=True) + 1e-05)
        hat = center * inverse
        normed = (hat * attend_gain + attend_shift).astype(BF16)
        expanded = (hat * expand_gain + expand_shift).astype(BF16)

        all_rows = 2 * rows
        joined_raw = (dot(normed, joined_full, 1, 0) + joined_bias_here).reshape(
            all_rows, length, 3, HEAD
        )
        cosine, sine = rotary_tables(segment_rows)
        allowed = allowed_pairs(segment_rows)
        scale = 1.0 / math.sqrt(HEAD)
        queries = (rotate(joined_raw[:, :, 0], cosine, sine) * scale).astype(BF16)
        keyset = rotate(joined_raw[:, :, 1], cosine, sine).astype(BF16)
        valueset = joined_raw[:, :, 2].astype(BF16)

        def ein(spec, left, right):
            return jnp.einsum(spec, left, right, preferred_element_type=F32)

        scores = jnp.where(allowed, ein("rqd,rkd->rqk", queries, keyset), NEGATIVE)
        shifted = jnp.exp(scores - jnp.max(scores, axis=-1, keepdims=True))
        probs = shifted / jnp.sum(shifted, axis=-1, keepdims=True)
        probs_low = probs.astype(BF16)
        mixed = ein("rqk,rkd->rqd", probs_low, valueset).astype(BF16).reshape(-1, HEAD)
        mixed_grad = dot(g, dense_full, 1, 1).astype(BF16).reshape(all_rows, length, HEAD)
        probs_grad = ein("rqd,rkd->rqk", mixed_grad, valueset)
        value_grad = ein("rqk,rqd->rkd", probs_low, mixed_grad)
        inner = jnp.sum(probs_grad * probs, axis=-1, keepdims=True)
        score_grad = (probs * (probs_grad - inner)).astype(BF16)
        query_grad = rotate(ein("rqk,rkd->rqd", score_grad, keyset), cosine, -sine) * scale
        key_grad = rotate(ein("rqk,rqd->rkd", score_grad, queries), cosine, -sine)
        joined_grad = (
            jnp.stack([query_grad, key_grad, value_grad], axis=2)
            .reshape(-1, head_columns)
            .astype(BF16)
        )
        dense_part = dot(g, mixed, 0, 0).astype(BF16)
        joined_part = dot(normed, joined_grad, 0, 0).astype(BF16)
        joined_bias_grad = jnp.sum(joined_grad.astype(F32), axis=0)
        normed_grad = dot(joined_grad, joined_full, 1, 1)

        hidden = dot(expanded, up_full, 1, 0) + up_bias_here
        activated_float, gelu_back = jax.vjp(lambda t: jax.nn.gelu(t, approximate=False), hidden)
        activated = activated_float.astype(BF16)
        down_part = dot(g, activated, 0, 0).astype(BF16)
        hidden_grad = gelu_back(dot(g, down_full, 1, 1))[0].astype(BF16)
        up_part = dot(expanded, hidden_grad, 0, 0).astype(BF16)
        up_bias_grad = jnp.sum(hidden_grad.astype(F32), axis=0)
        expanded_grad = dot(hidden_grad, up_full, 1, 1)

        def token_sum(term):
            mine, theirs = term[:tokens], term[tokens:]
            half = tokens // 2
            total = add_low(mine, swap_core(theirs)).reshape(2, half, branches, models, span)
            first, second = total[0], total[1]
            first_in = lax.ppermute(pick(first, 1 - b, 1), "branch", SWAP)
            second_in = lax.ppermute(pick(second, 1 - m, 2), "mp", SWAP)
            first = add_low(pick(first, b, 1), first_in)
            second = add_low(pick(second, m, 2), second_in)
            first_in = lax.ppermute(pick(first, 1 - m, 1), "mp", SWAP)
            second_in = lax.ppermute(pick(second, 1 - b, 1), "branch", SWAP)
            first = pick(first, m, 1).astype(F32) + first_in.astype(F32)
            second = pick(second, b, 1).astype(F32) + second_in.astype(F32)
            return jnp.concatenate([first, second])

        forward = (dot(mixed, dense_full, 1, 0) + dot(activated, down_full, 1, 0)).astype(BF16)
        forward_sum = token_sum(forward)
        residual = lax.dynamic_slice_in_dim(x_own, column_start, span, 1).astype(F32)
        column_bias = lax.dynamic_slice_in_dim(dense_bias + down_bias, column_start, span)
        block_output = (residual + forward_sum + column_bias).astype(BF16)

        weighted = normed_grad * attend_gain + expanded_grad * expand_gain
        input_term = inverse * (
            weighted
            - jnp.mean(weighted, axis=-1, keepdims=True)
            - hat * jnp.mean(weighted * hat, axis=-1, keepdims=True)
        )
        input_sum = token_sum(input_term.astype(BF16))
        g_float = g_piece.astype(F32)
        input_gradient = (g_float + input_sum).astype(BF16)

        row_share = width // (branches * datas)

        def weight_sum(term):
            columns = term.shape[1]
            view = term.reshape(branches, chips, cores * row_share, columns)
            share = chain_sum(lambda j: pick(view, j, 1), z, chips)
            share = share.astype(BF16).reshape(branches, cores, row_share, columns)
            out = jnp.zeros((branches, cores, row_share, columns), BF16)
            for db in range(branches):
                for dc in range(cores):
                    piece = pick(pick(share, b ^ db, 0), c ^ dc, 0)
                    axes = ([("branch", branches)] if db else []) + ([("core", cores)] if dc else [])
                    if axes:
                        count = math.prod(size for _, size in axes)
                        piece = lax.ppermute(
                            piece,
                            tuple(name for name, _ in axes),
                            [(i, count - 1 - i) for i in range(count)],
                        )
                    out = lax.dynamic_update_slice(
                        out, piece[None, None], (b ^ db, c ^ dc, 0, 0)
                    )
            return out.astype(F32)

        dense_sum = weight_sum(dense_part)
        joined_sum = weight_sum(joined_part)
        down_sum = weight_sum(down_part)
        up_sum = weight_sum(up_part)
        joined_out = joined_sum.transpose(2, 0, 1, 3).reshape(row_share, -1)
        dense_out = dense_sum.transpose(0, 1, 3, 2).reshape(-1, row_share)
        up_out = (
            up_sum.reshape(branches, cores, row_share, chips, part)
            .transpose(2, 3, 1, 0, 4)
            .reshape(row_share, hidden_columns)
        )
        down_out = (
            down_sum.reshape(branches, cores, row_share, chips, part)
            .transpose(3, 1, 0, 4, 2)
            .reshape(hidden_columns, row_share)
        )

        attend_gain_grad = jnp.sum(normed_grad * hat, axis=0)
        attend_shift_grad = jnp.sum(normed_grad, axis=0)
        expand_gain_grad = jnp.sum(expanded_grad * hat, axis=0)
        expand_shift_grad = jnp.sum(expanded_grad, axis=0)
        joined_slot = lax.dynamic_update_slice(
            jnp.zeros_like(joined_bias),
            joined_bias_grad,
            ((m * heads + head_slot) * head_columns,),
        )
        up_slot = lax.dynamic_update_slice(
            jnp.zeros((models, chips, cores, branches, part), F32),
            up_bias_grad.reshape(1, chips, 1, 1, part),
            (m, 0, c, b, 0),
        ).reshape(-1)
        out_slot = lax.dynamic_update_slice(
            jnp.zeros((width,), F32), jnp.sum(g_float, axis=0), (column_start,)
        )
        small = jnp.concatenate(
            [
                attend_gain_grad,
                attend_shift_grad,
                expand_gain_grad,
                expand_shift_grad,
                out_slot,
                joined_slot,
                up_slot,
            ]
        )
        small = lax.psum(small, ("branch", "mp", "z", "core"))
        w = width
        joined_end = 5 * w + joined_bias.shape[0]
        return (
            block_output.reshape(rows, length, span),
            input_gradient.reshape(rows, length, span),
            small[:w],
            small[w : 2 * w],
            joined_out,
            small[5 * w : joined_end],
            dense_out,
            small[4 * w : 5 * w],
            small[2 * w : 3 * w],
            small[3 * w : 4 * w],
            up_out,
            small[joined_end:],
            down_out,
            small[4 * w : 5 * w],
        )

    data = ("z", "core")
    everything = ("branch", "z", "core")
    in_specs = (
        P(data, None, None),
        P(data, None, ("branch", "mp")),
        P(data, None),
        P(),
        P(),
        P(data, "mp"),
        P(),
        P(("mp", "z", "core"), None),
        P(),
        P(),
        P(),
        P(data, "mp"),
        P(),
        P(("mp", "z", "core"), None),
        P(),
    )
    out_specs = (
        P(data, None, ("branch", "mp")),
        P(data, None, ("branch", "mp")),
        P(),
        P(),
        P(everything, "mp"),
        P(),
        P("mp", everything),
        P(),
        P(),
        P(),
        P(everything, "mp"),
        P(),
        P("mp", everything),
        P(),
    )
    return jax.shard_map(
        on_device, mesh=fine, in_specs=in_specs, out_specs=out_specs, check_vma=False
    )
```

time: 2390 us -> 807 us (0.34)
  waiting for transfers between devices: 1920 us -> 309 us
  other arithmetic: 166 us -> 80.5 us
  starting transfers between devices: 0.61 us -> 81.4 us
  matrix products: 122 us -> 183 us
    reduce_scatter x8 -> x0, waiting for transfers between devices: 1240 us -> none  [the longest x1 336 us: reduce_all(): lax.psum_scatter(grad_tuple[3], ('branch', 'dp'), scatter_dimension=1, ti...]
    all_gather x6 -> x4, waiting for transfers between devices: 618 us -> 0.94 us  [the longest x1 0.92 us: on_device(): down_full = lax.all_gather(down_piece, 'z', axis=0, tiled=True)]
    ppermute x0 -> x54, waiting for transfers between devices: none -> 197 us  [the longest x12 70.4 us: chain_sum(): from_left = lax.ppermute(to_right, 'z', [(i, i + 1) for i in range(step)])]
    add x7 -> x4, other arithmetic: 104 us -> 3.01 us  [the longest x2 1.52 us: token_sum(): second = pick(second, b, 1).astype(F32) + second_in.astype(F32)]
    ppermute x0 -> x54, starting transfers between devices: none -> 81.2 us  [the longest x12 41.8 us: chain_sum(): from_left = lax.ppermute(to_right, 'z', [(i, i + 1) for i in range(step)])]
    dot_general x24 -> x18, matrix products: 122 us -> 183 us  [the longest x12 177 us: dot(): lax.dot_general(left, right, (((left_dim,), (right_dim,)), ((), ())), pre...]
    psum x1, waiting for transfers between devices: 51 us -> 111 us  [on_device(): small = lax.psum(small, ('branch', 'mp', 'z', 'core'))]
    another operation x10 -> x2, local copies, waits for them, and re-layouts: 45 us -> 0.28 us
  transfers between devices with their start and end apart: 15 -> 59, of which waited for: 15 -> 27; matrix products, arithmetic and copies ran while one was open for 7% -> 47% of each run, Pallas kernels for 0% -> 0%
where the time goes in v1:
time: 807 us; the launch traced here: 802 us
  waiting for transfers between devices  309 us (38%)
  matrix products  183 us (23%)
  local copies, waits for them, and re-layouts  132 us (16%)
  starting transfers between devices  81.4 us (10%)
  other arithmetic  80.5 us (10%)
  between operations  15.8 us (2%)
    dot_general x12, matrix products, dot(): lax.dot_general(left, right, (((left_dim,), (right_dim,)), ((), ())), pre...  177 us
    psum x1, waiting for transfers between devices, on_device(): small = lax.psum(small, ('branch', 'mp', 'z', 'core'))  111 us
    ppermute x12, waiting for transfers between devices, chain_sum(): from_left = lax.ppermute(to_right, 'z', [(i, i + 1) for i in range(step)])  70.4 us
    ppermute x12, starting transfers between devices, chain_sum(): from_left = lax.ppermute(to_right, 'z', [(i, i + 1) for i in range(step)])  41.8 us
    ppermute x12, waiting for transfers between devices, chain_sum(): lax.ppermute(to_left, 'z', [(count - 1 - i, count - 2 - i) for i in range...  41.2 us
    ppermute x3, waiting for transfers between devices, on_device(): lax.ppermute(piece, tuple((name for name, _ in axes)), [(i, count - 1 - i...  34.5 us
    convert_element_type x16, other arithmetic, add_low(): return (left.astype(F32) + right.astype(F32)).astype(BF16)  31.2 us
    unnamed x152, local copies, waits for them, and re-layouts  28.8 us
  transfers between devices with their start and end apart: 59, of which 27 were waited for; matrix products, arithmetic and copies ran while one was open for 47% of the time, Pallas kernels for 0%

profile of v1, /device:TPU:0, one launch (start us, length us, event | category | flops | bytes accessed | tf_op | source)
XLA Modules:
  0.0 801.8 jit_solution(15488758854173720047)
XLA Ops:
  24.3 6.5 copy.305
  42.1 15.6 %collective-permute-done.9 = bf16[1024,512]{1,0:T(8,128)(2,1)} collective-permute-done((bf16[1024,512]{1,0:T(8,128)(2,1)S(1)}, bf16[1024,512]{1,0:T(8,128)(2,1)}, u32[]{:S(2)}, u32[]{:S(2)}) %collective-permute-start.9) | collective-permute-done | bytes 1048608 | tf_op jit(solution)/shard_map/ppermute | solution.py:154
  62.4 18.9 %collective-permute-done.11 = bf16[1024,512]{1,0:T(8,128)(2,1)} collective-permute-done((bf16[1024,512]{1,0:T(8,128)(2,1)S(1)}, bf16[1024,512]{1,0:T(8,128)(2,1)}, u32[]{:S(2)}, u32[]{:S(2)}) %collective-permute-start.11) | collective-permute-done | bytes 1048608 | tf_op jit(solution)/shard_map/ppermute | solution.py:154
  91.7 15.2 %convolution_add_fusion = f32[2048,768]{1,0:T(8,128)} fusion(bf16[2048,768]{1,0:T(8,128)(2,1)} %all-gather.5.cloned.1.call-done, f32[768]{0:T(1024)S(1)} %dynamic_slice.251, f32[2048]{0:T(1024)S(1)} %copy-done.60, f32[2048]{0:T(1024)S(1)} %copy-done.63, f32[2048]{0:T(1024)S(1)} %add_rsqrt_fusion, f32[2048]{0:T(1024)S(1)} %broadcast_multiply_fusion.2, ...), kind=kOutput, calls=%fused_computation.56 | convolution fusion | flops 6481772544 | bytes 17861632 | tf_op jit(solution)/shard_map/dot_general | solution.py:47
  106.8 6.6 copy.247
  113.4 8.8 %reshape.347 = f32[4,512,3,256]{1,0,3,2:T(4,128)} reshape(f32[2048,768]{0,1:T(8,128)} %copy.247) | data formatting | bytes 12582912 | tf_op jit(solution)/shard_map/reshape | solution.py:172
  142.7 6.3 convolution_convert_fusion.3
  153.5 11.4 %collective-permute-done.27 = bf16[2,256,256]{2,1,0:T(8,128)(2,1)S(1)} collective-permute-done((bf16[2,256,256]{2,1,0:T(8,128)(2,1)S(1)}, bf16[2,256,256]{2,1,0:T(8,128)(2,1)S(1)}, u32[]{:S(2)}, u32[]{:S(2)}) %collective-permute-start.27) | collective-permute-done | bytes 262176 | tf_op jit(solution)/shard_map/ppermute | solution.py:71
  183.5 8.5 %collective-permute-done.29 = bf16[2,256,256]{2,1,0:T(8,128)(2,1)S(1)} collective-permute-done((bf16[2,256,256]{2,1,0:T(8,128)(2,1)S(1)}, bf16[2,256,256]{2,1,0:T(8,128)(2,1)S(1)}, u32[]{:S(2)}, u32[]{:S(2)}) %collective-permute-start.29) | collective-permute-done | bytes 262176 | tf_op jit(solution)/shard_map/ppermute | solution.py:71
  192.0 23.4 %collective-permute-done.32 = bf16[2,256,256]{2,1,0:T(8,128)(2,1)S(1)} collective-permute-done((bf16[2,256,256]{2,1,0:T(8,128)(2,1)S(1)}, bf16[2,256,256]{2,1,0:T(8,128)(2,1)S(1)}, u32[]{:S(2)}, u32[]{:S(2)}) %collective-permute-start.32) | collective-permute-done | bytes 262176 | tf_op jit(solution)/shard_map/ppermute | solution.py:72
  222.6 35.7 %multiply_convert_fusion = (bf16[2048,1024]{1,0:T(8,128)(2,1)}, f32[2048,1024]{1,0:T(8,128)}, f32[2048,1024]{1,0:T(8,128)}) fusion(f32[1024]{0:T(1024)S(1)} %bitcast.343, bf16[2048,1024]{0,1:T(8,128)(2,1)} %all-gather.9.cloned.1.call-done, f32[2048]{0:T(1024)S(1)} %copy-done.59, f32[2048]{0:T(1024)S(1)} %copy-done.62, f32[2048]{0:T(1024)S(1)} %add_rsqrt_fusion, ...), kind=kOutput, calls=%fused_computation.32 | convolution fusion | flops 8766095360 | bytes 33591296 | tf_op jit(solution)/shard_map/dot_general | solution.py:47
  259.3 19.3 %convert_reduce_fusion.1 = (f32[1024]{0:T(1024)S(1)}, bf16[2048,1024]{1,0:T(8,128)(2,1)}) fusion(f32[2048,1024]{1,0:T(8,128)} %get-tuple-element.94, bf16[1024,2048]{1,0:T(8,128)(2,1)} %all-gather.11.cloned.1.call-done, bf16[1024,2048]{1,0:T(8,128)(2,1)} %collective-permute-done.12, bf16[1024,2048]{1,0:T(8,128)(2,1)} %constant_dynamic-update-slice_fusion.6, ...), kind=kOutput, calls=%fused_computation.28 | convolution fusion | flops 8642362368 | bytes 33562624 | tf_op jit(solution)/shard_map/dot_general | solution.py:47
  278.6 12.7 %convolution_convert_fusion = bf16[2048,1024]{1,0:T(8,128)(2,1)S(1)} fusion(bf16[2048,1024]{1,0:T(8,128)(2,1)} %get-tuple-element.169, f32[2048]{0:T(1024)S(1)} %copy-done.59, f32[2048]{0:T(1024)S(1)} %copy-done.62, f32[2048]{0:T(1024)S(1)} %add_rsqrt_fusion, f32[2048]{0:T(1024)S(1)} %broadcast_multiply_fusion.2, ...), kind=kOutput, calls=%fused_computation.53 | convolution fusion | flops 8629780480 | bytes 16809984 | tf_op jit(solution)/shard_map/dot_general | solution.py:47
  292.8 5.9 collective-permute-start.36
  300.4 11.4 %convolution_convert_fusion.1 = bf16[2048,1024]{1,0:T(8,128)(2,1)S(1)} fusion(bf16[2048,1024]{1,0:T(8,128)(2,1)S(1)} %copy-done.65, bf16[1024,2048]{1,0:T(8,128)(2,1)} %collective-permute-done.12, bf16[1024,2048]{1,0:T(8,128)(2,1)} %constant_dynamic-update-slice_fusion.6), kind=kOutput, calls=%fused_computation.54 | convolution fusion | flops 8608808960 | bytes 16777216 | tf_op jit(solution)/shard_map/dot_general | solution.py:47
  319.9 15.4 %fusion.126 = f32[2048,2048]{0,1:T(8,128)} fusion(bf16[2048,1024]{1,0:T(8,128)(2,1)} %get-tuple-element.93, bf16[1024,2048]{1,0:T(8,128)(2,1)} %all-gather.11.cloned.1.call-done), kind=kOutput, calls=%fused_computation.272 | convolution fusion | flops 8589934592 | bytes 25165824 | tf_op jit(solution)/shard_map/dot_general | solution.py:47
  335.3 6.2 convolution_convert_fusion.4
  354.4 9.6 %convolution_convert_fusion.2 = bf16[2048,768]{1,0:T(8,128)(2,1)S(1)} fusion(bf16[2048,768]{0,1:T(8,128)(2,1)S(1)} %bitcast.323, f32[2048]{0:T(1024)S(1)} %copy-done.61, f32[2048]{0:T(1024)S(1)} %copy-done.64, f32[2048]{0:T(1024)S(1)} %add_rsqrt_fusion, f32[2048]{0:T(1024)S(1)} %broadcast_multiply_fusion.2, bf16[1024,2048]{0,1:T(8,128)(2,1)} %collective-permute-done.1, ...), kind=kOutput, calls=%fused_computation.55 | convolution fusion | flops 6481772544 | bytes 14712832 | tf_op jit(solution)/shard_map/dot_general | solution.py:47
  365.6 9.9 %fusion.127 = f32[2048,2048]{0,1:T(8,128)} fusion(bf16[2048,768]{1,0:T(8,128)(2,1)S(1)} %copy-done.58, bf16[2048,768]{0,1:T(8,128)(2,1)S(1)} %bitcast.324), kind=kOutput, calls=%fused_computation.273 | convolution fusion | flops 6442450944 | bytes 23068672 | tf_op jit(solution)/shard_map/dot_general | solution.py:47
  375.5 23.4 %fusion.117 = (f32[2048]{0:T(1024)S(1)}, f32[2048]{0:T(1024)S(1)}, f32[2048]{0:T(1024)S(1)}, f32[2048]{0:T(1024)S(1)}, f32[2048,2048]{0,1:T(8,128)}, /*index=5*/f32[2048]{0:T(1024)S(1)}, f32[2048]{0:T(1024)S(1)}) fusion(f32[2048]{0:T(1024)S(1)} %add_rsqrt_fusion, f32[2048]{0:T(1024)S(1)} %broadcast_multiply_fusion.2, ...), kind=kOutput, calls=%fused_computation.264 | convolution fusion | flops 8665419776 | bytes 50413568 | tf_op jit(solution)/shard_map/dot_general | solution.py:47
  412.6 6.6 collective-permute-done.19
  421.5 9.0 %fusion.16 = bf16[2048,2048]{0,1:T(8,128)(2,1)S(1)} fusion(f32[2048,2048]{0,1:T(8,128)} %get-tuple-element.97, f32[2048]{0:T(1024)S(1)} %broadcast_multiply_fusion, f32[2048]{0:T(1024)S(1)} %broadcast_multiply_fusion.1, f32[2048]{0:T(1024)S(1)} %add_rsqrt_fusion, f32[2048]{0:T(1024)S(1)} %broadcast_multiply_fusion.2, ...), kind=kLoop, calls=%fused_computation.18 | loop fusion | flops 46137344 | bytes 33587200 | tf_op jit(solution)/shard_map/convert_element_type | solution.py:243
  435.0 6.6 collective-permute-done.37
  448.5 15.7 %collective-permute-done.46 = bf16[2,256,1024]{2,1,0:T(8,128)(2,1)S(1)} collective-permute-done((bf16[2,256,1024]{2,1,0:T(8,128)(2,1)}, bf16[2,256,1024]{2,1,0:T(8,128)(2,1)S(1)}, u32[]{:S(2)}, u32[]{:S(2)}) %collective-permute-start.46) | collective-permute-done | bytes 1048608 | tf_op jit(solution)/shard_map/ppermute | solution.py:71
  469.1 5.9 collective-permute-start.47
  476.3 11.7 %add_convert_fusion = bf16[2048,2048]{0,1:T(8,128)(2,1)} fusion(f32[2048,2048]{0,1:T(8,128)} %fusion.126, bf16[2048,256]{1,0:T(8,128)(2,1)S(1)} %bitcast.316, bf16[1024,2048]{1,0:T(8,128)(2,1)} %all-gather.7.cloned.1.call-done, s32[]{:T(128)S(6)} %select_n.224), kind=kOutput, calls=%fused_computation.23 | convolution fusion | flops 2155872256 | bytes 27262980 | tf_op jit(solution)/shard_map/dot_general | solution.py:47
  497.6 11.3 %collective-permute-done.47 = bf16[2,256,1024]{2,1,0:T(8,128)(2,1)} collective-permute-done((bf16[2,256,1024]{2,1,0:T(8,128)(2,1)}, bf16[2,256,1024]{2,1,0:T(8,128)(2,1)}, u32[]{:S(2)}, u32[]{:S(2)}) %collective-permute-start.47) | collective-permute-done | bytes 1048608 | tf_op jit(solution)/shard_map/ppermute | solution.py:71
  555.9 12.6 %collective-permute-done.23 = bf16[2,256,768]{2,1,0:T(8,128)(2,1)} collective-permute-done((bf16[2,256,768]{2,1,0:T(8,128)(2,1)}, bf16[2,256,768]{2,1,0:T(8,128)(2,1)}, u32[]{:S(2)}, u32[]{:S(2)}) %collective-permute-start.23) | collective-permute-done | bytes 786464 | tf_op jit(solution)/shard_map/ppermute | solution.py:72
  595.4 5.7 add_convert_fusion.1
  620.3 8.5 %collective-permute-done.14 = bf16[512,2,512]{0,2,1:T(8,128)(2,1)} collective-permute-done((bf16[512,2,512]{0,2,1:T(8,128)(2,1)}, bf16[512,2,512]{0,2,1:T(8,128)(2,1)}, u32[]{:S(2)}, u32[]{:S(2)}) %collective-permute-start.14) | collective-permute-done | bytes 1048608 | tf_op jit(solution)/shard_map/ppermute | solution.py:221
  635.2 16.1 %collective-permute-done.5 = bf16[512,2,512]{0,2,1:T(8,128)(2,1)} collective-permute-done((bf16[512,2,512]{0,2,1:T(8,128)(2,1)}, bf16[512,2,512]{0,2,1:T(8,128)(2,1)}, u32[]{:S(2)}, u32[]{:S(2)}) %collective-permute-start.5) | collective-permute-done | bytes 1048608 | tf_op jit(solution)/shard_map/ppermute | solution.py:221
  679.5 110.7 %all-reduce.2.cloned.1.call-done = f32[24576]{0:T(1024)} async-done(((f32[24576]{0:T(1024)}), f32[24576]{0:T(1024)}) %all-reduce.2.cloned.1.call-update) | async-done | bytes 98320 | tf_op jit(solution)/shard_map/psum | solution.py:316
  (407 shorter events, 294.7 us)
Async XLA Ops:
  7.2 84.4 %all-gather.5.cloned.1.call-start = ((), (), s32[]{:S(2)}) async-start(), calls=%async_computation | async-start | bytes 3932160 | tf_op jit(solution)/shard_map/all_gather | solution.py:130
  15.5 207.1 %all-gather.9.cloned.1.call-start = ((), (), s32[]{:S(2)}) async-start(), calls=%async_computation.2 | async-start | bytes 5242880 | tf_op jit(solution)/shard_map/all_gather | solution.py:133
  24.2 235.1 %all-gather.11.cloned.1.call-start = ((), (), s32[]{:S(2)}) async-start(), calls=%async_computation.3 | async-start | bytes 5242880 | tf_op jit(solution)/shard_map/all_gather | solution.py:135
  30.8 52.9 %collective-permute-start.1 = (bf16[1024,2048]{0,1:T(8,128)(2,1)}, bf16[1024,2048]{0,1:T(8,128)(2,1)}, u32[]{:S(2)}, u32[]{:S(2)}) collective-permute-start(bf16[1024,2048]{0,1:T(8,128)(2,1)} %copy.305), channel_id=1, source_target_pairs={{0,1},{1,0},{2,3},{3,2},{4,5},{5,4},{6,7},{7,6},{8,9},{9,8},{10,11... | collective-permute-start | bytes 12582920 | tf_op jit(solution)/shard_map/ppermute | solution.py:116
  31.2 26.5 %collective-permute-start.9 = (bf16[1024,512]{1,0:T(8,128)(2,1)S(1)}, bf16[1024,512]{1,0:T(8,128)(2,1)}, u32[]{:S(2)}, u32[]{:S(2)}) collective-permute-start(bf16[1024,512]{1,0:T(8,128)(2,1)S(1)} %bitcast.311), channel_id=1, source_target_pairs={{0,8},{8,0},{1,9},{9,1},{2,10},{10,2},{3,11},{11,3},{4,12},{12,4},... | collective-permute-start | bytes 3145736 | tf_op jit(solution)/shard_map/ppermute | solution.py:154
  35.4 45.9 %collective-permute-start.11 = (bf16[1024,512]{1,0:T(8,128)(2,1)S(1)}, bf16[1024,512]{1,0:T(8,128)(2,1)}, u32[]{:S(2)}, u32[]{:S(2)}) collective-permute-start(bf16[1024,512]{1,0:T(8,128)(2,1)S(1)} %bitcast.313), channel_id=1, source_target_pairs={{0,24},{8,16},{16,8},{24,0},{1,25},{9,17},{17,9},{25,1},{2,26},{10... | collective-permute-start | bytes 3145736 | tf_op jit(solution)/shard_map/ppermute | solution.py:154
  36.5 298.8 %all-gather.7.cloned.1.call-start = ((), (), s32[]{:S(2)}) async-start(), calls=%async_computation.1 | async-start | bytes 4718592 | tf_op jit(solution)/shard_map/all_gather | solution.py:131
  83.7 59.0 %collective-permute-start.12 = (bf16[1024,2048]{1,0:T(8,128)(2,1)}, bf16[1024,2048]{1,0:T(8,128)(2,1)}, u32[]{:S(2)}, u32[]{:S(2)}) collective-permute-start(bf16[1024,2048]{1,0:T(8,128)(2,1)} %constant_dynamic-update-slice_fusion.6), channel_id=1, source_target_pairs={{0,1},{1,0},{2,3},{3,2},{4,5},{5,4},{6,7},{7,6},{8,9},{9,8},{10,11... | collective-permute-start | bytes 12582920 | tf_op jit(solution)/shard_map/ppermute | solution.py:116
  180.7 34.7 %collective-permute-start.32 = (bf16[2,256,256]{2,1,0:T(8,128)(2,1)S(1)}, bf16[2,256,256]{2,1,0:T(8,128)(2,1)S(1)}, u32[]{:S(2)}, u32[]{:S(2)}) collective-permute-start(bf16[2,256,256]{2,1,0:T(8,128)(2,1)S(1)} %fusion.65), channel_id=1, source_target_pairs={{6,4},{4,2},{2,0},{7,5},{5,3},{3,1},{14,12},{12,10},{10,8},{15,13}... | collective-permute-start | bytes 786440 | tf_op jit(solution)/shard_map/ppermute | solution.py:72
  182.0 608.3 %all-reduce.2.cloned.1.call-start = ((), (), s32[]{:S(2)}) async-start(), calls=%async_computation.4 | async-start | bytes 196608 | tf_op jit(solution)/shard_map/psum | solution.py:316
  292.8 107.2 %collective-permute-start.36 = (bf16[2,256,1024]{2,1,0:T(8,128)(2,1)}, bf16[2,256,1024]{2,1,0:T(8,128)(2,1)}, u32[]{:S(2)}, u32[]{:S(2)}) collective-permute-start(bf16[2,256,1024]{2,1,0:T(8,128)(2,1)} %get-tuple-element.112), channel_id=1, source_target_pairs={{0,2},{1,3},{8,10},{9,11},{16,18},{17,19},{24,26},{25,27}} | collective-permute-start | bytes 3145736 | tf_op jit(solution)/shard_map/ppermute | solution.py:71
  298.7 102.8 %collective-permute-start.39 = (bf16[2,256,1024]{2,1,0:T(8,128)(2,1)}, bf16[2,256,1024]{2,1,0:T(8,128)(2,1)}, u32[]{:S(2)}, u32[]{:S(2)}) collective-permute-start(bf16[2,256,1024]{2,1,0:T(8,128)(2,1)} %get-tuple-element.113), channel_id=1, source_target_pairs={{6,4},{7,5},{14,12},{15,13},{22,20},{23,21},{30,28},{31,29}} | collective-permute-start | bytes 3145736 | tf_op jit(solution)/shard_map/ppermute | solution.py:72
  315.3 90.0 %collective-permute-start.45 = (bf16[2,256,1024]{2,1,0:T(8,128)(2,1)}, bf16[2,256,1024]{2,1,0:T(8,128)(2,1)}, u32[]{:S(2)}, u32[]{:S(2)}) collective-permute-start(bf16[2,256,1024]{2,1,0:T(8,128)(2,1)} %get-tuple-element.106), channel_id=1, source_target_pairs={{0,2},{1,3},{8,10},{9,11},{16,18},{17,19},{24,26},{25,27}} | collective-permute-start | bytes 3145736 | tf_op jit(solution)/shard_map/ppermute | solution.py:71
  317.5 88.5 %collective-permute-start.48 = (bf16[2,256,1024]{2,1,0:T(8,128)(2,1)}, bf16[2,256,1024]{2,1,0:T(8,128)(2,1)}, u32[]{:S(2)}, u32[]{:S(2)}) collective-permute-start(bf16[2,256,1024]{2,1,0:T(8,128)(2,1)} %get-tuple-element.107), channel_id=1, source_target_pairs={{6,4},{7,5},{14,12},{15,13},{22,20},{23,21},{30,28},{31,29}} | collective-permute-start | bytes 3145736 | tf_op jit(solution)/shard_map/ppermute | solution.py:72
  364.2 34.7 %collective-permute-start.18 = (bf16[2,256,768]{2,1,0:T(8,128)(2,1)S(1)}, bf16[2,256,768]{2,1,0:T(8,128)(2,1)S(1)}, u32[]{:S(2)}, u32[]{:S(2)}) collective-permute-start(bf16[2,256,768]{2,1,0:T(8,128)(2,1)S(1)} %get-tuple-element.120), channel_id=1, source_target_pairs={{0,2},{1,3},{8,10},{9,11},{16,18},{17,19},{24,26},{25,27}} | collective-permute-start | bytes 2359304 | tf_op jit(solution)/shard_map/ppermute | solution.py:71
  403.9 37.7 %collective-permute-start.37 = (bf16[2,256,1024]{2,1,0:T(8,128)(2,1)S(1)}, bf16[2,256,1024]{2,1,0:T(8,128)(2,1)S(1)}, u32[]{:S(2)}, u32[]{:S(2)}) collective-permute-start(bf16[2,256,1024]{2,1,0:T(8,128)(2,1)S(1)} %get-tuple-element.110), channel_id=1, source_target_pairs={{0,2},{2,4},{1,3},{3,5},{8,10},{10,12},{9,11},{11,13},{16,18},{18,... | collective-permute-start | bytes 3145736 | tf_op jit(solution)/shard_map/ppermute | solution.py:71
  405.3 36.4 %collective-permute-start.40 = (bf16[2,256,1024]{2,1,0:T(8,128)(2,1)S(1)}, bf16[2,256,1024]{2,1,0:T(8,128)(2,1)S(1)}, u32[]{:S(2)}, u32[]{:S(2)}) collective-permute-start(bf16[2,256,1024]{2,1,0:T(8,128)(2,1)S(1)} %get-tuple-element.111), channel_id=1, source_target_pairs={{6,4},{4,2},{7,5},{5,3},{14,12},{12,10},{15,13},{13,11},{22,20},{2... | collective-permute-start | bytes 3145736 | tf_op jit(solution)/shard_map/ppermute | solution.py:72
  409.6 54.7 %collective-permute-start.46 = (bf16[2,256,1024]{2,1,0:T(8,128)(2,1)}, bf16[2,256,1024]{2,1,0:T(8,128)(2,1)S(1)}, u32[]{:S(2)}, u32[]{:S(2)}) collective-permute-start(bf16[2,256,1024]{2,1,0:T(8,128)(2,1)} %get-tuple-element.104), channel_id=1, source_target_pairs={{0,2},{2,4},{1,3},{3,5},{8,10},{10,12},{9,11},{11,13},{16,18},{18,... | collective-permute-start | bytes 3145736 | tf_op jit(solution)/shard_map/ppermute | solution.py:71
  410.9 54.6 %collective-permute-start.49 = (bf16[2,256,1024]{2,1,0:T(8,128)(2,1)S(1)}, bf16[2,256,1024]{2,1,0:T(8,128)(2,1)}, u32[]{:S(2)}, u32[]{:S(2)}) collective-permute-start(bf16[2,256,1024]{2,1,0:T(8,128)(2,1)S(1)} %get-tuple-element.105), channel_id=1, source_target_pairs={{6,4},{4,2},{7,5},{5,3},{14,12},{12,10},{15,13},{13,11},{22,20},{2... | collective-permute-start | bytes 3145736 | tf_op jit(solution)/shard_map/ppermute | solution.py:72
  420.8 54.2 %collective-permute-start.22 = (bf16[2,256,768]{2,1,0:T(8,128)(2,1)}, bf16[2,256,768]{2,1,0:T(8,128)(2,1)S(1)}, u32[]{:S(2)}, u32[]{:S(2)}) collective-permute-start(bf16[2,256,768]{2,1,0:T(8,128)(2,1)} %get-tuple-element.119), channel_id=1, source_target_pairs={{6,4},{4,2},{7,5},{5,3},{14,12},{12,10},{15,13},{13,11},{22,20},{2... | collective-permute-start | bytes 2359304 | tf_op jit(solution)/shard_map/ppermute | solution.py:72
  441.7 152.8 %collective-permute-start.13 = (bf16[1024,2048]{0,1:T(8,128)(2,1)}, bf16[1024,2048]{0,1:T(8,128)(2,1)}, u32[]{:S(2)}, u32[]{:S(2)}) collective-permute-start(bf16[1024,2048]{0,1:T(8,128)(2,1)} %slice.147), channel_id=1, source_target_pairs={{0,1},{1,0},{2,3},{3,2},{4,5},{5,4},{6,7},{7,6},{8,9},{9,8},{10,11... | collective-permute-start | bytes 12582920 | tf_op jit(solution)/shard_map/ppermute | solution.py:116
  444.0 53.6 %collective-permute-start.38 = (bf16[2,256,1024]{2,1,0:T(8,128)(2,1)}, bf16[2,256,1024]{2,1,0:T(8,128)(2,1)S(1)}, u32[]{:S(2)}, u32[]{:S(2)}) collective-permute-start(bf16[2,256,1024]{2,1,0:T(8,128)(2,1)} %get-tuple-element.108), channel_id=1, source_target_pairs={{0,2},{2,4},{4,6},{1,3},{3,5},{5,7},{8,10},{10,12},{12,14},{9,11},... | collective-permute-start | bytes 3145736 | tf_op jit(solution)/shard_map/ppermute | solution.py:71
  464.3 33.3 %collective-permute-start.41 = (bf16[2,256,1024]{2,1,0:T(8,128)(2,1)}, bf16[2,256,1024]{2,1,0:T(8,128)(2,1)S(1)}, u32[]{:S(2)}, u32[]{:S(2)}) collective-permute-start(bf16[2,256,1024]{2,1,0:T(8,128)(2,1)} %get-tuple-element.109), channel_id=1, source_target_pairs={{6,4},{4,2},{2,0},{7,5},{5,3},{3,1},{14,12},{12,10},{10,8},{15,13}... | collective-permute-start | bytes 3145736 | tf_op jit(solution)/shard_map/ppermute | solution.py:72
  469.1 39.8 %collective-permute-start.47 = (bf16[2,256,1024]{2,1,0:T(8,128)(2,1)}, bf16[2,256,1024]{2,1,0:T(8,128)(2,1)}, u32[]{:S(2)}, u32[]{:S(2)}) collective-permute-start(bf16[2,256,1024]{2,1,0:T(8,128)(2,1)} %get-tuple-element.102), channel_id=1, source_target_pairs={{0,2},{2,4},{4,6},{1,3},{3,5},{5,7},{8,10},{10,12},{12,14},{9,11},... | collective-permute-start | bytes 3145736 | tf_op jit(solution)/shard_map/ppermute | solution.py:71
  475.0 39.1 %collective-permute-start.50 = (bf16[2,256,1024]{2,1,0:T(8,128)(2,1)}, bf16[2,256,1024]{2,1,0:T(8,128)(2,1)}, u32[]{:S(2)}, u32[]{:S(2)}) collective-permute-start(bf16[2,256,1024]{2,1,0:T(8,128)(2,1)} %get-tuple-element.103), channel_id=1, source_target_pairs={{6,4},{4,2},{2,0},{7,5},{5,3},{3,1},{14,12},{12,10},{10,8},{15,13}... | collective-permute-start | bytes 3145736 | tf_op jit(solution)/shard_map/ppermute | solution.py:72
  497.6 107.8 %collective-permute-start.4 = (bf16[1024,2048]{0,1:T(8,128)(2,1)}, bf16[1024,2048]{0,1:T(8,128)(2,1)}, u32[]{:S(2)}, u32[]{:S(2)}) collective-permute-start(bf16[1024,2048]{0,1:T(8,128)(2,1)} %slice.137), channel_id=1, source_target_pairs={{0,1},{1,0},{2,3},{3,2},{4,5},{5,4},{6,7},{7,6},{8,9},{9,8},{10,11... | collective-permute-start | bytes 12582920 | tf_op jit(solution)/shard_map/ppermute | solution.py:116
  538.9 29.6 %collective-permute-start.23 = (bf16[2,256,768]{2,1,0:T(8,128)(2,1)}, bf16[2,256,768]{2,1,0:T(8,128)(2,1)}, u32[]{:S(2)}, u32[]{:S(2)}) collective-permute-start(bf16[2,256,768]{2,1,0:T(8,128)(2,1)} %fusion.52), channel_id=1, source_target_pairs={{6,4},{4,2},{2,0},{7,5},{5,3},{3,1},{14,12},{12,10},{10,8},{15,13}... | collective-permute-start | bytes 2359304 | tf_op jit(solution)/shard_map/ppermute | solution.py:72
  603.8 28.4 %collective-permute-start.16 = (bf16[512,2,512]{0,2,1:T(8,128)(2,1)S(1)}, bf16[512,2,512]{0,2,1:T(8,128)(2,1)}, u32[]{:S(2)}, u32[]{:S(2)}) collective-permute-start(bf16[512,2,512]{0,2,1:T(8,128)(2,1)S(1)} %dynamic-slice_bitcast_fusion.4), channel_id=1, source_target_pairs={{0,8},{8,0},{1,9},{9,1},{2,10},{10,2},{3,11},{11,3},{4,12},{12,4},... | collective-permute-start | bytes 3145736 | tf_op jit(solution)/shard_map/ppermute | solution.py:222
  612.4 38.9 %collective-permute-start.5 = (bf16[512,2,512]{0,2,1:T(8,128)(2,1)}, bf16[512,2,512]{0,2,1:T(8,128)(2,1)}, u32[]{:S(2)}, u32[]{:S(2)}) collective-permute-start(bf16[512,2,512]{0,2,1:T(8,128)(2,1)} %dynamic-slice_bitcast_fusion.7), channel_id=1, source_target_pairs={{0,16},{16,0},{1,17},{17,1},{2,18},{18,2},{3,19},{19,3},{4,20},{20... | collective-permute-start | bytes 3145736 | tf_op jit(solution)/shard_map/ppermute | solution.py:221
  618.7 36.4 %collective-permute-start.7 = (bf16[512,2,512]{0,2,1:T(8,128)(2,1)S(1)}, bf16[512,2,512]{0,2,1:T(8,128)(2,1)S(1)}, u32[]{:S(2)}, u32[]{:S(2)}) collective-permute-start(bf16[512,2,512]{0,2,1:T(8,128)(2,1)S(1)} %dynamic-slice_bitcast_fusion.6), channel_id=1, source_target_pairs={{0,8},{8,0},{1,9},{9,1},{2,10},{10,2},{3,11},{11,3},{4,12},{12,4},... | collective-permute-start | bytes 3145736 | tf_op jit(solution)/shard_map/ppermute | solution.py:222
  630.6 33.0 %collective-permute-start.15 = (bf16[512,512]{0,1:T(8,128)(2,1)S(1)}, bf16[512,512]{0,1:T(8,128)(2,1)S(1)}, u32[]{:S(2)}, u32[]{:S(2)}) collective-permute-start(bf16[512,512]{0,1:T(8,128)(2,1)S(1)} %dynamic-slice_bitcast_fusion.11), channel_id=1, source_target_pairs={{0,8},{8,0},{1,9},{9,1},{2,10},{10,2},{3,11},{11,3},{4,12},{12,4},... | collective-permute-start | bytes 1572872 | tf_op jit(solution)/shard_map/ppermute | solution.py:225
  633.8 30.0 %collective-permute-start.17 = (bf16[512,512]{0,1:T(8,128)(2,1)S(1)}, bf16[512,512]{0,1:T(8,128)(2,1)S(1)}, u32[]{:S(2)}, u32[]{:S(2)}) collective-permute-start(bf16[512,512]{0,1:T(8,128)(2,1)S(1)} %dynamic-slice_bitcast_fusion.10), channel_id=1, source_target_pairs={{0,16},{16,0},{1,17},{17,1},{2,18},{18,2},{3,19},{19,3},{4,20},{20... | collective-permute-start | bytes 1572872 | tf_op jit(solution)/shard_map/ppermute | solution.py:226
  (95 other events, 1285.5 us)
Sparse Core Ops, SparseCore 0:
  15.7 66.1 all-gather.4
  84.0 81.0 all-gather.8
  167.2 92.0 all-gather.10
  260.8 44.2 all-gather.6
  671.1 119.1 all-reduce.1

commit v2 on v1

v2 whole, which is shorter than its diff:
```python
import functools
import math

import jax
import jax.numpy as jnp
from jax import lax
from jax.experimental import pallas as pl
from jax.experimental.pallas import tpu as pltpu
from jax.sharding import Mesh, PartitionSpec as P

HEAD = 256
ROT = 64
LANES = 128
NEGATIVE = -1e30
VMEM_BYTES = 56 * 1024 * 1024
F32 = jnp.float32
BF16 = jnp.bfloat16


def rotary_tables(segment_rows):
    length = segment_rows.shape[1]
    before = jnp.sum(
        (segment_rows[:, None, :] < segment_rows[:, :, None]).astype(jnp.int32), axis=2
    )
    places = (jnp.arange(length, dtype=jnp.int32)[None] - before).astype(F32)
    frequency = 10000.0 ** (-jnp.arange(0, ROT, 2).astype(F32) / ROT)
    angles = (places[:, :, None] * frequency).reshape(-1, ROT // 2)
    cosine, sine = jnp.cos(angles), jnp.sin(angles)
    none = jnp.zeros_like(sine)
    rest = jnp.zeros((angles.shape[0], LANES - ROT), F32)
    return (
        jnp.concatenate([cosine, cosine, rest + 1.0], axis=1),
        jnp.concatenate([-sine, none, rest], axis=1),
        jnp.concatenate([none, sine, rest], axis=1),
    )


def rotate(values, self_factor, right_factor, left_factor):
    half = ROT // 2
    front = values[:, :LANES]
    turned = (
        front * self_factor
        + pltpu.roll(front, LANES - half, 1) * right_factor
        + pltpu.roll(front, half, 1) * left_factor
    )
    return jnp.concatenate([turned, values[:, LANES:]], axis=1)


def dot(left, right, left_dim, right_dim):
    return lax.dot_general(
        left, right, (((left_dim,), (right_dim,)), ((), ())), preferred_element_type=F32
    )


def whole(shape):
    return pl.BlockSpec(shape, lambda i: (0,) * len(shape), pipeline_mode=pl.Buffered(1))


def tile(rows, columns):
    return pl.BlockSpec((rows, columns), lambda i: (i, 0))


def run(body, steps, ins, outs, args, flops, transcendentals=0):
    shapes = [jax.ShapeDtypeStruct(shape, dtype) for _, shape, dtype in outs]
    moved = sum(a.size * a.dtype.itemsize for a in list(args) + shapes)
    return pl.pallas_call(
        body,
        grid=(steps,),
        in_specs=ins,
        out_specs=[spec for spec, _, _ in outs],
        out_shape=shapes,
        cost_estimate=pl.CostEstimate(
            flops=flops, bytes_accessed=moved, transcendentals=transcendentals
        ),
        compiler_params=pltpu.CompilerParams(vmem_limit_bytes=VMEM_BYTES),
    )(*args)


def statistics(x):
    center = x - jnp.mean(x, axis=-1, keepdims=True)
    inverse = lax.rsqrt(jnp.mean(center * center, axis=-1, keepdims=True) + 1e-05)
    return center * inverse, inverse


def either(steps, mine_ref, other_ref):
    return jnp.where(pl.program_id(0) < steps, mine_ref[...], other_ref[...])


def halves(rows, columns, steps):
    return [
        pl.BlockSpec((rows, columns), lambda i: (jnp.minimum(i, steps - 1), 0)),
        pl.BlockSpec((rows, columns), lambda i: (jnp.maximum(i - steps, 0), 0)),
    ]


def norm_body(steps, mine_ref, other_ref, gain_a, shift_a, gain_e, shift_e, normed_ref, expanded_ref):
    hat, _ = statistics(either(steps, mine_ref, other_ref).astype(F32))
    normed_ref[...] = (hat * gain_a[...] + shift_a[...]).astype(BF16)
    expanded_ref[...] = (hat * gain_e[...] + shift_e[...]).astype(BF16)


def gather_body(steps, starts_ref, *refs):
    pieces, out_ref = refs[:-1], refs[-1]
    span = pieces[0].shape[1]
    for k in range(len(pieces) // 2):
        columns = pl.ds(pl.multiple_of(starts_ref[k], span), span)
        out_ref[:, columns] = either(steps, pieces[2 * k], pieces[2 * k + 1])


def accumulate(ref, value):
    @pl.when(pl.program_id(0) == 0)
    def _():
        ref[...] = value

    @pl.when(pl.program_id(0) != 0)
    def _():
        ref[...] += value


def attention_body(
    normed_ref, joined_ref, bias_ref, self_ref, right_ref, left_ref, column_ref, row_ref, g_ref, dense_ref,
    mixed_ref, grad_ref, bias_grad_ref,
):
    length = normed_ref.shape[0]
    scale = 1.0 / math.sqrt(HEAD)
    factors = self_ref[...], right_ref[...], left_ref[...]
    raw = dot(normed_ref[...], joined_ref[...], 1, 0) + bias_ref[...]
    queries = (rotate(raw[:, :HEAD], *factors) * scale).astype(BF16)
    keyset = rotate(raw[:, HEAD : 2 * HEAD], *factors).astype(BF16)
    valueset = raw[:, 2 * HEAD :].astype(BF16)
    query_index = lax.broadcasted_iota(jnp.int32, (length, length), 0)
    key_index = lax.broadcasted_iota(jnp.int32, (length, length), 1)
    allowed = (column_ref[0] == row_ref[0]) & (key_index <= query_index)
    scores = jnp.where(allowed, dot(queries, keyset, 1, 1), NEGATIVE)
    shifted = jnp.exp(scores - jnp.max(scores, axis=-1, keepdims=True))
    probs = shifted / jnp.sum(shifted, axis=-1, keepdims=True)
    low = probs.astype(BF16)
    mixed_ref[...] = dot(low, valueset, 1, 0).astype(BF16)
    mixed_grad = dot(g_ref[...], dense_ref[...], 1, 1).astype(BF16)
    probs_grad = dot(mixed_grad, valueset, 1, 1)
    value_grad = dot(low, mixed_grad, 0, 0)
    inner = jnp.sum(probs_grad * probs, axis=-1, keepdims=True)
    score_grad = (probs * (probs_grad - inner)).astype(BF16)
    query_grad = rotate(dot(score_grad, keyset, 1, 0) * scale, *back_factors(factors))
    key_grad = rotate(dot(score_grad, queries, 0, 0), *back_factors(factors))
    joined_grad = jnp.concatenate([query_grad, key_grad, value_grad], axis=1).astype(BF16)
    grad_ref[...] = joined_grad
    accumulate(bias_grad_ref, jnp.sum(joined_grad.astype(F32), axis=0, keepdims=True))


def back_factors(factors):
    return factors[0], -factors[1], -factors[2]


def hidden_body(expanded_ref, up_ref, bias_ref, activated_ref, slope_ref):
    block = up_ref.shape[1] // 4
    for k in range(4):
        columns = pl.ds(k * block, block)
        hidden = dot(expanded_ref[...], up_ref[:, columns], 1, 0) + bias_ref[:, columns]
        below = 0.5 * (1.0 + lax.erf(hidden * math.sqrt(0.5)))
        density = jnp.exp(hidden * hidden * -0.5) * (1.0 / math.sqrt(2.0 * math.pi))
        activated_ref[:, columns] = (hidden * below).astype(BF16)
        slope_ref[:, columns] = (below + hidden * density).astype(BF16)


def terms_body(*refs):
    out_ref, start = refs[-1], 0
    for left_ref, right_ref in zip(refs[:-1:2], refs[1:-1:2]):
        stop = start + right_ref.shape[1]
        term = dot(left_ref[...], right_ref[...], 0, 0).astype(BF16)
        out_ref[:, :, :, start:stop] = term.reshape(*out_ref.shape[:3], stop - start)
        start = stop


def hidden_grad_body(g_ref, down_ref, slope_ref, grad_ref, bias_grad_ref):
    grad = dot(g_ref[...], down_ref[...], 1, 1) * slope_ref[...].astype(F32)
    grad = grad.astype(BF16)
    grad_ref[...] = grad
    accumulate(bias_grad_ref, jnp.sum(grad.astype(F32), axis=0, keepdims=True))


def store_blocks(ref, values):
    blocks, span = ref.shape[0], ref.shape[2]
    for k in range(blocks):
        ref[k] = values[:, k * span : (k + 1) * span].astype(BF16)


def forward_body(mixed_ref, dense_ref, active_ref, down_ref, out_ref):
    total = dot(mixed_ref[...], dense_ref[...], 1, 0)
    total += dot(active_ref[...], down_ref[...], 1, 0)
    store_blocks(out_ref, total)


def input_body(
    x_ref, joined_grad_ref, joined_ref, hidden_grad_ref, up_ref, gain_a, gain_e, out_ref, sums_ref
):
    normed_grad = dot(joined_grad_ref[...], joined_ref[...], 1, 1)
    expanded_grad = dot(hidden_grad_ref[...], up_ref[...], 1, 1)
    hat, inverse = statistics(x_ref[...].astype(F32))
    weighted = normed_grad * gain_a[...] + expanded_grad * gain_e[...]
    weighted_mean = jnp.mean(weighted, axis=-1, keepdims=True)
    along = jnp.mean(weighted * hat, axis=-1, keepdims=True)
    store_blocks(out_ref, inverse * (weighted - weighted_mean - hat * along))

    def down(values):
        return jnp.sum(values, axis=0, keepdims=True)

    sums = jnp.concatenate(
        [down(normed_grad * hat), down(normed_grad), down(expanded_grad * hat), down(expanded_grad)]
    )
    accumulate(sums_ref, sums)


def pick(array, index, axis):
    return lax.dynamic_index_in_dim(array, index, axis, keepdims=False)


def add_low(left, right):
    return (left.astype(F32) + right.astype(F32)).astype(BF16)


SWAP = [(0, 1), (1, 0)]


class Chain:
    def __init__(self, view, index, count):
        self.view, self.index, self.count, self.step = view, index, count, 0
        self.held = self.flight = ()

    def term(self, share):
        return pick(self.view, jnp.clip(share, 0, self.count - 1), 0)

    def send(self):
        self.step += 1
        step, count = self.step, self.count
        out = [self.term(self.index + count - step), self.term(self.index - count + step)]
        if self.held:
            out = [add_low(one, two) for one, two in zip(out, self.held)]
        self.flight = (
            lax.ppermute(out[0], "z", [(i, i + 1) for i in range(step)]),
            lax.ppermute(out[1], "z", [(count - 1 - i, count - 2 - i) for i in range(step)]),
        )

    def total(self):
        own = self.term(self.index).astype(F32)
        return (own + self.held[0].astype(F32) + self.held[1].astype(F32)).astype(BF16)


fence = lax.optimization_barrier


def solution(mesh):
    branches, models, datas = (mesh.shape[name] for name in ("branch", "mp", "dp"))
    cores = 2
    chips = datas // cores
    fine = Mesh(
        mesh.devices.reshape(branches, models, chips, cores), ("branch", "mp", "z", "core")
    )

    def on_device(
        block_input,
        cotangent,
        segments,
        attend_gain,
        attend_shift,
        joined_weight,
        joined_bias,
        dense_weight,
        dense_bias,
        expand_gain,
        expand_shift,
        up_weight,
        up_bias,
        down_weight,
        down_bias,
    ):
        rows, length, width = block_input.shape
        b, m, z, c = (lax.axis_index(name) for name in ("branch", "mp", "z", "core"))
        tokens = rows * length
        span = width // (branches * models)
        column_start = (b * models + m) * span
        heads = branches * cores
        head_columns = joined_weight.shape[1] // heads
        hidden_columns = up_weight.shape[1]
        part = down_weight.shape[0] // branches
        units = chips * part
        head_slot = b * cores + c
        row_share = width // (branches * datas)

        def partner(array, **flips):
            names = tuple(name for name, flip in flips.items() if flip)
            if not names:
                return array
            count = 2 ** len(names)
            return lax.ppermute(array, names, [(i, count - 1 - i) for i in range(count)])

        def swap_core(array):
            return partner(array, core=1)

        def in_core_order(mine, other):
            return jnp.where(c == 0, jnp.concatenate([mine, other]), jnp.concatenate([other, mine]))

        def columns_of(array, start, size):
            return lax.dynamic_slice_in_dim(array, start, size, array.ndim - 1)

        def unit_columns(array, core):
            return jnp.concatenate(
                [
                    columns_of(array, ((k * cores + core) * branches + b) * part, part)
                    for k in range(chips)
                ],
                axis=-1,
            )

        def gather(piece):
            return lax.all_gather(piece, "z", axis=0, tiled=True)

        x_own = block_input.reshape(tokens, width)
        g_piece = cotangent.reshape(tokens, span)
        joined_piece = in_core_order(
            columns_of(joined_weight, head_slot * head_columns, head_columns),
            swap_core(columns_of(joined_weight, (b * cores + 1 - c) * head_columns, head_columns)),
        )
        flips = [(db, dm) for db in range(2) for dm in range(2)]
        g_mine = [partner(g_piece, branch=db, mp=dm) for db, dm in flips]
        x_other = swap_core(x_own)
        segment_rows = jnp.concatenate([segments, swap_core(segments)])
        joined_piece, dense_weight = fence((joined_piece, dense_weight))
        spread_dense = chips == heads and HEAD == cores * dense_weight.shape[0]
        if spread_dense:
            few = HEAD // chips
            per_core = chips // cores
            dense_piece = 0
            for j in range(per_core):
                moves = [
                    (
                        (one * chips + one * cores + to) * cores + at,
                        (one * chips + at * per_core + j) * cores + to,
                    )
                    for one in range(branches)
                    for to in range(cores)
                    for at in range(cores)
                ]
                dense_piece = dense_piece + lax.ppermute(
                    dense_weight[j * few : (j + 1) * few], ("branch", "z", "core"), moves
                )
        else:
            dense_piece = dense_weight

        joined_bias_here = columns_of(joined_bias, (m * heads + head_slot) * head_columns, head_columns)
        up_bias_here = unit_columns(columns_of(up_bias, m * hidden_columns, hidden_columns), c)
        down_piece = lax.dynamic_slice_in_dim(down_weight, b * part, part, 0)

        def flat(vector):
            return vector.reshape(1, -1)

        all_tokens = 2 * tokens
        gains = flat(attend_gain), flat(expand_gain)
        small_tile = min(256, length)
        half_steps = tokens // small_tile
        joined_full = gather(joined_piece)
        x_other, joined_piece, up_weight, dense_piece = fence(
            (x_other, joined_piece, up_weight, dense_piece)
        )
        if spread_dense:
            dense_full = gather(dense_piece)
        else:
            dense_full = lax.all_gather(dense_piece, ("z", "core"), axis=0, tiled=True)
            dense_full = lax.dynamic_slice_in_dim(dense_full, head_slot * HEAD, HEAD, 0)
        up_piece = in_core_order(unit_columns(up_weight, c), swap_core(unit_columns(up_weight, 1 - c)))
        normed, expanded = run(
            functools.partial(norm_body, half_steps),
            2 * half_steps,
            halves(small_tile, width, half_steps) + [whole((1, width))] * 4,
            [(tile(small_tile, width), (all_tokens, width), BF16)] * 2,
            (x_own, x_other, gains[0], flat(attend_shift), gains[1], flat(expand_shift)),
            20 * all_tokens * width,
        )
        rotary = rotary_tables(segment_rows)
        normed, expanded, rotary, g_mine, up_piece, down_piece = fence(
            (normed, expanded, rotary, g_mine, up_piece, down_piece)
        )
        g_other = [swap_core(piece) for piece in g_mine]
        starts = jnp.stack([((b ^ db) * models + (m ^ dm)) * span for db, dm in flips])
        (g,) = run(
            functools.partial(gather_body, half_steps),
            2 * half_steps,
            [pl.BlockSpec(memory_space=pltpu.SMEM)]
            + [spec for _ in flips for spec in halves(small_tile, span, half_steps)],
            [(tile(small_tile, width), (all_tokens, width), BF16)],
            (starts, *[piece for pair in zip(g_mine, g_other) for piece in pair]),
            all_tokens * width,
        )
        normed, expanded, rotary, g, up_piece, down_piece = fence(
            (normed, expanded, rotary, g, up_piece, down_piece)
        )
        up_full = gather(up_piece)

        all_rows = 2 * rows
        mixed, joined_grad, joined_bias_grad = run(
            attention_body,
            all_rows,
            [
                tile(length, width),
                whole((width, head_columns)),
                whole((1, head_columns)),
                tile(length, LANES),
                tile(length, LANES),
                tile(length, LANES),
                pl.BlockSpec((1, length, 1), lambda i: (i, 0, 0)),
                pl.BlockSpec((1, 1, length), lambda i: (i, 0, 0)),
                tile(length, width),
                whole((HEAD, width)),
            ],
            [
                (tile(length, HEAD), (all_tokens, HEAD), BF16),
                (tile(length, head_columns), (all_tokens, head_columns), BF16),
                (whole((1, head_columns)), (1, head_columns), F32),
            ],
            (
                normed,
                joined_full,
                flat(joined_bias_here),
                *rotary,
                segment_rows[:, :, None],
                segment_rows[:, None, :],
                g,
                dense_full,
            ),
            2 * all_tokens * (width * (head_columns + HEAD) + 7 * length * HEAD),
            all_tokens * length,
        )

        live = dict(
            mixed=mixed, joined_grad=joined_grad, normed=normed, expanded=expanded, g=g, down=down_piece
        )

        def step(*landing):
            fresh, held, views = fence(
                (dict(live), [chain.flight for chain in landing], [chain.view for chain in waiting])
            )
            live.update(fresh)
            for chain, one in zip(landing, held):
                chain.held, chain.flight = one, ()
            for chain, view in zip(waiting, views):
                chain.view = view
            waiting.clear()

        waiting = []
        share_rows = cores * row_share

        def terms(*pairs):
            rows_tile = max(256, share_rows)
            group = rows_tile // share_rows
            groups = chips // group
            columns = sum(right.shape[1] for _, right in pairs)
            ins, args = [], []
            for left, right in pairs:
                ins += [pl.BlockSpec((all_tokens, rows_tile), lambda i: (0, i)), whole(right.shape)]
                args += [left, right]
            (view,) = run(
                terms_body,
                branches * groups,
                ins,
                [
                    (
                        pl.BlockSpec(
                            (group, 1, share_rows, columns), lambda i: (i % groups, i // groups, 0, 0)
                        ),
                        (chips, branches, share_rows, columns),
                        BF16,
                    )
                ],
                args,
                2 * all_tokens * width * columns,
            )
            chain = Chain(view, z, chips)
            waiting.append(chain)
            return chain

        def spread(chain):
            share = chain.total().reshape(branches, cores, row_share, -1)
            pieces = {}
            for db in range(2):
                for dc in range(2):
                    piece = pick(pick(share, b ^ db, 0), c ^ dc, 0)
                    pieces[db, dc] = partner(piece, branch=db, core=dc)
            return pieces

        def from_device(pieces, branch, core):
            same_core = c == core
            return jnp.where(
                b == branch,
                jnp.where(same_core, pieces[0, 0], pieces[0, 1]),
                jnp.where(same_core, pieces[1, 0], pieces[1, 1]),
            ).astype(F32)

        unit_flops = 2 * all_tokens * width * units
        big_tile = min(512, length)

        def hidden_values():
            return run(
                hidden_body,
                all_tokens // big_tile,
                [tile(big_tile, width), whole((width, units)), whole((1, units))],
                [(tile(big_tile, units), (all_tokens, units), BF16)] * 2,
                (live["expanded"], up_full, flat(up_bias_here)),
                unit_flops,
                2 * all_tokens * units,
            )

        def hidden_gradient():
            return run(
                hidden_grad_body,
                all_tokens // big_tile,
                [tile(big_tile, width), whole((units, width)), tile(big_tile, units)],
                [
                    (tile(big_tile, units), (all_tokens, units), BF16),
                    (whole((1, units)), (1, units), F32),
                ],
                (live["g"], down_full, live.pop("slope")),
                unit_flops,
            )

        blocks = branches * models

        def of_core(core, columns):
            return pl.BlockSpec((small_tile, columns), lambda i: (core * half_steps + i, 0))

        out_blocks = (
            pl.BlockSpec((blocks, small_tile, span), lambda i: (0, i, 0)),
            (blocks, tokens, span),
            BF16,
        )

        def input_terms(core):
            return run(
                input_body,
                half_steps,
                [
                    tile(small_tile, width),
                    of_core(core, head_columns),
                    whole((width, head_columns)),
                    of_core(core, units),
                    whole((width, units)),
                    whole((1, width)),
                    whole((1, width)),
                ],
                [out_blocks, (whole((4, width)), (4, width), F32)],
                (
                    (x_own, x_other)[core],
                    live["joined_grad"],
                    joined_full,
                    live["grad"],
                    up_full,
                    *gains,
                ),
                unit_flops // 2 + all_tokens * width * head_columns,
            )

        def forward_terms(core):
            return run(
                forward_body,
                half_steps,
                [
                    of_core(core, HEAD),
                    whole((HEAD, width)),
                    of_core(core, units),
                    whole((units, width)),
                ],
                [out_blocks],
                (live["mixed"], dense_full, live["active"], down_full),
                unit_flops // 2 + all_tokens * width * HEAD,
            )[0]

        def core_sum(mine, theirs):
            total = add_low(mine, theirs).reshape(branches, models, 2, tokens // 2, span)
            return total[:, :, 0], total[:, :, 1]

        def first_sum(pair):
            one, two = pair
            return (
                add_low(pick(one, b, 0), partner(pick(one, 1 - b, 0), branch=1)),
                add_low(pick(two, m, 1), partner(pick(two, 1 - m, 1), mp=1)),
            )

        def second_sum(pair):
            one, two = pair
            return jnp.concatenate(
                [
                    pick(one, m, 0).astype(F32) + partner(pick(one, 1 - m, 0), mp=1).astype(F32),
                    pick(two, b, 0).astype(F32) + partner(pick(two, 1 - b, 0), branch=1).astype(F32),
                ]
            )

        joined_chain = terms((normed, joined_grad), (g, mixed))
        step()
        down_full = gather(live.pop("down"))
        live.pop("normed")
        for _ in range(chips - 3):
            joined_chain.send()
            step(joined_chain)
        joined_chain.send()
        live["active"], live["slope"] = hidden_values()
        step(joined_chain)
        joined_chain.send()
        down_chain = terms((live["g"], live["active"]))
        step(joined_chain)
        joined_pieces = spread(joined_chain)
        for _ in range(chips - 4):
            down_chain.send()
            step(down_chain)
        down_chain.send()
        live["grad"], live["bias"] = hidden_gradient()
        step(down_chain)
        down_chain.send()
        up_chain = terms((live.pop("expanded"), live["grad"]))
        live.pop("g")
        step(down_chain)
        down_chain.send()
        for _ in range(chips - 3):
            up_chain.send()
            live["out_other"] = forward_terms(1)
            live["out_own"] = forward_terms(0)
            step(*([down_chain] if down_chain.flight else []), up_chain)
        up_chain.send()
        down_pieces = spread(down_chain)
        live["out_other"] = swap_core(live["out_other"])
        live["in_other"], live["sums_other"] = input_terms(1)
        step(up_chain)
        live["out"] = core_sum(live.pop("out_own"), live.pop("out_other"))
        up_chain.send()
        live["out"] = first_sum(live["out"])
        live["in_other"] = swap_core(live["in_other"])
        live["in_own"], live["sums_own"] = input_terms(0)
        step(up_chain)
        live["in"] = core_sum(live.pop("in_own"), live.pop("in_other"))
        live["in"] = first_sum(live["in"])
        up_pieces = spread(up_chain)
        forward_sum = second_sum(live.pop("out"))

        g_float = g_piece.astype(F32)
        joined_slot = lax.dynamic_update_slice(
            jnp.zeros_like(joined_bias),
            joined_bias_grad.reshape(-1),
            ((m * heads + head_slot) * head_columns,),
        )
        up_slot = lax.dynamic_update_slice(
            jnp.zeros((models, chips, cores, branches, part), F32),
            live.pop("bias").reshape(1, chips, 1, 1, part),
            (m, 0, c, b, 0),
        ).reshape(-1)
        out_slot = lax.dynamic_update_slice(
            jnp.zeros((width,), F32), jnp.sum(g_float, axis=0), (column_start,)
        )
        small = jnp.concatenate(
            [
                (live.pop("sums_own") + live.pop("sums_other")).reshape(-1),
                out_slot,
                joined_slot,
                up_slot,
            ]
        )
        small = small + partner(small, core=1)
        small = small + partner(small, branch=1)
        small = small + partner(small, mp=1)
        flip = 1
        while flip < chips:
            small = small + lax.ppermute(small, "z", [(i, i ^ flip) for i in range(chips)])
            flip *= 2
        input_sum = second_sum(live.pop("in"))

        residual = columns_of(x_own, column_start, span).astype(F32)
        column_bias = columns_of(dense_bias + down_bias, column_start, span)
        block_output = (residual + forward_sum + column_bias).astype(BF16)
        input_gradient = (g_float + input_sum).astype(BF16)

        def by_device(pieces):
            return jnp.stack(
                [
                    jnp.stack([from_device(pieces, one, core) for one in range(branches)])
                    for core in range(cores)
                ]
            )

        joined_out = jnp.concatenate(
            [from_device(joined_pieces, *divmod(k, cores))[:, :head_columns] for k in range(heads)],
            axis=1,
        )
        dense_out = jnp.concatenate(
            [from_device(joined_pieces, *divmod(k, cores))[:, head_columns:].T for k in range(heads)]
        )
        up_out = by_device(up_pieces).reshape(cores, branches, row_share, chips, part)
        up_out = up_out.transpose(2, 3, 0, 1, 4).reshape(row_share, hidden_columns)
        down_out = by_device(down_pieces).reshape(cores, branches, row_share, chips, part)
        down_out = down_out.transpose(3, 0, 1, 4, 2).reshape(hidden_columns, row_share)
        w = width
        joined_end = 5 * w + joined_bias.shape[0]
        return (
            block_output.reshape(rows, length, span),
            input_gradient.reshape(rows, length, span),
            small[:w],
            small[w : 2 * w],
            joined_out,
            small[5 * w : joined_end],
            dense_out,
            small[4 * w : 5 * w],
            small[2 * w : 3 * w],
            small[3 * w : 4 * w],
            up_out,
            small[joined_end:],
            down_out,
            small[4 * w : 5 * w],
        )

    data = ("z", "core")
    everything = ("branch", "z", "core")
    in_specs = (
        P(data, None, None),
        P(data, None, ("branch", "mp")),
        P(data, None),
        P(),
        P(),
        P(data, "mp"),
        P(),
        P(("mp", "z", "core"), None),
        P(),
        P(),
        P(),
        P(data, "mp"),
        P(),
        P(("mp", "z", "core"), None),
        P(),
    )
    out_specs = (
        P(data, None, ("branch", "mp")),
        P(data, None, ("branch", "mp")),
        P(),
        P(),
        P(everything, "mp"),
        P(),
        P("mp", everything),
        P(),
        P(),
        P(),
        P(everything, "mp"),
        P(),
        P("mp", everything),
        P(),
    )
    return jax.shard_map(
        on_device, mesh=fine, in_specs=in_specs, out_specs=out_specs, check_vma=False
    )
```

time: 807 us -> 646 us (0.80)
  matrix products: 183 us -> 0 us
  Pallas kernels: 0 us -> 178 us
  waiting for transfers between devices: 309 us -> 177 us
  local copies, waits for them, and re-layouts: 132 us -> 56.7 us
  starting transfers between devices: 81.4 us -> 127 us
    dot_general x18 -> x0, matrix products: 183 us -> none  [the longest x12 177 us: dot(): lax.dot_general(left, right, (((left_dim,), (right_dim,)), ((), ())), pre...]
    pallas_call x0 -> x12, Pallas kernels: none -> 178 us  [run(): pl.pallas_call(body, grid=(steps,), in_specs=ins, out_specs=[spec for spe...]
    psum x1 -> x0, waiting for transfers between devices: 111 us -> none  [on_device(): small = lax.psum(small, ('branch', 'mp', 'z', 'core'))]
    ppermute x54 -> x55, starting transfers between devices: 81.2 us -> 126 us  [the longest x9 70.9 us: send(): lax.ppermute(out[0], 'z', [(i, i + 1) for i in range(step)])]
    ppermute x54 -> x55, waiting for transfers between devices: 197 us -> 153 us  [the longest x9 68.7 us: send(): lax.ppermute(out[0], 'z', [(i, i + 1) for i in range(step)])]
    all_gather x4, waiting for transfers between devices: 0.94 us -> 24.2 us  [gather(): return lax.all_gather(piece, 'z', axis=0, tiled=True)]
    dynamic_update_slice x21 -> x1, local copies, waits for them, and re-layouts: 23.9 us -> 1.43 us  [on_device(): lax.dynamic_update_slice(jnp.zeros_like(joined_bias), joined_bias_grad.re...]
    unnamed x152 -> x89, local copies, waits for them, and re-layouts: 28.8 us -> 6.63 us
  transfers between devices with their start and end apart: 59 -> 59, of which waited for: 27 -> 19; matrix products, arithmetic and copies ran while one was open for 47% -> 19% of each run, Pallas kernels for 0% -> 28%
where the time goes in v2:
time: 646 us; the launch traced here: 636 us
  Pallas kernels  178 us (28%)
  waiting for transfers between devices  177 us (27%)
  starting transfers between devices  127 us (20%)
  other arithmetic  81.5 us (13%)
  local copies, waits for them, and re-layouts  56.7 us (9%)
  between operations  15.1 us (2%)
    pallas_call x12, Pallas kernels, run(): pl.pallas_call(body, grid=(steps,), in_specs=ins, out_specs=[spec for spe...  178 us
    ppermute x9, starting transfers between devices, send(): lax.ppermute(out[0], 'z', [(i, i + 1) for i in range(step)])  70.9 us
    ppermute x9, waiting for transfers between devices, send(): lax.ppermute(out[0], 'z', [(i, i + 1) for i in range(step)])  68.7 us
    ppermute x9, waiting for transfers between devices, send(): lax.ppermute(out[1], 'z', [(count - 1 - i, count - 2 - i) for i in range(...  44.3 us
    convert_element_type x12, other arithmetic, add_low(): return (left.astype(F32) + right.astype(F32)).astype(BF16)  34.6 us
    ppermute x33, starting transfers between devices, partner(): lax.ppermute(array, names, [(i, count - 1 - i) for i in range(count)])  34.5 us
    ppermute x33, waiting for transfers between devices, partner(): lax.ppermute(array, names, [(i, count - 1 - i) for i in range(count)])  32.8 us
    all_gather x4, waiting for transfers between devices, gather(): return lax.all_gather(piece, 'z', axis=0, tiled=True)  24.2 us
  transfers between devices with their start and end apart: 59, of which 19 were waited for; matrix products, arithmetic and copies ran while one was open for 19% of the time, Pallas kernels for 28%

profile of v2, /device:TPU:0, one launch (start us, length us, event | category | flops | bytes accessed | tf_op | source)
XLA Modules:
  0.0 635.6 jit_solution(4716126304380072790)
XLA Ops:
  26.7 5.4 multiply_sine_fusion
  32.0 5.7 collective-permute-done.3
  41.5 10.7 %collective-permute-start.8 = (bf16[256,1024]{1,0:T(8,128)(2,1)}, bf16[256,1024]{1,0:T(8,128)(2,1)}, u32[]{:S(2)}, u32[]{:S(2)}) collective-permute-start(bf16[256,1024]{1,0:T(8,128)(2,1)} %pad_maximum_fusion.2), channel_id=1, source_target_pairs={{0,1},{1,0},{2,3},{3,2},{4,5},{5,4},{6,7},{7,6},{8,9},{9,8},{10,11... | collective-permute-start | bytes 1572872 | tf_op jit(solution)/shard_map/ppermute | solution.py:295
  56.3 14.4 %shard_map.254 = (bf16[2048,2048]{1,0:T(8,128)(2,1)}, bf16[2048,2048]{1,0:T(8,128)(2,1)}) custom-call(bf16[1024,2048]{1,0:T(8,128)(2,1)} %bitcast.215, bf16[1024,2048]{1,0:T(8,128)(2,1)} %collective-permute-done.other_ref.x_ref, f32[1,2048]{1,0:T(1,128)} %bitcast.251, f32[1,2048]{1,0:T(1,128)} %bitcast.249, f32[1,2048]{1,0:T(1,128)} %bitcast.254, ...), custom_call_target="tpu_custom_call" | custom-call | flops 83886080 | bytes 25198592 | tf_op jit(solution)/shard_map/pallas_call | solution.py:66
  80.8 9.6 %shard_map.255.g_ref.refs_2_.refs_0_ = bf16[2048,2048]{1,0:T(8,128)(2,1)} custom-call(s32[4]{0:T(128)} %pad_add_fusion.1.starts_ref, bf16[1024,512]{1,0:T(8,128)(2,1)} %bitcast.221, bf16[1024,512]{1,0:T(8,128)(2,1)} %copy-done.25, bf16[1024,512]{1,0:T(8,128)(2,1)} %collective-permute-done.5.refs_2_, bf16[1024,512]{1,0:T(8,128)(2,1)} %copy-done.26, ...), custom_call_target="tpu_custom_call" | custom-call | flops 4194304 | bytes 16777232 | tf_op jit(solution)/shard_map/pallas_call | solution.py:66
  93.8 24.2 %all-gather.7.cloned.1.call-done.dense_ref = bf16[256,2048]{1,0:T(8,128)(2,1)} async-done(((bf16[64,2048]{1,0:T(8,128)(2,1)}), bf16[256,2048]{1,0:T(8,128)(2,1)}) %all-gather.7.cloned.1.call-update) | async-done | bytes 1048592 | tf_op jit(solution)/shard_map/all_gather | solution.py:316
  118.0 24.1 %shard_map.256 = (bf16[2048,256]{1,0:T(8,128)(2,1)}, bf16[2048,768]{1,0:T(8,128)(2,1)}, f32[1,768]{1,0:T(1,128)}) custom-call(bf16[2048,2048]{1,0:T(8,128)(2,1)} %get-tuple-element.143.normed_ref.refs_0_, bf16[2048,768]{1,0:T(8,128)(2,1)} %all-gather.5.cloned.1.call-done.joined_ref, f32[1,768]{1,0:T(1,128)} %reshape.248.bias_ref, ...), custom_call_target="tpu_custom_call" | custom-call | flops 12348030976 | bytes 28334080 | tf_op jit(solution)/shard_map/pallas_call | solution.py:66
  142.1 15.7 %shard_map.257 = bf16[4,2,256,1024]{3,2,1,0:T(8,128)(2,1)} custom-call(bf16[2048,2048]{1,0:T(8,128)(2,1)} %get-tuple-element.143.normed_ref.refs_0_, bf16[2048,768]{1,0:T(8,128)(2,1)} %get-tuple-element.210.refs_1_.joined_grad_ref, bf16[2048,2048]{1,0:T(8,128)(2,1)} %shard_map.255.g_ref.refs_2_.refs_0_, bf16[2048,256]{1,0:T(8,128)(2,1)} %get-tuple-element.194.refs_3_.mixed_ref), custom_call_target="tpu_custom_call" | custom-call | flops 8589934592 | bytes 25165824 | tf_op jit(solution)/shard_map/pallas_call | solution.py:66
  160.2 4.6 collective-permute-start.13
  164.8 44.3 %collective-permute-done.13 = bf16[2,256,1024]{2,1,0:T(8,128)(2,1)} collective-permute-done((bf16[2,256,1024]{2,1,0:T(8,128)(2,1)S(1)}, bf16[2,256,1024]{2,1,0:T(8,128)(2,1)}, u32[]{:S(2)}, u32[]{:S(2)}) %collective-permute-start.13) | collective-permute-done | bytes 1048608 | tf_op jit(solution)/shard_map/ppermute | solution.py:240
  213.6 5.1 collective-permute-start.15
  220.3 16.6 %shard_map.258 = (bf16[2048,1024]{1,0:T(8,128)(2,1)}, bf16[2048,1024]{1,0:T(8,128)(2,1)}) custom-call(bf16[2048,2048]{1,0:T(8,128)(2,1)} %get-tuple-element.189.expanded_ref.refs_0_, bf16[2048,1024]{1,0:T(8,128)(2,1)} %all-gather.9.cloned.1.call-done.up_ref, f32[1,1024]{1,0:T(1,128)} %bitcast.258), custom_call_target="tpu_custom_call" | custom-call | flops 8589934592 | bytes 20975616 | tf_op jit(solution)/shard_map/pallas_call | solution.py:66
  236.9 11.7 %collective-permute-done.15 = bf16[2,256,1024]{2,1,0:T(8,128)(2,1)S(1)} collective-permute-done((bf16[2,256,1024]{2,1,0:T(8,128)(2,1)S(1)}, bf16[2,256,1024]{2,1,0:T(8,128)(2,1)S(1)}, u32[]{:S(2)}, u32[]{:S(2)}) %collective-permute-start.15) | collective-permute-done | bytes 1048608 | tf_op jit(solution)/shard_map/ppermute | solution.py:240
  252.2 14.3 %collective-permute-start.17 = (bf16[2,256,1024]{2,1,0:T(8,128)(2,1)}, bf16[2,256,1024]{2,1,0:T(8,128)(2,1)S(1)}, u32[]{:S(2)}, u32[]{:S(2)}) collective-permute-start(bf16[2,256,1024]{2,1,0:T(8,128)(2,1)} %get-tuple-element.291), channel_id=1, source_target_pairs={{0,2},{2,4},{4,6},{1,3},{3,5},{5,7},{8,10},{10,12},{12,14},{9,11},... | collective-permute-start | bytes 3145736 | tf_op jit(solution)/shard_map/ppermute | solution.py:240
  266.5 14.2 %shard_map.259 = bf16[4,2,256,1024]{3,2,1,0:T(8,128)(2,1)} custom-call(bf16[2048,2048]{1,0:T(8,128)(2,1)} %shard_map.255.g_ref.refs_2_.refs_0_, bf16[2048,1024]{1,0:T(8,128)(2,1)} %get-tuple-element.190.refs_1_.active_ref), custom_call_target="tpu_custom_call" | custom-call | flops 8589934592 | bytes 16777216 | tf_op jit(solution)/shard_map/pallas_call | solution.py:66
  280.7 44.2 %collective-permute-done.18 = bf16[2,256,1024]{2,1,0:T(8,128)(2,1)S(1)} collective-permute-done((bf16[2,256,1024]{2,1,0:T(8,128)(2,1)}, bf16[2,256,1024]{2,1,0:T(8,128)(2,1)S(1)}, u32[]{:S(2)}, u32[]{:S(2)}) %collective-permute-start.18) | collective-permute-done | bytes 1048608 | tf_op jit(solution)/shard_map/ppermute | solution.py:241
  329.3 10.3 %collective-permute-start.19 = (bf16[2,256,1024]{2,1,0:T(8,128)(2,1)S(1)}, bf16[2,256,1024]{2,1,0:T(8,128)(2,1)}, u32[]{:S(2)}, u32[]{:S(2)}) collective-permute-start(bf16[2,256,1024]{2,1,0:T(8,128)(2,1)S(1)} %get-tuple-element.289), channel_id=1, source_target_pairs={{0,2},{1,3},{8,10},{9,11},{16,18},{17,19},{24,26},{25,27}} | collective-permute-start | bytes 3145736 | tf_op jit(solution)/shard_map/ppermute | solution.py:240
  339.6 14.8 %shard_map.260 = (bf16[2048,1024]{1,0:T(8,128)(2,1)}, f32[1,1024]{1,0:T(1,128)}) custom-call(bf16[2048,2048]{1,0:T(8,128)(2,1)} %shard_map.255.g_ref.refs_2_.refs_0_, bf16[1024,2048]{1,0:T(8,128)(2,1)} %all-gather.11.cloned.1.call-done.down_ref, bf16[2048,1024]{1,0:T(8,128)(2,1)} %get-tuple-element.175.slope_ref), custom_call_target="tpu_custom_call" | custom-call | flops 8589934592 | bytes 20975616 | tf_op jit(solution)/shard_map/pallas_call | solution.py:66
  359.0 4.8 collective-permute-start.21
  363.8 14.1 %shard_map.261 = bf16[4,2,256,1024]{3,2,1,0:T(8,128)(2,1)} custom-call(bf16[2048,2048]{1,0:T(8,128)(2,1)} %get-tuple-element.189.expanded_ref.refs_0_, bf16[2048,1024]{1,0:T(8,128)(2,1)} %get-tuple-element.208.refs_1_.hidden_grad_ref), custom_call_target="tpu_custom_call" | custom-call | flops 8589934592 | bytes 16777216 | tf_op jit(solution)/shard_map/pallas_call | solution.py:66
  384.4 7.6 %collective-permute-start.25 = (bf16[2,256,1024]{2,1,0:T(8,128)(2,1)}, bf16[2,256,1024]{2,1,0:T(8,128)(2,1)}, u32[]{:S(2)}, u32[]{:S(2)}) collective-permute-start(bf16[2,256,1024]{2,1,0:T(8,128)(2,1)} %get-tuple-element.283), channel_id=1, source_target_pairs={{0,2},{1,3},{8,10},{9,11},{16,18},{17,19},{24,26},{25,27}} | collective-permute-start | bytes 3145736 | tf_op jit(solution)/shard_map/ppermute | solution.py:240
  396.9 14.9 %collective-permute-start.23 = (bf16[2,256,1024]{2,1,0:T(8,128)(2,1)}, bf16[2,256,1024]{2,1,0:T(8,128)(2,1)}, u32[]{:S(2)}, u32[]{:S(2)}) collective-permute-start(bf16[2,256,1024]{2,1,0:T(8,128)(2,1)} %get-tuple-element.285), channel_id=1, source_target_pairs={{0,2},{2,4},{4,6},{1,3},{3,5},{5,7},{8,10},{10,12},{12,14},{9,11},... | collective-permute-start | bytes 3145736 | tf_op jit(solution)/shard_map/ppermute | solution.py:240
  411.7 9.9 %shard_map.263 = bf16[4,1024,512]{2,1,0:T(8,128)(2,1)} custom-call(bf16[2048,256]{1,0:T(8,128)(2,1)} %get-tuple-element.194.refs_3_.mixed_ref, bf16[256,2048]{1,0:T(8,128)(2,1)} %all-gather.7.cloned.1.call-done.dense_ref, bf16[2048,1024]{1,0:T(8,128)(2,1)} %get-tuple-element.190.refs_1_.active_ref, bf16[1024,2048]{1,0:T(8,128)(2,1)} %all-gather.11.cloned.1.call-done.down_ref), custom_call_target="tpu_custom_call" | custom-call | flops 5368709120 | bytes 14680064 | tf_op jit(solution)/shard_map/pallas_call | solution.py:66
  421.7 10.1 %shard_map.262 = bf16[4,1024,512]{2,1,0:T(8,128)(2,1)} custom-call(bf16[2048,256]{1,0:T(8,128)(2,1)} %get-tuple-element.194.refs_3_.mixed_ref, bf16[256,2048]{1,0:T(8,128)(2,1)} %all-gather.7.cloned.1.call-done.dense_ref, bf16[2048,1024]{1,0:T(8,128)(2,1)} %get-tuple-element.190.refs_1_.active_ref, bf16[1024,2048]{1,0:T(8,128)(2,1)} %all-gather.11.cloned.1.call-done.down_ref), custom_call_target="tpu_custom_call" | custom-call | flops 5368709120 | bytes 14680064 | tf_op jit(solution)/shard_map/pallas_call | solution.py:66
  431.8 4.1 fusion.15
  453.8 10.3 %collective-permute-done.28 = bf16[2,256,1024]{2,1,0:T(8,128)(2,1)} collective-permute-done((bf16[2,256,1024]{2,1,0:T(8,128)(2,1)}, bf16[2,256,1024]{2,1,0:T(8,128)(2,1)}, u32[]{:S(2)}, u32[]{:S(2)}) %collective-permute-start.28) | collective-permute-done | bytes 1048608 | tf_op jit(solution)/shard_map/ppermute | solution.py:240
  465.6 17.4 %shard_map.264 = (bf16[4,1024,512]{2,1,0:T(8,128)(2,1)}, f32[4,2048]{1,0:T(4,128)}) custom-call(bf16[1024,2048]{1,0:T(8,128)(2,1)} %collective-permute-done.other_ref.x_ref, bf16[2048,768]{1,0:T(8,128)(2,1)} %get-tuple-element.210.refs_1_.joined_grad_ref, bf16[2048,768]{1,0:T(8,128)(2,1)} %all-gather.5.cloned.1.call-done.joined_ref, ...), custom_call_target="tpu_custom_call" | custom-call | flops 7516192768 | bytes 23117824 | tf_op jit(solution)/shard_map/pallas_call | solution.py:66
  503.3 5.3 collective-permute-start.33
  508.7 17.4 %shard_map.265 = (bf16[4,1024,512]{2,1,0:T(8,128)(2,1)}, f32[4,2048]{1,0:T(4,128)}) custom-call(bf16[1024,2048]{1,0:T(8,128)(2,1)} %bitcast.216, bf16[2048,768]{1,0:T(8,128)(2,1)} %get-tuple-element.210.refs_1_.joined_grad_ref, bf16[2048,768]{1,0:T(8,128)(2,1)} %all-gather.5.cloned.1.call-done.joined_ref, ...), custom_call_target="tpu_custom_call" | custom-call | flops 7516192768 | bytes 23117824 | tf_op jit(solution)/shard_map/pallas_call | solution.py:66
  547.8 13.9 %collective-permute-done.39 = bf16[2,512,512]{2,1,0:T(8,128)(2,1)} collective-permute-done((bf16[2,512,512]{2,1,0:T(8,128)(2,1)}, bf16[2,512,512]{2,1,0:T(8,128)(2,1)}, u32[]{:S(2)}, u32[]{:S(2)}) %collective-permute-start.39) | collective-permute-done | bytes 1048608 | tf_op jit(solution)/shard_map/ppermute | solution.py:295
  564.7 4.9 collective-permute-done.37
  601.7 5.0 convert_bitcast_fusion
  (304 shorter events, 190.9 us)
Async XLA Ops:
  7.2 86.6 %all-gather.5.cloned.1.call-start = ((), (), s32[]{:S(2)}) async-start(), calls=%async_computation | async-start | bytes 3932160 | tf_op jit(solution)/shard_map/all_gather | solution.py:316
  9.8 28.8 %collective-permute-start = (bf16[1024,2048]{1,0:T(8,128)(2,1)}, bf16[1024,2048]{1,0:T(8,128)(2,1)}, u32[]{:S(2)}, u32[]{:S(2)}) collective-permute-start(bf16[1024,2048]{1,0:T(8,128)(2,1)} %bitcast.214), channel_id=1, source_target_pairs={{0,1},{1,0},{2,3},{3,2},{4,5},{5,4},{6,7},{7,6},{8,9},{9,8},{10,11... | collective-permute-start | bytes 12582920 | tf_op jit(solution)/shard_map/ppermute | solution.py:295
  13.7 104.2 %all-gather.7.cloned.1.call-start = ((), (), s32[]{:S(2)}) async-start(), calls=%async_computation.1 | async-start | bytes 1310720 | tf_op jit(solution)/shard_map/all_gather | solution.py:316
  13.8 59.4 %collective-permute-start.7 = (bf16[1024,512]{1,0:T(8,128)(2,1)S(1)}, bf16[1024,512]{1,0:T(8,128)(2,1)}, u32[]{:S(2)}, u32[]{:S(2)}) collective-permute-start(bf16[1024,512]{1,0:T(8,128)(2,1)S(1)} %bitcast.222), channel_id=1, source_target_pairs={{0,24},{8,16},{16,8},{24,0},{1,25},{9,17},{17,9},{25,1},{2,26},{10... | collective-permute-start | bytes 3145736 | tf_op jit(solution)/shard_map/ppermute | solution.py:295
  17.7 55.5 %collective-permute-start.6 = (bf16[1024,512]{1,0:T(8,128)(2,1)S(1)}, bf16[1024,512]{1,0:T(8,128)(2,1)}, u32[]{:S(2)}, u32[]{:S(2)}) collective-permute-start(bf16[1024,512]{1,0:T(8,128)(2,1)S(1)} %bitcast.223), channel_id=1, source_target_pairs={{0,16},{16,0},{1,17},{17,1},{2,18},{18,2},{3,19},{19,3},{4,20},{20... | collective-permute-start | bytes 3145736 | tf_op jit(solution)/shard_map/ppermute | solution.py:295
  37.7 35.5 %collective-permute-start.5 = (bf16[1024,512]{1,0:T(8,128)(2,1)S(1)}, bf16[1024,512]{1,0:T(8,128)(2,1)}, u32[]{:S(2)}, u32[]{:S(2)}) collective-permute-start(bf16[1024,512]{1,0:T(8,128)(2,1)S(1)} %bitcast.224), channel_id=1, source_target_pairs={{0,8},{8,0},{1,9},{9,1},{2,10},{10,2},{3,11},{11,3},{4,12},{12,4},... | collective-permute-start | bytes 3145736 | tf_op jit(solution)/shard_map/ppermute | solution.py:295
  41.5 29.1 %collective-permute-start.8 = (bf16[256,1024]{1,0:T(8,128)(2,1)}, bf16[256,1024]{1,0:T(8,128)(2,1)}, u32[]{:S(2)}, u32[]{:S(2)}) collective-permute-start(bf16[256,1024]{1,0:T(8,128)(2,1)} %pad_maximum_fusion.2), channel_id=1, source_target_pairs={{0,1},{1,0},{2,3},{3,2},{4,5},{5,4},{6,7},{7,6},{8,9},{9,8},{10,11... | collective-permute-start | bytes 1572872 | tf_op jit(solution)/shard_map/ppermute | solution.py:295
  54.2 166.0 %all-gather.9.cloned.1.call-start = ((), (), s32[]{:S(2)}) async-start(), calls=%async_computation.2 | async-start | bytes 5242880 | tf_op jit(solution)/shard_map/all_gather | solution.py:316
  90.4 249.2 %all-gather.11.cloned.1.call-start = ((), (), s32[]{:S(2)}) async-start(), calls=%async_computation.3 | async-start | bytes 5242880 | tf_op jit(solution)/shard_map/all_gather | solution.py:316
  160.2 48.9 %collective-permute-start.13 = (bf16[2,256,1024]{2,1,0:T(8,128)(2,1)S(1)}, bf16[2,256,1024]{2,1,0:T(8,128)(2,1)}, u32[]{:S(2)}, u32[]{:S(2)}) collective-permute-start(bf16[2,256,1024]{2,1,0:T(8,128)(2,1)S(1)} %get-tuple-element.295), channel_id=1, source_target_pairs={{0,2},{1,3},{8,10},{9,11},{16,18},{17,19},{24,26},{25,27}} | collective-permute-start | bytes 3145736 | tf_op jit(solution)/shard_map/ppermute | solution.py:240
  213.6 35.0 %collective-permute-start.15 = (bf16[2,256,1024]{2,1,0:T(8,128)(2,1)S(1)}, bf16[2,256,1024]{2,1,0:T(8,128)(2,1)S(1)}, u32[]{:S(2)}, u32[]{:S(2)}) collective-permute-start(bf16[2,256,1024]{2,1,0:T(8,128)(2,1)S(1)} %get-tuple-element.293), channel_id=1, source_target_pairs={{0,2},{2,4},{1,3},{3,5},{8,10},{10,12},{9,11},{11,13},{16,18},{18,... | collective-permute-start | bytes 3145736 | tf_op jit(solution)/shard_map/ppermute | solution.py:240
  250.9 74.0 %collective-permute-start.18 = (bf16[2,256,1024]{2,1,0:T(8,128)(2,1)}, bf16[2,256,1024]{2,1,0:T(8,128)(2,1)S(1)}, u32[]{:S(2)}, u32[]{:S(2)}) collective-permute-start(bf16[2,256,1024]{2,1,0:T(8,128)(2,1)} %get-tuple-element.290), channel_id=1, source_target_pairs={{6,4},{4,2},{2,0},{7,5},{5,3},{3,1},{14,12},{12,10},{10,8},{15,13}... | collective-permute-start | bytes 3145736 | tf_op jit(solution)/shard_map/ppermute | solution.py:241
  252.2 72.7 %collective-permute-start.17 = (bf16[2,256,1024]{2,1,0:T(8,128)(2,1)}, bf16[2,256,1024]{2,1,0:T(8,128)(2,1)S(1)}, u32[]{:S(2)}, u32[]{:S(2)}) collective-permute-start(bf16[2,256,1024]{2,1,0:T(8,128)(2,1)} %get-tuple-element.291), channel_id=1, source_target_pairs={{0,2},{2,4},{4,6},{1,3},{3,5},{5,7},{8,10},{10,12},{12,14},{9,11},... | collective-permute-start | bytes 3145736 | tf_op jit(solution)/shard_map/ppermute | solution.py:240
  327.6 26.8 %collective-permute-start.20 = (bf16[2,256,1024]{2,1,0:T(8,128)(2,1)}, bf16[2,256,1024]{2,1,0:T(8,128)(2,1)}, u32[]{:S(2)}, u32[]{:S(2)}) collective-permute-start(bf16[2,256,1024]{2,1,0:T(8,128)(2,1)} %get-tuple-element.288), channel_id=1, source_target_pairs={{6,4},{7,5},{14,12},{15,13},{22,20},{23,21},{30,28},{31,29}} | collective-permute-start | bytes 3145736 | tf_op jit(solution)/shard_map/ppermute | solution.py:241
  329.3 25.2 %collective-permute-start.19 = (bf16[2,256,1024]{2,1,0:T(8,128)(2,1)S(1)}, bf16[2,256,1024]{2,1,0:T(8,128)(2,1)}, u32[]{:S(2)}, u32[]{:S(2)}) collective-permute-start(bf16[2,256,1024]{2,1,0:T(8,128)(2,1)S(1)} %get-tuple-element.289), channel_id=1, source_target_pairs={{0,2},{1,3},{8,10},{9,11},{16,18},{17,19},{24,26},{25,27}} | collective-permute-start | bytes 3145736 | tf_op jit(solution)/shard_map/ppermute | solution.py:240
  382.8 48.9 %collective-permute-start.26 = (bf16[2,256,1024]{2,1,0:T(8,128)(2,1)}, bf16[2,256,1024]{2,1,0:T(8,128)(2,1)}, u32[]{:S(2)}, u32[]{:S(2)}) collective-permute-start(bf16[2,256,1024]{2,1,0:T(8,128)(2,1)} %get-tuple-element.282), channel_id=1, source_target_pairs={{6,4},{7,5},{14,12},{15,13},{22,20},{23,21},{30,28},{31,29}} | collective-permute-start | bytes 3145736 | tf_op jit(solution)/shard_map/ppermute | solution.py:241
  384.4 47.3 %collective-permute-start.25 = (bf16[2,256,1024]{2,1,0:T(8,128)(2,1)}, bf16[2,256,1024]{2,1,0:T(8,128)(2,1)}, u32[]{:S(2)}, u32[]{:S(2)}) collective-permute-start(bf16[2,256,1024]{2,1,0:T(8,128)(2,1)} %get-tuple-element.283), channel_id=1, source_target_pairs={{0,2},{1,3},{8,10},{9,11},{16,18},{17,19},{24,26},{25,27}} | collective-permute-start | bytes 3145736 | tf_op jit(solution)/shard_map/ppermute | solution.py:240
  395.6 36.1 %collective-permute-start.24 = (bf16[2,256,1024]{2,1,0:T(8,128)(2,1)}, bf16[2,256,1024]{2,1,0:T(8,128)(2,1)S(1)}, u32[]{:S(2)}, u32[]{:S(2)}) collective-permute-start(bf16[2,256,1024]{2,1,0:T(8,128)(2,1)} %get-tuple-element.284), channel_id=1, source_target_pairs={{6,4},{4,2},{2,0},{7,5},{5,3},{3,1},{14,12},{12,10},{10,8},{15,13}... | collective-permute-start | bytes 3145736 | tf_op jit(solution)/shard_map/ppermute | solution.py:241
  396.9 34.9 %collective-permute-start.23 = (bf16[2,256,1024]{2,1,0:T(8,128)(2,1)}, bf16[2,256,1024]{2,1,0:T(8,128)(2,1)}, u32[]{:S(2)}, u32[]{:S(2)}) collective-permute-start(bf16[2,256,1024]{2,1,0:T(8,128)(2,1)} %get-tuple-element.285), channel_id=1, source_target_pairs={{0,2},{2,4},{4,6},{1,3},{3,5},{5,7},{8,10},{10,12},{12,14},{9,11},... | collective-permute-start | bytes 3145736 | tf_op jit(solution)/shard_map/ppermute | solution.py:240
  431.8 33.9 %collective-permute-start.27 = (bf16[4,1024,512]{2,1,0:T(8,128)(2,1)}, bf16[4,1024,512]{2,1,0:T(8,128)(2,1)}, u32[]{:S(2)}, u32[]{:S(2)}) collective-permute-start(bf16[4,1024,512]{2,1,0:T(8,128)(2,1)} %shard_map.262), channel_id=1, source_target_pairs={{0,1},{1,0},{2,3},{3,2},{4,5},{5,4},{6,7},{7,6},{8,9},{9,8},{10,11... | collective-permute-start | bytes 12582920 | tf_op jit(solution)/shard_map/ppermute | solution.py:295
  437.6 26.5 %collective-permute-start.28 = (bf16[2,256,1024]{2,1,0:T(8,128)(2,1)}, bf16[2,256,1024]{2,1,0:T(8,128)(2,1)}, u32[]{:S(2)}, u32[]{:S(2)}) collective-permute-start(bf16[2,256,1024]{2,1,0:T(8,128)(2,1)} %get-tuple-element.281), channel_id=1, source_target_pairs={{0,2},{2,4},{1,3},{3,5},{8,10},{10,12},{9,11},{11,13},{16,18},{18,... | collective-permute-start | bytes 3145736 | tf_op jit(solution)/shard_map/ppermute | solution.py:240
  448.7 34.5 %collective-permute-start.47 = (bf16[128,1024]{0,1:T(8,128)(2,1)}, bf16[128,1024]{0,1:T(8,128)(2,1)S(1)}, u32[]{:S(2)}, u32[]{:S(2)}) collective-permute-start(bf16[128,1024]{0,1:T(8,128)(2,1)} %bitcast.55), channel_id=1, source_target_pairs={{0,16},{16,0},{1,17},{17,1},{2,18},{18,2},{3,19},{19,3},{4,20},{20... | collective-permute-start | bytes 786440 | tf_op jit(solution)/shard_map/ppermute | solution.py:295
  453.1 30.8 %collective-permute-start.48 = (bf16[128,1024]{0,1:T(8,128)(2,1)S(1)}, bf16[128,1024]{0,1:T(8,128)(2,1)S(1)}, u32[]{:S(2)}, u32[]{:S(2)}) collective-permute-start(bf16[128,1024]{0,1:T(8,128)(2,1)S(1)} %bitcast.240), channel_id=1, source_target_pairs={{0,17},{1,16},{16,1},{17,0},{2,19},{3,18},{18,3},{19,2},{4,21},{5,... | collective-permute-start | bytes 786440 | tf_op jit(solution)/shard_map/ppermute | solution.py:295
  453.2 30.6 %collective-permute-start.52 = (bf16[128,1024]{0,1:T(8,128)(2,1)S(1)}, bf16[128,1024]{0,1:T(8,128)(2,1)S(1)}, u32[]{:S(2)}, u32[]{:S(2)}) collective-permute-start(bf16[128,1024]{0,1:T(8,128)(2,1)S(1)} %bitcast.245), channel_id=1, source_target_pairs={{0,1},{1,0},{2,3},{3,2},{4,5},{5,4},{6,7},{7,6},{8,9},{9,8},{10,11... | collective-permute-start | bytes 786440 | tf_op jit(solution)/shard_map/ppermute | solution.py:295
  483.2 47.5 %collective-permute-start.30 = (bf16[4,1024,512]{2,1,0:T(8,128)(2,1)}, bf16[4,1024,512]{2,1,0:T(8,128)(2,1)}, u32[]{:S(2)}, u32[]{:S(2)}) collective-permute-start(bf16[4,1024,512]{2,1,0:T(8,128)(2,1)} %get-tuple-element.209), channel_id=1, source_target_pairs={{0,1},{1,0},{2,3},{3,2},{4,5},{5,4},{6,7},{7,6},{8,9},{9,8},{10,11... | collective-permute-start | bytes 12582920 | tf_op jit(solution)/shard_map/ppermute | solution.py:295
  494.1 32.0 %collective-permute-start.31 = (bf16[2,512,512]{2,1,0:T(8,128)(2,1)S(1)}, bf16[2,512,512]{2,1,0:T(8,128)(2,1)}, u32[]{:S(2)}, u32[]{:S(2)}) collective-permute-start(bf16[2,512,512]{2,1,0:T(8,128)(2,1)S(1)} %dynamic-slice_bitcast_fusion.3), channel_id=1, source_target_pairs={{0,16},{16,0},{1,17},{17,1},{2,18},{18,2},{3,19},{19,3},{4,20},{20... | collective-permute-start | bytes 3145736 | tf_op jit(solution)/shard_map/ppermute | solution.py:295
  496.7 31.0 %collective-permute-start.32 = (bf16[2,512,512]{2,1,0:T(8,128)(2,1)}, bf16[2,512,512]{2,1,0:T(8,128)(2,1)}, u32[]{:S(2)}, u32[]{:S(2)}) collective-permute-start(bf16[2,512,512]{2,1,0:T(8,128)(2,1)} %dynamic-slice_bitcast_fusion.2), channel_id=1, source_target_pairs={{0,8},{8,0},{1,9},{9,1},{2,10},{10,2},{3,11},{11,3},{4,12},{12,4},... | collective-permute-start | bytes 3145736 | tf_op jit(solution)/shard_map/ppermute | solution.py:295
  502.1 28.2 %collective-permute-start.34 = (bf16[2,256,1024]{2,1,0:T(8,128)(2,1)}, bf16[2,256,1024]{2,1,0:T(8,128)(2,1)S(1)}, u32[]{:S(2)}, u32[]{:S(2)}) collective-permute-start(bf16[2,256,1024]{2,1,0:T(8,128)(2,1)} %get-tuple-element.276), channel_id=1, source_target_pairs={{6,4},{4,2},{2,0},{7,5},{5,3},{3,1},{14,12},{12,10},{10,8},{15,13}... | collective-permute-start | bytes 3145736 | tf_op jit(solution)/shard_map/ppermute | solution.py:241
  503.3 27.4 %collective-permute-start.33 = (bf16[2,256,1024]{2,1,0:T(8,128)(2,1)}, bf16[2,256,1024]{2,1,0:T(8,128)(2,1)S(1)}, u32[]{:S(2)}, u32[]{:S(2)}) collective-permute-start(bf16[2,256,1024]{2,1,0:T(8,128)(2,1)} %get-tuple-element.277), channel_id=1, source_target_pairs={{0,2},{2,4},{4,6},{1,3},{3,5},{5,7},{8,10},{10,12},{12,14},{9,11},... | collective-permute-start | bytes 3145736 | tf_op jit(solution)/shard_map/ppermute | solution.py:240
  543.5 26.2 %collective-permute-start.37 = (bf16[2,512,512]{2,1,0:T(8,128)(2,1)S(1)}, bf16[2,512,512]{2,1,0:T(8,128)(2,1)S(1)}, u32[]{:S(2)}, u32[]{:S(2)}) collective-permute-start(bf16[2,512,512]{2,1,0:T(8,128)(2,1)S(1)} %dynamic-slice_bitcast_fusion.1), channel_id=1, source_target_pairs={{0,16},{16,0},{1,17},{17,1},{2,18},{18,2},{3,19},{19,3},{4,20},{20... | collective-permute-start | bytes 3145736 | tf_op jit(solution)/shard_map/ppermute | solution.py:295
  583.9 26.9 %collective-permute-start.36 = (bf16[512,512]{1,0:T(8,128)(2,1)}, bf16[512,512]{1,0:T(8,128)(2,1)}, u32[]{:S(2)}, u32[]{:S(2)}) collective-permute-start(bf16[512,512]{1,0:T(8,128)(2,1)} %dynamic-slice_bitcast_fusion.12), channel_id=1, source_target_pairs={{0,16},{16,0},{1,17},{17,1},{2,18},{18,2},{3,19},{19,3},{4,20},{20... | collective-permute-start | bytes 1572872 | tf_op jit(solution)/shard_map/ppermute | solution.py:295
  585.7 31.4 %collective-permute-start.35 = (bf16[512,512]{1,0:T(8,128)(2,1)}, bf16[512,512]{1,0:T(8,128)(2,1)}, u32[]{:S(2)}, u32[]{:S(2)}) collective-permute-start(bf16[512,512]{1,0:T(8,128)(2,1)} %dynamic-slice_bitcast_fusion.13), channel_id=1, source_target_pairs={{0,8},{8,0},{1,9},{9,1},{2,10},{10,2},{3,11},{11,3},{4,12},{12,4},... | collective-permute-start | bytes 1572872 | tf_op jit(solution)/shard_map/ppermute | solution.py:295
  (69 other events, 593.5 us)
Sparse Core Ops, SparseCore 0:
  13.9 70.5 all-gather.4
  86.1 31.8 all-gather.6
  119.6 98.9 all-gather.8
  219.9 112.2 all-gather.10

commit v3 on v2

--- a/solution.py
+++ b/solution.py
@@ -61,6 +61,9 @@
 
 
 def run(body, steps, ins, outs, args, flops, transcendentals=0):
+    scratch = []
+    if any(isinstance(arg, Line) for arg in args):
+        body, ins, args, scratch = put_together(body, ins, args)
     shapes = [jax.ShapeDtypeStruct(shape, dtype) for _, shape, dtype in outs]
     moved = sum(a.size * a.dtype.itemsize for a in list(args) + shapes)
     return pl.pallas_call(
@@ -69,11 +72,78 @@
         in_specs=ins,
         out_specs=[spec for spec, _, _ in outs],
         out_shape=shapes,
+        scratch_shapes=scratch,
         cost_estimate=pl.CostEstimate(
-            flops=flops, bytes_accessed=moved, transcendentals=transcendentals
+            flops=flops // 64, bytes_accessed=moved // 64, transcendentals=transcendentals // 64
         ),
         compiler_params=pltpu.CompilerParams(vmem_limit_bytes=VMEM_BYTES),
     )(*args)
+
+
+def put_together(body, ins, args):
+    new_ins, new_args, places, scratch = [], [], [], []
+    for spec, arg in zip(ins, args):
+        if not isinstance(arg, Line):
+            new_ins.append(spec)
+            new_args.append(arg)
+            places.append(None)
+        elif arg.full is not None:
+            new_ins.append(spec)
+            new_args.append(arg.full)
+            places.append(None)
+        else:
+            slots = arg.slots()
+            rows, columns = slots[0].shape
+            new_ins += [pl.BlockSpec(memory_space=pl.ANY)] * len(slots)
+            new_args += slots
+            places.append((len(slots), rows, arg.count))
+            scratch += [
+                pltpu.VMEM((arg.count * rows, columns), slots[0].dtype),
+                pltpu.SemaphoreType.DMA((arg.count,)),
+            ]
+            index = arg.index
+    if not scratch:
+        return body, new_ins, new_args, []
+
+    def whole_body(index_ref, *refs):
+        kept, held = refs[: len(refs) - len(scratch)], refs[len(refs) - len(scratch) :]
+        inner, lines, at = [], [], 0
+        for place in places:
+            if place is None:
+                inner.append(kept[at])
+                at += 1
+            else:
+                full_ref, sems = held[2 * len(lines) : 2 * len(lines) + 2]
+                lines.append((kept[at : at + place[0]], full_ref, sems, place))
+                inner.append(full_ref)
+                at += place[0]
+
+        @pl.when(pl.program_id(0) == 0)
+        def _():
+            for blocks, full_ref, sems, (_, rows, count) in lines:
+                for j in range(count):
+                    for k, block in enumerate(blocks):
+
+                        @pl.when(count - 1 - index_ref[0] + j == k)
+                        def _():
+                            pltpu.make_async_copy(
+                                block, full_ref.at[pl.ds(j * rows, rows)], sems.at[j]
+                            ).start()
+
+            for blocks, full_ref, sems, (_, rows, count) in lines:
+                for j in range(count):
+                    pltpu.make_async_copy(
+                        blocks[0], full_ref.at[pl.ds(j * rows, rows)], sems.at[j]
+                    ).wait()
+
+        body(*inner, *kept[at:])
+
+    return (
+        whole_body,
+        [pl.BlockSpec(memory_space=pltpu.SMEM)] + new_ins,
+        [index.reshape(1)] + new_args,
+        scratch,
+    )
 
 
 def statistics(x):
@@ -179,28 +249,32 @@
     accumulate(bias_grad_ref, jnp.sum(grad.astype(F32), axis=0, keepdims=True))
 
 
-def store_blocks(ref, values):
-    blocks, span = ref.shape[0], ref.shape[2]
+def store_blocks(out_ref, values, got_refs):
+    blocks, span = out_ref.shape[1], out_ref.shape[3]
     for k in range(blocks):
-        ref[k] = values[:, k * span : (k + 1) * span].astype(BF16)
-
-
-def forward_body(mixed_ref, dense_ref, active_ref, down_ref, out_ref):
+        block = values[:, k * span : (k + 1) * span]
+        for got_ref in got_refs:
+            block = block + got_ref[0, k].astype(F32)
+        out_ref[0, k] = block.astype(BF16)
+
+
+def forward_body(mixed_ref, dense_ref, active_ref, down_ref, *refs):
     total = dot(mixed_ref[...], dense_ref[...], 1, 0)
     total += dot(active_ref[...], down_ref[...], 1, 0)
-    store_blocks(out_ref, total)
+    store_blocks(refs[-1], total, refs[:-1])
 
 
 def input_body(
-    x_ref, joined_grad_ref, joined_ref, hidden_grad_ref, up_ref, gain_a, gain_e, out_ref, sums_ref
+    x_ref, joined_grad_ref, joined_ref, hidden_grad_ref, up_ref, gain_a, gain_e, *refs
 ):
+    got_refs, (out_ref, sums_ref) = refs[:-2], refs[-2:]
     normed_grad = dot(joined_grad_ref[...], joined_ref[...], 1, 1)
     expanded_grad = dot(hidden_grad_ref[...], up_ref[...], 1, 1)
     hat, inverse = statistics(x_ref[...].astype(F32))
     weighted = normed_grad * gain_a[...] + expanded_grad * gain_e[...]
     weighted_mean = jnp.mean(weighted, axis=-1, keepdims=True)
     along = jnp.mean(weighted * hat, axis=-1, keepdims=True)
-    store_blocks(out_ref, inverse * (weighted - weighted_mean - hat * along))
+    store_blocks(out_ref, inverse * (weighted - weighted_mean - hat * along), got_refs)
 
     def down(values):
         return jnp.sum(values, axis=0, keepdims=True)
@@ -211,6 +285,17 @@
     accumulate(sums_ref, sums)
 
 
+def place_body(layouts, pieces_ref, *outs):
+    for device in range(pieces_ref.shape[0]):
+        for start, size, target, where, turned in layouts:
+            offset = where(device) * size
+            values = pieces_ref[device, :, start : start + size].astype(F32)
+            if turned:
+                outs[target][offset : offset + size, :] = values.T
+            else:
+                outs[target][:, offset : offset + size] = values
+
+
 def pick(array, index, axis):
     return lax.dynamic_index_in_dim(array, index, axis, keepdims=False)
 
@@ -226,24 +311,67 @@
     def __init__(self, view, index, count):
         self.view, self.index, self.count, self.step = view, index, count, 0
         self.held = self.flight = ()
+        self.out = []
 
     def term(self, share):
         return pick(self.view, jnp.clip(share, 0, self.count - 1), 0)
 
-    def send(self):
+    def prepare(self):
+        if self.step == self.count - 1:
+            return
         self.step += 1
         step, count = self.step, self.count
-        out = [self.term(self.index + count - step), self.term(self.index - count + step)]
+        self.out = [self.term(self.index + count - step), self.term(self.index - count + step)]
         if self.held:
-            out = [add_low(one, two) for one, two in zip(out, self.held)]
+            self.out = [add_low(one, two) for one, two in zip(self.out, self.held)]
+
+    def send(self):
+        if not self.out:
+            self.prepare()
+        if not self.out:
+            return
+        step, count = self.step, self.count
         self.flight = (
-            lax.ppermute(out[0], "z", [(i, i + 1) for i in range(step)]),
-            lax.ppermute(out[1], "z", [(count - 1 - i, count - 2 - i) for i in range(step)]),
-        )
+            lax.ppermute(self.out[0], "z", [(i, i + 1) for i in range(step)]),
+            lax.ppermute(self.out[1], "z", [(count - 1 - i, count - 2 - i) for i in range(step)]),
+        )
+        self.out = []
+
+    def land(self, values):
+        if values:
+            self.held, self.flight = values, ()
 
     def total(self):
         own = self.term(self.index).astype(F32)
         return (own + self.held[0].astype(F32) + self.held[1].astype(F32)).astype(BF16)
+
+
+class Line:
+    def __init__(self, piece, index, count):
+        self.index, self.count, self.step, self.flight = index, count, 0, ()
+        self.from_left, self.from_right, self.own, self.full = [], [], piece, None
+        if count > 4:
+            self.full = lax.all_gather(piece, "z", axis=0, tiled=True)
+
+    def send(self):
+        if self.full is not None or self.step == self.count - 1:
+            return
+        step, count = self.step, self.count
+        right, left = (self.from_left[-1], self.from_right[-1]) if step else (self.own, self.own)
+        self.flight = (
+            lax.ppermute(right, "z", [(i, i + 1) for i in range(step, count - 1)]),
+            lax.ppermute(left, "z", [(i + 1, i) for i in range(count - 1 - step)]),
+        )
+        self.step += 1
+
+    def land(self, values):
+        if values:
+            self.from_left.append(values[0])
+            self.from_right.append(values[1])
+            self.flight = ()
+
+    def slots(self):
+        return [*self.from_left[::-1], self.own, *self.from_right]
 
 
 fence = lax.optimization_barrier
@@ -391,10 +519,11 @@
             (starts, *[piece for pair in zip(g_mine, g_other) for piece in pair]),
             all_tokens * width,
         )
-        normed, expanded, rotary, g, up_piece, down_piece = fence(
-            (normed, expanded, rotary, g, up_piece, down_piece)
-        )
-        up_full = gather(up_piece)
+        normed, expanded, rotary, g, up_piece, down_piece, joined_full, dense_full = fence(
+            (normed, expanded, rotary, g, up_piece, down_piece, joined_full, dense_full)
+        )
+        up_line = Line(up_piece, z, chips)
+        up_line.send()
 
         all_rows = 2 * rows
         mixed, joined_grad, joined_bias_grad = run(
@@ -436,17 +565,24 @@
         )
 
         def step(*landing):
-            fresh, held, views = fence(
-                (dict(live), [chain.flight for chain in landing], [chain.view for chain in waiting])
-            )
+            fresh, held, views, outs = fence(
+                (
+                    dict(live),
+                    [chain.flight for chain in landing],
+                    [chain.view for chain in waiting],
+                    [chain.out for chain in chains],
+                )
+            )
+            for chain, out in zip(chains, outs):
+                chain.out = out
             live.update(fresh)
             for chain, one in zip(landing, held):
-                chain.held, chain.flight = one, ()
+                chain.land(one)
             for chain, view in zip(waiting, views):
                 chain.view = view
             waiting.clear()
 
-        waiting = []
+        waiting, chains = [], []
         share_rows = cores * row_share
 
         def terms(*pairs):
@@ -476,24 +612,13 @@
             )
             chain = Chain(view, z, chips)
             waiting.append(chain)
+            chains.append(chain)
             return chain
 
         def spread(chain):
-            share = chain.total().reshape(branches, cores, row_share, -1)
-            pieces = {}
-            for db in range(2):
-                for dc in range(2):
-                    piece = pick(pick(share, b ^ db, 0), c ^ dc, 0)
-                    pieces[db, dc] = partner(piece, branch=db, core=dc)
-            return pieces
-
-        def from_device(pieces, branch, core):
-            same_core = c == core
-            return jnp.where(
-                b == branch,
-                jnp.where(same_core, pieces[0, 0], pieces[0, 1]),
-                jnp.where(same_core, pieces[1, 0], pieces[1, 1]),
-            ).astype(F32)
+            share = chain.total().reshape(branches * cores * row_share, -1)
+            pieces = lax.all_to_all(share, ("branch", "core"), 0, 0, tiled=True)
+            return pieces.reshape(branches * cores, row_share, -1)
 
         unit_flops = 2 * all_tokens * width * units
         big_tile = min(512, length)
@@ -504,7 +629,7 @@
                 all_tokens // big_tile,
                 [tile(big_tile, width), whole((width, units)), whole((1, units))],
                 [(tile(big_tile, units), (all_tokens, units), BF16)] * 2,
-                (live["expanded"], up_full, flat(up_bias_here)),
+                (live["expanded"], up_line, flat(up_bias_here)),
                 unit_flops,
                 2 * all_tokens * units,
             )
@@ -518,7 +643,7 @@
                     (tile(big_tile, units), (all_tokens, units), BF16),
                     (whole((1, units)), (1, units), F32),
                 ],
-                (live["g"], down_full, live.pop("slope")),
+                (live["g"], down_line, live.pop("slope")),
                 unit_flops,
             )
 
@@ -527,13 +652,15 @@
         def of_core(core, columns):
             return pl.BlockSpec((small_tile, columns), lambda i: (core * half_steps + i, 0))
 
-        out_blocks = (
-            pl.BlockSpec((blocks, small_tile, span), lambda i: (0, i, 0)),
-            (blocks, tokens, span),
-            BF16,
-        )
-
-        def input_terms(core):
+        def out_blocks(pieces):
+            steps = half_steps // pieces
+            return (
+                pl.BlockSpec((1, blocks, small_tile, span), lambda i: (i // steps, 0, i % steps, 0)),
+                (pieces, blocks, tokens // pieces, span),
+                BF16,
+            )
+
+        def input_terms(core, *got):
             return run(
                 input_body,
                 half_steps,
@@ -545,20 +672,22 @@
                     whole((width, units)),
                     whole((1, width)),
                     whole((1, width)),
+                    *[out_blocks(2)[0]] * len(got),
                 ],
-                [out_blocks, (whole((4, width)), (4, width), F32)],
+                [out_blocks(2), (whole((4, width)), (4, width), F32)],
                 (
                     (x_own, x_other)[core],
                     live["joined_grad"],
                     joined_full,
                     live["grad"],
-                    up_full,
+                    up_line,
                     *gains,
+                    *got,
                 ),
                 unit_flops // 2 + all_tokens * width * head_columns,
             )
 
-        def forward_terms(core):
+        def forward_terms(core, *got):
             return run(
                 forward_body,
                 half_steps,
@@ -567,133 +696,192 @@
                     whole((HEAD, width)),
                     of_core(core, units),
                     whole((units, width)),
+                    *[out_blocks(1)[0]] * len(got),
                 ],
-                [out_blocks],
-                (live["mixed"], dense_full, live["active"], down_full),
+                [out_blocks(1)],
+                (live["mixed"], dense_full, live["active"], down_line, *got),
                 unit_flops // 2 + all_tokens * width * HEAD,
             )[0]
 
-        def core_sum(mine, theirs):
-            total = add_low(mine, theirs).reshape(branches, models, 2, tokens // 2, span)
-            return total[:, :, 0], total[:, :, 1]
-
-        def first_sum(pair):
+        def block_sum(blocks):
+            return lax.psum_scatter(blocks[0], ("branch", "mp"), scatter_dimension=0, tiled=True)[0]
+
+        def first_sends(term):
+            one, two = (term[h].reshape(branches, models, tokens // 2, span) for h in range(2))
+            return partner(pick(one, 1 - b, 0), branch=1), partner(pick(two, 1 - m, 1), mp=1)
+
+        def first_sum(term, got):
+            one, two = (term[h].reshape(branches, models, tokens // 2, span) for h in range(2))
+            return add_low(pick(one, b, 0), got[0]), add_low(pick(two, m, 1), got[1])
+
+        def second_sends(pair):
             one, two = pair
-            return (
-                add_low(pick(one, b, 0), partner(pick(one, 1 - b, 0), branch=1)),
-                add_low(pick(two, m, 1), partner(pick(two, 1 - m, 1), mp=1)),
-            )
-
-        def second_sum(pair):
+            return partner(pick(one, 1 - m, 0), mp=1), partner(pick(two, 1 - b, 0), branch=1)
+
+        def second_sum(pair, got):
             one, two = pair
             return jnp.concatenate(
                 [
-                    pick(one, m, 0).astype(F32) + partner(pick(one, 1 - m, 0), mp=1).astype(F32),
-                    pick(two, b, 0).astype(F32) + partner(pick(two, 1 - b, 0), branch=1).astype(F32),
+                    pick(one, m, 0).astype(F32) + got[0].astype(F32),
+                    pick(two, b, 0).astype(F32) + got[1].astype(F32),
                 ]
             )
 
-        joined_chain = terms((normed, joined_grad), (g, mixed))
-        step()
-        down_full = gather(live.pop("down"))
-        live.pop("normed")
-        for _ in range(chips - 3):
-            joined_chain.send()
-            step(joined_chain)
+        def finish(chain):
+            while chain.step < chips - 1:
+                chain.send()
+                step(chain)
+            return spread(chain)
+
+        step(up_line)
+        up_line.send()
+        joined_chain = terms((live.pop("normed"), live["joined_grad"]), (live["g"], live["mixed"]))
+        step(up_line)
+        up_line.send()
         joined_chain.send()
+        step(up_line, joined_chain)
+        down_line = Line(live.pop("down"), z, chips)
+        down_line.send()
         live["active"], live["slope"] = hidden_values()
-        step(joined_chain)
-        joined_chain.send()
         down_chain = terms((live["g"], live["active"]))
-        step(joined_chain)
-        joined_pieces = spread(joined_chain)
-        for _ in range(chips - 4):
-            down_chain.send()
-            step(down_chain)
+        down_chain.prepare()
+        step(down_line)
+        down_line.send()
         down_chain.send()
-        live["grad"], live["bias"] = hidden_gradient()
-        step(down_chain)
-        down_chain.send()
-        up_chain = terms((live.pop("expanded"), live["grad"]))
-        live.pop("g")
-        step(down_chain)
-        down_chain.send()
-        for _ in range(chips - 3):
-            up_chain.send()
-            live["out_other"] = forward_terms(1)
-            live["out_own"] = forward_terms(0)
-            step(*([down_chain] if down_chain.flight else []), up_chain)
-        up_chain.send()
-        down_pieces = spread(down_chain)
-        live["out_other"] = swap_core(live["out_other"])
-        live["in_other"], live["sums_other"] = input_terms(1)
-        step(up_chain)
-        live["out"] = core_sum(live.pop("out_own"), live.pop("out_other"))
-        up_chain.send()
-        live["out"] = first_sum(live["out"])
-        live["in_other"] = swap_core(live["in_other"])
-        live["in_own"], live["sums_own"] = input_terms(0)
-        step(up_chain)
-        live["in"] = core_sum(live.pop("in_own"), live.pop("in_other"))
-        live["in"] = first_sum(live["in"])
-        up_pieces = spread(up_chain)
-        forward_sum = second_sum(live.pop("out"))
-
+        joined_chain.prepare()
         g_float = g_piece.astype(F32)
+        out_slot = lax.dynamic_update_slice(
+            jnp.zeros((width,), F32), jnp.sum(g_float, axis=0), (column_start,)
+        )
         joined_slot = lax.dynamic_update_slice(
             jnp.zeros_like(joined_bias),
             joined_bias_grad.reshape(-1),
             ((m * heads + head_slot) * head_columns,),
         )
+        live["slots"] = jnp.concatenate([out_slot, joined_slot])
+        step(down_line, down_chain)
+        down_line.send()
+        joined_chain.send()
+        down_chain.prepare()
+        step(down_line, joined_chain)
+        joined_chain.send()
+        live["grad"], live["bias"] = hidden_gradient()
+        live["out_other"] = forward_terms(1)
+        step(joined_chain)
+        down_chain.send()
+        live["out_got"] = swap_core(live.pop("out_other"))
+        live["joined_pieces"] = finish(joined_chain)
+        up_chain = terms((live.pop("expanded"), live["grad"]))
+        live.pop("g")
+        up_chain.prepare()
+        step(down_chain)
+        up_chain.send()
+        down_chain.prepare()
+        live["out"] = forward_terms(0, live.pop("out_got"))
+        live["in_other"], live["sums_other"] = input_terms(1)
+        step(up_chain)
+        forward_sum = block_sum(live.pop("out"))
+        down_chain.send()
+        live["in_got"] = swap_core(live.pop("in_other"))
+        up_chain.prepare()
+        live["in"], live["sums_own"] = input_terms(0, live.pop("in_got"))
+        step(down_chain)
+        up_chain.send()
         up_slot = lax.dynamic_update_slice(
             jnp.zeros((models, chips, cores, branches, part), F32),
             live.pop("bias").reshape(1, chips, 1, 1, part),
             (m, 0, c, b, 0),
         ).reshape(-1)
-        out_slot = lax.dynamic_update_slice(
-            jnp.zeros((width,), F32), jnp.sum(g_float, axis=0), (column_start,)
-        )
-        small = jnp.concatenate(
-            [
-                (live.pop("sums_own") + live.pop("sums_other")).reshape(-1),
-                out_slot,
-                joined_slot,
-                up_slot,
-            ]
-        )
-        small = small + partner(small, core=1)
-        small = small + partner(small, branch=1)
-        small = small + partner(small, mp=1)
-        flip = 1
+        sums = live.pop("sums_own") + live.pop("sums_other")
+        small = jnp.concatenate([sums.reshape(-1), live.pop("slots"), up_slot])
+        live["in_got"] = first_sends(live["in"])
+        live["small"] = (
+            small
+            + partner(small, core=1)
+            + partner(small, branch=1)
+            + partner(small, branch=1, core=1)
+        )
+        step(up_chain)
+        up_chain.send()
+        live["in"] = first_sum(live["in"], live.pop("in_got"))
+        live["in_got"] = second_sends(live["in"])
+        small = live["small"]
+        near = lax.ppermute(small, "z", [(i, i ^ 1) for i in range(chips)])
+        far = [
+            lax.ppermute(
+                small,
+                ("mp", "z"),
+                [
+                    (one * chips + i, (1 - one) * chips + (i ^ flip))
+                    for one in range(models)
+                    for i in range(chips)
+                ],
+            )
+            for flip in range(2)
+        ]
+        live["small"] = small + near + far[0] + far[1]
+        live["down_pieces"] = finish(down_chain)
+        step(up_chain)
+        live["up_pieces"] = finish(up_chain)
+        small = live["small"]
+        flip = 2
         while flip < chips:
             small = small + lax.ppermute(small, "z", [(i, i ^ flip) for i in range(chips)])
             flip *= 2
-        input_sum = second_sum(live.pop("in"))
+        input_sum = second_sum(live.pop("in"), live.pop("in_got"))
+        joined_pieces, down_pieces, up_pieces = (
+            live[name] for name in ("joined_pieces", "down_pieces", "up_pieces")
+        )
 
         residual = columns_of(x_own, column_start, span).astype(F32)
         column_bias = columns_of(dense_bias + down_bias, column_start, span)
         block_output = (residual + forward_sum + column_bias).astype(BF16)
         input_gradient = (g_float + input_sum).astype(BF16)
 
-        def by_device(pieces):
-            return jnp.stack(
-                [
-                    jnp.stack([from_device(pieces, one, core) for one in range(branches)])
-                    for core in range(cores)
+        if part % LANES == 0 and row_share % 8 == 0:
+
+            def put(pieces, shapes, layouts):
+                return run(
+                    functools.partial(place_body, layouts),
+                    1,
+                    [whole(pieces.shape)],
+                    [(whole(shape), shape, F32) for shape in shapes],
+                    [pieces],
+                    0,
+                )
+
+            def unit_layouts(turned):
+                return [
+                    (
+                        k * part,
+                        part,
+                        0,
+                        lambda device, k=k: (k * cores + device % cores) * branches + device // cores,
+                        turned,
+                    )
+                    for k in range(chips)
                 ]
-            )
-
-        joined_out = jnp.concatenate(
-            [from_device(joined_pieces, *divmod(k, cores))[:, :head_columns] for k in range(heads)],
-            axis=1,
-        )
-        dense_out = jnp.concatenate(
-            [from_device(joined_pieces, *divmod(k, cores))[:, head_columns:].T for k in range(heads)]
-        )
-        up_out = by_device(up_pieces).reshape(cores, branches, row_share, chips, part)
-        up_out = up_out.transpose(2, 3, 0, 1, 4).reshape(row_share, hidden_columns)
-        down_out = by_device(down_pieces).reshape(cores, branches, row_share, chips, part)
-        down_out = down_out.transpose(3, 0, 1, 4, 2).reshape(hidden_columns, row_share)
+
+            def same(device):
+                return device
+
+            joined_out, dense_out = put(
+                joined_pieces,
+                [(row_share, heads * head_columns), (heads * HEAD, row_share)],
+                [(0, head_columns, 0, same, False), (head_columns, HEAD, 1, same, True)],
+            )
+            (down_out,) = put(down_pieces, [(hidden_columns, row_share)], unit_layouts(True))
+            (up_out,) = put(up_pieces, [(row_share, hidden_columns)], unit_layouts(False))
+        else:
+            joined_pieces, down_pieces, up_pieces = (
+                pieces.astype(F32) for pieces in (joined_pieces, down_pieces, up_pieces)
+            )
+            joined_out = joined_pieces[:, :, :head_columns].transpose(1, 0, 2).reshape(row_share, -1)
+            dense_out = joined_pieces[:, :, head_columns:].transpose(0, 2, 1).reshape(-1, row_share)
+            up_out = up_pieces.reshape(branches, cores, row_share, chips, part)
+            up_out = up_out.transpose(2, 3, 1, 0, 4).reshape(row_share, hidden_columns)
+            down_out = down_pieces.reshape(branches, cores, row_share, chips, part)
+            down_out = down_out.transpose(3, 1, 0, 4, 2).reshape(hidden_columns, row_share)
         w = width
         joined_end = 5 * w + joined_bias.shape[0]
         return (

time: 646 us -> 570 us (0.88)
  waiting for transfers between devices: 177 us -> 138 us
  local copies, waits for them, and re-layouts: 56.7 us -> 26.6 us
  other arithmetic: 81.5 us -> 62.2 us
  Pallas kernels: 178 us -> 194 us
    ppermute x18 -> x33, waiting for transfers between devices: 113 us -> 73.7 us  [the longest x6 41.6 us: send(): lax.ppermute(left, 'z', [(i + 1, i) for i in range(count - 1 - step)])]
    pallas_call x12 -> x15, Pallas kernels: 178 us -> 194 us  [run(): pl.pallas_call(body, grid=(steps,), in_specs=ins, out_specs=[spec for spe...]
    all_to_all x0 -> x3, starting transfers between devices: none -> 10.7 us  [spread(): pieces = lax.all_to_all(share, ('branch', 'core'), 0, 0, tiled=True)]
    dynamic_slice x15 -> x0, local copies, waits for them, and re-layouts: 10.5 us -> none  [pick(): return lax.dynamic_index_in_dim(array, index, axis, keepdims=False)]
    ppermute x33 -> x20, starting transfers between devices: 34.5 us -> 24.9 us  [partner(): lax.ppermute(array, names, [(i, count - 1 - i) for i in range(count)])]
    convert_element_type x12 -> x8, other arithmetic: 34.6 us -> 27.2 us  [add_low(): return (left.astype(F32) + right.astype(F32)).astype(BF16)]
    reshape x2 -> x0, other arithmetic: 6.47 us -> none  [the longest x1 5.01 us: on_device(): up_out = up_out.transpose(2, 3, 0, 1, 4).reshape(row_share, hidden_columns)]
    ppermute x18 -> x33, starting transfers between devices: 81.9 us -> 77 us  [the longest x9 39.1 us: send(): lax.ppermute(self.out[0], 'z', [(i, i + 1) for i in range(step)])]
  transfers between devices with their start and end apart: 59 -> 62, of which waited for: 19 -> 22; matrix products, arithmetic and copies ran while one was open for 19% -> 14% of each run, Pallas kernels for 28% -> 35%
where the time goes in v3:
time: 570 us; the launch traced here: 559 us
  Pallas kernels  194 us (34%)
  waiting for transfers between devices  138 us (24%)
  starting transfers between devices  122 us (21%)
  other arithmetic  62.2 us (11%)
  local copies, waits for them, and re-layouts  26.6 us (5%)
  between operations  15.3 us (3%)
    pallas_call x15, Pallas kernels, run(): pl.pallas_call(body, grid=(steps,), in_specs=ins, out_specs=[spec for spe...  194 us
    ppermute x6, waiting for transfers between devices, send(): lax.ppermute(left, 'z', [(i + 1, i) for i in range(count - 1 - step)])  41.6 us
    ppermute x9, starting transfers between devices, send(): lax.ppermute(self.out[0], 'z', [(i, i + 1) for i in range(step)])  39.1 us
    ppermute x20, waiting for transfers between devices, partner(): lax.ppermute(array, names, [(i, count - 1 - i) for i in range(count)])  33.3 us
    ppermute x9, waiting for transfers between devices, send(): lax.ppermute(self.out[0], 'z', [(i, i + 1) for i in range(step)])  28 us
    convert_element_type x8, other arithmetic, add_low(): return (left.astype(F32) + right.astype(F32)).astype(BF16)  27.2 us
    all_gather x2, waiting for transfers between devices, gather(): return lax.all_gather(piece, 'z', axis=0, tiled=True)  25.4 us
    ppermute x20, starting transfers between devices, partner(): lax.ppermute(array, names, [(i, count - 1 - i) for i in range(count)])  24.9 us
  transfers between devices with their start and end apart: 62, of which 22 were waited for; matrix products, arithmetic and copies ran while one was open for 14% of the time, Pallas kernels for 35%

profile of v3, /device:TPU:0, one launch (start us, length us, event | category | flops | bytes accessed | tf_op | source)
XLA Modules:
  0.0 558.5 jit_solution(18315853984235584789)
XLA Ops:
  20.9 4.9 collective-permute-start.3
  26.4 5.4 multiply_sine_fusion
  31.8 5.7 %collective-permute-done.3 = bf16[64,2048]{1,0:T(8,128)(2,1)S(1)} collective-permute-done((bf16[64,2048]{1,0:T(8,128)(2,1)S(1)}, bf16[64,2048]{1,0:T(8,128)(2,1)S(1)}, u32[]{:S(2)}, u32[]{:S(2)}) %collective-permute-start.3) | collective-permute-done | bytes 262176 | tf_op jit(solution)/shard_map/ppermute | solution.py:472
  42.7 11.0 %collective-permute-start.8 = (bf16[256,1024]{1,0:T(8,128)(2,1)}, bf16[256,1024]{1,0:T(8,128)(2,1)}, u32[]{:S(2)}, u32[]{:S(2)}) collective-permute-start(bf16[256,1024]{1,0:T(8,128)(2,1)} %pad_maximum_fusion.1), channel_id=1, source_target_pairs={{0,1},{1,0},{2,3},{3,2},{4,5},{5,4},{6,7},{7,6},{8,9},{9,8},{10,11... | collective-permute-start | bytes 1572872 | tf_op jit(solution)/shard_map/ppermute | solution.py:423
  57.8 14.3 %shard_map.254 = (bf16[2048,2048]{1,0:T(8,128)(2,1)}, bf16[2048,2048]{1,0:T(8,128)(2,1)}) custom-call(bf16[1024,2048]{1,0:T(8,128)(2,1)} %bitcast.115, bf16[1024,2048]{1,0:T(8,128)(2,1)} %collective-permute-done.other_ref.refs_0_, f32[1,2048]{1,0:T(1,128)} %bitcast.128, f32[1,2048]{1,0:T(1,128)} %bitcast.136, f32[1,2048]{1,0:T(1,128)} %bitcast.131, ...), custom_call_target="tpu_custom_call" | custom-call | flops 1310720 | bytes 393728 | tf_op jit(solution)/shard_map/pallas_call | solution.py:69
  81.3 9.6 %shard_map.255.g_ref.refs_2_.refs_0_ = bf16[2048,2048]{1,0:T(8,128)(2,1)} custom-call(s32[4]{0:T(128)} %pad_add_fusion.1.starts_ref, bf16[1024,512]{1,0:T(8,128)(2,1)} %bitcast.6.refs_0_, bf16[1024,512]{1,0:T(8,128)(2,1)} %copy-done.25, bf16[1024,512]{1,0:T(8,128)(2,1)} %collective-permute-done.5.refs_2_, bf16[1024,512]{1,0:T(8,128)(2,1)} %collective-permute-done.10.refs_3_, ...), custom_call_target="tpu_custom_call" | custom-call | flops 65536 | bytes 262144 | tf_op jit(solution)/shard_map/pallas_call | solution.py:69
  91.0 25.4 %all-gather.5.cloned.1.call-done.dense_ref.refs_1_ = bf16[256,2048]{1,0:T(8,128)(2,1)} async-done(((bf16[64,2048]{1,0:T(8,128)(2,1)}), bf16[256,2048]{1,0:T(8,128)(2,1)}) %all-gather.5.cloned.1.call-update) | async-done | bytes 1048592 | tf_op jit(solution)/shard_map/all_gather | solution.py:444
  117.6 5.5 collective-permute-start.13
  126.5 24.1 %shard_map.256 = (bf16[2048,256]{1,0:T(8,128)(2,1)}, bf16[2048,768]{1,0:T(8,128)(2,1)}, f32[1,768]{1,0:T(1,128)}) custom-call(bf16[2048,2048]{1,0:T(8,128)(2,1)} %get-tuple-element.217.normed_ref.refs_0_, bf16[2048,768]{1,0:T(8,128)(2,1)} %all-gather.3.cloned.1.call-done.joined_ref.refs_2_, f32[1,768]{1,0:T(1,128)} %reshape.168.bias_ref, ...), custom_call_target="tpu_custom_call" | custom-call | flops 192937984 | bytes 442720 | tf_op jit(solution)/shard_map/pallas_call | solution.py:69
  152.7 15.7 %shard_map.257 = bf16[4,2,256,1024]{3,2,1,0:T(8,128)(2,1)} custom-call(bf16[2048,2048]{1,0:T(8,128)(2,1)} %get-tuple-element.217.normed_ref.refs_0_, bf16[2048,768]{1,0:T(8,128)(2,1)} %get-tuple-element.306.refs_1_, bf16[2048,2048]{1,0:T(8,128)(2,1)} %shard_map.255.g_ref.refs_2_.refs_0_, bf16[2048,256]{1,0:T(8,128)(2,1)} %get-tuple-element.295.refs_3_.refs_0_), custom_call_target="tpu_custom_call" | custom-call | flops 134217728 | bytes 393216 | tf_op jit(solution)/shard_map/pallas_call | solution.py:69
  168.3 10.2 %collective-permute-done.16.refs_6_.refs_9_ = bf16[512,1024]{1,0:T(8,128)(2,1)} collective-permute-done((bf16[512,1024]{1,0:T(8,128)(2,1)S(1)}, bf16[512,1024]{1,0:T(8,128)(2,1)}, u32[]{:S(2)}, u32[]{:S(2)}) %collective-permute-start.16) | collective-permute-done | bytes 1048608 | tf_op jit(solution)/shard_map/ppermute | solution.py:363
  187.9 16.9 %collective-permute-done.18.refs_7_.refs_10_ = bf16[512,1024]{1,0:T(8,128)(2,1)S(1)} collective-permute-done((bf16[512,1024]{1,0:T(8,128)(2,1)}, bf16[512,1024]{1,0:T(8,128)(2,1)S(1)}, u32[]{:S(2)}, u32[]{:S(2)}) %collective-permute-start.18) | collective-permute-done | bytes 1048608 | tf_op jit(solution)/shard_map/ppermute | solution.py:363
  209.8 5.1 collective-permute-start.21
  216.4 17.5 %shard_map.258 = (bf16[2048,1024]{1,0:T(8,128)(2,1)}, bf16[2048,1024]{1,0:T(8,128)(2,1)}) custom-call(s32[1]{0:T(128)} %bitcast.1.index_ref, bf16[2048,2048]{1,0:T(8,128)(2,1)} %get-tuple-element.288.refs_0_, bf16[512,1024]{1,0:T(8,128)(2,1)} %copy-done.14, bf16[512,1024]{1,0:T(8,128)(2,1)} %copy-done.13, ...), custom_call_target="tpu_custom_call" | custom-call | flops 134217728 | bytes 376896 | tf_op jit(solution)/shard_map/pallas_call | solution.py:69
  233.9 14.2 %shard_map.259 = bf16[4,2,256,1024]{3,2,1,0:T(8,128)(2,1)} custom-call(bf16[2048,2048]{1,0:T(8,128)(2,1)} %shard_map.255.g_ref.refs_2_.refs_0_, bf16[2048,1024]{1,0:T(8,128)(2,1)} %get-tuple-element.289.refs_1_.refs_2_), custom_call_target="tpu_custom_call" | custom-call | flops 134217728 | bytes 262144 | tf_op jit(solution)/shard_map/pallas_call | solution.py:69
  266.2 8.3 %collective-permute-done.25 = bf16[2,256,1024]{2,1,0:T(8,128)(2,1)} collective-permute-done((bf16[2,256,1024]{2,1,0:T(8,128)(2,1)}, bf16[2,256,1024]{2,1,0:T(8,128)(2,1)}, u32[]{:S(2)}, u32[]{:S(2)}) %collective-permute-start.25) | collective-permute-done | bytes 1048608 | tf_op jit(solution)/shard_map/ppermute | solution.py:335
  274.5 7.2 %collective-permute-done.24.refs_6_.refs_8_ = bf16[256,2048]{1,0:T(8,128)(2,1)} collective-permute-done((bf16[256,2048]{1,0:T(8,128)(2,1)S(1)}, bf16[256,2048]{1,0:T(8,128)(2,1)}, u32[]{:S(2)}, u32[]{:S(2)}) %collective-permute-start.24) | collective-permute-done | bytes 1048608 | tf_op jit(solution)/shard_map/ppermute | solution.py:363
  293.8 9.2 %collective-permute-done.29 = bf16[2,256,1024]{2,1,0:T(8,128)(2,1)} collective-permute-done((bf16[2,256,1024]{2,1,0:T(8,128)(2,1)}, bf16[2,256,1024]{2,1,0:T(8,128)(2,1)}, u32[]{:S(2)}, u32[]{:S(2)}) %collective-permute-start.29) | collective-permute-done | bytes 1048608 | tf_op jit(solution)/shard_map/ppermute | solution.py:335
  303.1 7.4 %collective-permute-done.28.refs_7_.refs_9_ = bf16[256,2048]{1,0:T(8,128)(2,1)S(1)} collective-permute-done((bf16[256,2048]{1,0:T(8,128)(2,1)}, bf16[256,2048]{1,0:T(8,128)(2,1)S(1)}, u32[]{:S(2)}, u32[]{:S(2)}) %collective-permute-start.28) | collective-permute-done | bytes 1048608 | tf_op jit(solution)/shard_map/ppermute | solution.py:363
  319.5 11.1 %shard_map.261 = bf16[1,4,1024,512]{3,2,1,0:T(8,128)(2,1)} custom-call(s32[1]{0:T(128)} %bitcast.1.index_ref, bf16[2048,256]{1,0:T(8,128)(2,1)} %get-tuple-element.295.refs_3_.refs_0_, bf16[256,2048]{1,0:T(8,128)(2,1)} %all-gather.5.cloned.1.call-done.dense_ref.refs_1_, bf16[2048,1024]{1,0:T(8,128)(2,1)} %get-tuple-element.289.refs_1_.refs_2_, ...), custom_call_target="tpu_custom_call" | custom-call | flops 83886080 | bytes 278528 | tf_op jit(solution)/shard_map/pallas_call | solution.py:69
  330.6 15.2 %shard_map.260 = (bf16[2048,1024]{1,0:T(8,128)(2,1)}, f32[1,1024]{1,0:T(1,128)}) custom-call(s32[1]{0:T(128)} %bitcast.1.index_ref, bf16[2048,2048]{1,0:T(8,128)(2,1)} %shard_map.255.g_ref.refs_2_.refs_0_, bf16[256,2048]{1,0:T(8,128)(2,1)} %copy-done.10, bf16[256,2048]{1,0:T(8,128)(2,1)} %copy-done.9, bf16[256,2048]{1,0:T(8,128)(2,1)} %copy-done.8, ...), custom_call_target="tpu_custom_call" | custom-call | flops 134217728 | bytes 376896 | tf_op jit(solution)/shard_map/pallas_call | solution.py:69
  356.8 14.1 %shard_map.262 = bf16[4,2,256,1024]{3,2,1,0:T(8,128)(2,1)} custom-call(bf16[2048,2048]{1,0:T(8,128)(2,1)} %get-tuple-element.288.refs_0_, bf16[2048,1024]{1,0:T(8,128)(2,1)} %get-tuple-element.305.refs_1_.refs_3_), custom_call_target="tpu_custom_call" | custom-call | flops 134217728 | bytes 262144 | tf_op jit(solution)/shard_map/pallas_call | solution.py:69
  372.8 5.6 %collective-permute-start.36 = (bf16[2,256,1024]{2,1,0:T(8,128)(2,1)S(1)}, bf16[2,256,1024]{2,1,0:T(8,128)(2,1)}, u32[]{:S(2)}, u32[]{:S(2)}) collective-permute-start(bf16[2,256,1024]{2,1,0:T(8,128)(2,1)S(1)} %get-tuple-element.299), channel_id=1, source_target_pairs={{0,2},{1,3},{8,10},{9,11},{16,18},{17,19},{24,26},{25,27}} | collective-permute-start | bytes 3145736 | tf_op jit(solution)/shard_map/ppermute | solution.py:335
  380.1 11.6 %shard_map.264 = bf16[1,4,1024,512]{3,2,1,0:T(8,128)(2,1)} custom-call(s32[1]{0:T(128)} %bitcast.1.index_ref, bf16[2048,256]{1,0:T(8,128)(2,1)} %get-tuple-element.295.refs_3_.refs_0_, bf16[256,2048]{1,0:T(8,128)(2,1)} %all-gather.5.cloned.1.call-done.dense_ref.refs_1_, bf16[2048,1024]{1,0:T(8,128)(2,1)} %get-tuple-element.289.refs_1_.refs_2_, ...), custom_call_target="tpu_custom_call" | custom-call | flops 83886080 | bytes 344064 | tf_op jit(solution)/shard_map/pallas_call | solution.py:69
  391.8 18.9 %shard_map.263 = (bf16[2,4,512,512]{3,2,1,0:T(8,128)(2,1)}, f32[4,2048]{1,0:T(4,128)}) custom-call(s32[1]{0:T(128)} %bitcast.1.index_ref, bf16[1024,2048]{1,0:T(8,128)(2,1)} %collective-permute-done.other_ref.refs_0_, bf16[2048,768]{1,0:T(8,128)(2,1)} %get-tuple-element.306.refs_1_, bf16[2048,768]{1,0:T(8,128)(2,1)} %all-gather.3.cloned.1.call-done.joined_ref.refs_2_, ...), custom_call_target="tpu_custom_call" | custom-call | flops 117440512 | bytes 410368 | tf_op jit(solution)/shard_map/pallas_call | solution.py:69
  417.7 4.9 fusion.7
  422.6 19.7 %shard_map.265 = (bf16[2,4,512,512]{3,2,1,0:T(8,128)(2,1)}, f32[4,2048]{1,0:T(4,128)}) custom-call(s32[1]{0:T(128)} %bitcast.1.index_ref, bf16[1024,2048]{1,0:T(8,128)(2,1)} %bitcast.116, bf16[2048,768]{1,0:T(8,128)(2,1)} %get-tuple-element.306.refs_1_, bf16[2048,768]{1,0:T(8,128)(2,1)} %all-gather.3.cloned.1.call-done.joined_ref.refs_2_, ...), custom_call_target="tpu_custom_call" | custom-call | flops 117440512 | bytes 475904 | tf_op jit(solution)/shard_map/pallas_call | solution.py:69
  446.2 5.4 collective-permute-start.46
  467.6 5.7 %collective-permute-done.46 = bf16[2,256,1024]{2,1,0:T(8,128)(2,1)} collective-permute-done((bf16[2,256,1024]{2,1,0:T(8,128)(2,1)}, bf16[2,256,1024]{2,1,0:T(8,128)(2,1)}, u32[]{:S(2)}, u32[]{:S(2)}) %collective-permute-start.46) | collective-permute-done | bytes 1048608 | tf_op jit(solution)/shard_map/ppermute | solution.py:335
  473.3 13.9 %collective-permute-done.41 = bf16[2,512,512]{2,1,0:T(8,128)(2,1)} collective-permute-done((bf16[2,512,512]{2,1,0:T(8,128)(2,1)}, bf16[2,512,512]{2,1,0:T(8,128)(2,1)}, u32[]{:S(2)}, u32[]{:S(2)}) %collective-permute-start.41) | collective-permute-done | bytes 1048608 | tf_op jit(solution)/shard_map/ppermute | solution.py:423
  496.4 5.6 collective-permute-start.53
  507.2 9.7 %collective-permute-done.49 = bf16[512,512]{1,0:T(8,128)(2,1)S(1)} collective-permute-done((bf16[512,512]{1,0:T(8,128)(2,1)S(1)}, bf16[512,512]{1,0:T(8,128)(2,1)S(1)}, u32[]{:S(2)}, u32[]{:S(2)}) %collective-permute-start.49) | collective-permute-done | bytes 524320 | tf_op jit(solution)/shard_map/ppermute | solution.py:423
  (265 shorter events, 184.5 us)
Async XLA Ops:
  7.2 83.8 %all-gather.3.cloned.1.call-start = ((), (), s32[]{:S(2)}) async-start(), calls=%async_computation.4 | async-start | bytes 3932160 | tf_op jit(solution)/shard_map/all_gather | solution.py:444
  11.7 104.7 %all-gather.5.cloned.1.call-start = ((), (), s32[]{:S(2)}) async-start(), calls=%async_computation.5 | async-start | bytes 1310720 | tf_op jit(solution)/shard_map/all_gather | solution.py:444
  11.7 28.1 %collective-permute-start = (bf16[1024,2048]{1,0:T(8,128)(2,1)}, bf16[1024,2048]{1,0:T(8,128)(2,1)}, u32[]{:S(2)}, u32[]{:S(2)}) collective-permute-start(bf16[1024,2048]{1,0:T(8,128)(2,1)} %bitcast.114), channel_id=1, source_target_pairs={{0,1},{1,0},{2,3},{3,2},{4,5},{5,4},{6,7},{7,6},{8,9},{9,8},{10,11... | collective-permute-start | bytes 12582920 | tf_op jit(solution)/shard_map/ppermute | solution.py:423
  12.1 61.6 %collective-permute-start.7 = (bf16[1024,512]{1,0:T(8,128)(2,1)}, bf16[1024,512]{1,0:T(8,128)(2,1)}, u32[]{:S(2)}, u32[]{:S(2)}) collective-permute-start(bf16[1024,512]{1,0:T(8,128)(2,1)} %bitcast.6.refs_0_), channel_id=1, source_target_pairs={{0,24},{8,16},{16,8},{24,0},{1,25},{9,17},{17,9},{25,1},{2,26},{10... | collective-permute-start | bytes 3145736 | tf_op jit(solution)/shard_map/ppermute | solution.py:423
  15.7 58.0 %collective-permute-start.6 = (bf16[1024,512]{1,0:T(8,128)(2,1)}, bf16[1024,512]{1,0:T(8,128)(2,1)}, u32[]{:S(2)}, u32[]{:S(2)}) collective-permute-start(bf16[1024,512]{1,0:T(8,128)(2,1)} %bitcast.6.refs_0_), channel_id=1, source_target_pairs={{0,16},{16,0},{1,17},{17,1},{2,18},{18,2},{3,19},{19,3},{4,20},{20... | collective-permute-start | bytes 3145736 | tf_op jit(solution)/shard_map/ppermute | solution.py:423
  37.5 36.2 %collective-permute-start.5 = (bf16[1024,512]{1,0:T(8,128)(2,1)}, bf16[1024,512]{1,0:T(8,128)(2,1)}, u32[]{:S(2)}, u32[]{:S(2)}) collective-permute-start(bf16[1024,512]{1,0:T(8,128)(2,1)} %bitcast.6.refs_0_), channel_id=1, source_target_pairs={{0,8},{8,0},{1,9},{9,1},{2,10},{10,2},{3,11},{11,3},{4,12},{12,4},... | collective-permute-start | bytes 3145736 | tf_op jit(solution)/shard_map/ppermute | solution.py:423
  42.7 29.5 %collective-permute-start.8 = (bf16[256,1024]{1,0:T(8,128)(2,1)}, bf16[256,1024]{1,0:T(8,128)(2,1)}, u32[]{:S(2)}, u32[]{:S(2)}) collective-permute-start(bf16[256,1024]{1,0:T(8,128)(2,1)} %pad_maximum_fusion.1), channel_id=1, source_target_pairs={{0,1},{1,0},{2,3},{3,2},{4,5},{5,4},{6,7},{7,6},{8,9},{9,8},{10,11... | collective-permute-start | bytes 1572872 | tf_op jit(solution)/shard_map/ppermute | solution.py:423
  116.3 34.2 %collective-permute-start.14 = (bf16[512,1024]{1,0:T(8,128)(2,1)S(1)}, bf16[512,1024]{1,0:T(8,128)(2,1)S(1)}, u32[]{:S(2)}, u32[]{:S(2)}) collective-permute-start(bf16[512,1024]{1,0:T(8,128)(2,1)S(1)} %maximum_select_fusion.refs_4_.refs_7_), channel_id=1, source_target_pairs={{2,0},{4,2},{6,4},{3,1},{5,3},{7,5},{10,8},{12,10},{14,12},{11,9},... | collective-permute-start | bytes 3145736 | tf_op jit(solution)/shard_map/ppermute | solution.py:363
  117.6 33.0 %collective-permute-start.13 = (bf16[512,1024]{1,0:T(8,128)(2,1)S(1)}, bf16[512,1024]{1,0:T(8,128)(2,1)}, u32[]{:S(2)}, u32[]{:S(2)}) collective-permute-start(bf16[512,1024]{1,0:T(8,128)(2,1)S(1)} %maximum_select_fusion.refs_4_.refs_7_), channel_id=1, source_target_pairs={{0,2},{2,4},{4,6},{1,3},{3,5},{5,7},{8,10},{10,12},{12,14},{9,11},... | collective-permute-start | bytes 3145736 | tf_op jit(solution)/shard_map/ppermute | solution.py:362
  151.3 27.2 %collective-permute-start.16 = (bf16[512,1024]{1,0:T(8,128)(2,1)S(1)}, bf16[512,1024]{1,0:T(8,128)(2,1)}, u32[]{:S(2)}, u32[]{:S(2)}) collective-permute-start(bf16[512,1024]{1,0:T(8,128)(2,1)S(1)} %collective-permute-done.14.refs_5_.refs_8_), channel_id=1, source_target_pairs={{2,0},{4,2},{3,1},{5,3},{10,8},{12,10},{11,9},{13,11},{18,16},{20,... | collective-permute-start | bytes 3145736 | tf_op jit(solution)/shard_map/ppermute | solution.py:363
  179.2 25.5 %collective-permute-start.18 = (bf16[512,1024]{1,0:T(8,128)(2,1)}, bf16[512,1024]{1,0:T(8,128)(2,1)S(1)}, u32[]{:S(2)}, u32[]{:S(2)}) collective-permute-start(bf16[512,1024]{1,0:T(8,128)(2,1)} %collective-permute-done.16.refs_6_.refs_9_), channel_id=1, source_target_pairs={{2,0},{3,1},{10,8},{11,9},{18,16},{19,17},{26,24},{27,25}} | collective-permute-start | bytes 3145736 | tf_op jit(solution)/shard_map/ppermute | solution.py:363
  183.2 25.3 %collective-permute-start.19 = (bf16[2,256,1024]{2,1,0:T(8,128)(2,1)S(1)}, bf16[2,256,1024]{2,1,0:T(8,128)(2,1)S(1)}, u32[]{:S(2)}, u32[]{:S(2)}) collective-permute-start(bf16[2,256,1024]{2,1,0:T(8,128)(2,1)S(1)} %get-tuple-element.367), channel_id=1, source_target_pairs={{0,2},{1,3},{8,10},{9,11},{16,18},{17,19},{24,26},{25,27}} | collective-permute-start | bytes 3145736 | tf_op jit(solution)/shard_map/ppermute | solution.py:335
  208.4 42.7 %collective-permute-start.22 = (bf16[256,2048]{1,0:T(8,128)(2,1)S(1)}, bf16[256,2048]{1,0:T(8,128)(2,1)S(1)}, u32[]{:S(2)}, u32[]{:S(2)}) collective-permute-start(bf16[256,2048]{1,0:T(8,128)(2,1)S(1)} %constant_dynamic-slice_fusion.refs_4_.refs_6_), channel_id=1, source_target_pairs={{2,0},{4,2},{6,4},{3,1},{5,3},{7,5},{10,8},{12,10},{14,12},{11,9},... | collective-permute-start | bytes 3145736 | tf_op jit(solution)/shard_map/ppermute | solution.py:363
  209.8 41.4 %collective-permute-start.21 = (bf16[256,2048]{1,0:T(8,128)(2,1)S(1)}, bf16[256,2048]{1,0:T(8,128)(2,1)S(1)}, u32[]{:S(2)}, u32[]{:S(2)}) collective-permute-start(bf16[256,2048]{1,0:T(8,128)(2,1)S(1)} %constant_dynamic-slice_fusion.refs_4_.refs_6_), channel_id=1, source_target_pairs={{0,2},{2,4},{4,6},{1,3},{3,5},{5,7},{8,10},{10,12},{12,14},{9,11},... | collective-permute-start | bytes 3145736 | tf_op jit(solution)/shard_map/ppermute | solution.py:362
  251.1 23.3 %collective-permute-start.25 = (bf16[2,256,1024]{2,1,0:T(8,128)(2,1)}, bf16[2,256,1024]{2,1,0:T(8,128)(2,1)}, u32[]{:S(2)}, u32[]{:S(2)}) collective-permute-start(bf16[2,256,1024]{2,1,0:T(8,128)(2,1)} %get-tuple-element.244), channel_id=1, source_target_pairs={{0,2},{1,3},{8,10},{9,11},{16,18},{17,19},{24,26},{25,27}} | collective-permute-start | bytes 3145736 | tf_op jit(solution)/shard_map/ppermute | solution.py:335
  258.3 23.4 %collective-permute-start.24 = (bf16[256,2048]{1,0:T(8,128)(2,1)S(1)}, bf16[256,2048]{1,0:T(8,128)(2,1)}, u32[]{:S(2)}, u32[]{:S(2)}) collective-permute-start(bf16[256,2048]{1,0:T(8,128)(2,1)S(1)} %collective-permute-done.22.refs_5_.refs_7_), channel_id=1, source_target_pairs={{2,0},{4,2},{3,1},{5,3},{10,8},{12,10},{11,9},{13,11},{18,16},{20,... | collective-permute-start | bytes 3145736 | tf_op jit(solution)/shard_map/ppermute | solution.py:363
  313.4 32.4 %collective-permute-start.32 = (bf16[2,256,1024]{2,1,0:T(8,128)(2,1)S(1)}, bf16[2,256,1024]{2,1,0:T(8,128)(2,1)S(1)}, u32[]{:S(2)}, u32[]{:S(2)}) collective-permute-start(bf16[2,256,1024]{2,1,0:T(8,128)(2,1)S(1)} %get-tuple-element.358), channel_id=1, source_target_pairs={{6,4},{4,2},{2,0},{7,5},{5,3},{3,1},{14,12},{12,10},{10,8},{15,13}... | collective-permute-start | bytes 3145736 | tf_op jit(solution)/shard_map/ppermute | solution.py:336
  314.7 31.1 %collective-permute-start.31 = (bf16[2,256,1024]{2,1,0:T(8,128)(2,1)S(1)}, bf16[2,256,1024]{2,1,0:T(8,128)(2,1)S(1)}, u32[]{:S(2)}, u32[]{:S(2)}) collective-permute-start(bf16[2,256,1024]{2,1,0:T(8,128)(2,1)S(1)} %get-tuple-element.359), channel_id=1, source_target_pairs={{0,2},{2,4},{4,6},{1,3},{3,5},{5,7},{8,10},{10,12},{12,14},{9,11},... | collective-permute-start | bytes 3145736 | tf_op jit(solution)/shard_map/ppermute | solution.py:335
  345.8 27.0 %collective-permute-start.33 = (bf16[1,4,1024,512]{3,2,1,0:T(8,128)(2,1)}, bf16[1,4,1024,512]{3,2,1,0:T(8,128)(2,1)}, u32[]{:S(2)}, u32[]{:S(2)}) collective-permute-start(bf16[1,4,1024,512]{3,2,1,0:T(8,128)(2,1)} %shard_map.261), channel_id=1, source_target_pairs={{0,1},{1,0},{2,3},{3,2},{4,5},{5,4},{6,7},{7,6},{8,9},{9,8},{10,11... | collective-permute-start | bytes 12582920 | tf_op jit(solution)/shard_map/ppermute | solution.py:423
  345.9 26.9 %collective-permute-start.34 = (bf16[2,256,1024]{2,1,0:T(8,128)(2,1)}, bf16[2,256,1024]{2,1,0:T(8,128)(2,1)}, u32[]{:S(2)}, u32[]{:S(2)}) collective-permute-start(bf16[2,256,1024]{2,1,0:T(8,128)(2,1)} %get-tuple-element.286), channel_id=1, source_target_pairs={{0,2},{2,4},{1,3},{3,5},{8,10},{10,12},{9,11},{11,13},{16,18},{18,... | collective-permute-start | bytes 3145736 | tf_op jit(solution)/shard_map/ppermute | solution.py:335
  348.7 24.0 %collective-permute-start.35 = (bf16[2,256,1024]{2,1,0:T(8,128)(2,1)}, bf16[2,256,1024]{2,1,0:T(8,128)(2,1)}, u32[]{:S(2)}, u32[]{:S(2)}) collective-permute-start(bf16[2,256,1024]{2,1,0:T(8,128)(2,1)} %get-tuple-element.287), channel_id=1, source_target_pairs={{6,4},{4,2},{7,5},{5,3},{14,12},{12,10},{15,13},{13,11},{22,20},{2... | collective-permute-start | bytes 3145736 | tf_op jit(solution)/shard_map/ppermute | solution.py:336
  356.7 191.4 %reduce-scatter.4.cloned.1.call-start = ((), (), s32[]{:S(2)}) async-start(), calls=%async_computation.6 | async-start | bytes 5242880
  372.8 41.8 %collective-permute-start.36 = (bf16[2,256,1024]{2,1,0:T(8,128)(2,1)S(1)}, bf16[2,256,1024]{2,1,0:T(8,128)(2,1)}, u32[]{:S(2)}, u32[]{:S(2)}) collective-permute-start(bf16[2,256,1024]{2,1,0:T(8,128)(2,1)S(1)} %get-tuple-element.299), channel_id=1, source_target_pairs={{0,2},{1,3},{8,10},{9,11},{16,18},{17,19},{24,26},{25,27}} | collective-permute-start | bytes 3145736 | tf_op jit(solution)/shard_map/ppermute | solution.py:335
  378.4 36.1 %collective-permute-start.37 = (bf16[2,256,1024]{2,1,0:T(8,128)(2,1)S(1)}, bf16[2,256,1024]{2,1,0:T(8,128)(2,1)}, u32[]{:S(2)}, u32[]{:S(2)}) collective-permute-start(bf16[2,256,1024]{2,1,0:T(8,128)(2,1)S(1)} %get-tuple-element.300), channel_id=1, source_target_pairs={{6,4},{7,5},{14,12},{15,13},{22,20},{23,21},{30,28},{31,29}} | collective-permute-start | bytes 3145736 | tf_op jit(solution)/shard_map/ppermute | solution.py:336
  414.7 27.7 %collective-permute-start.39 = (bf16[2,256,1024]{2,1,0:T(8,128)(2,1)}, bf16[2,256,1024]{2,1,0:T(8,128)(2,1)S(1)}, u32[]{:S(2)}, u32[]{:S(2)}) collective-permute-start(bf16[2,256,1024]{2,1,0:T(8,128)(2,1)} %get-tuple-element.313), channel_id=1, source_target_pairs={{0,2},{2,4},{4,6},{1,3},{3,5},{5,7},{8,10},{10,12},{12,14},{9,11},... | collective-permute-start | bytes 3145736 | tf_op jit(solution)/shard_map/ppermute | solution.py:335
  416.2 27.4 %collective-permute-start.40 = (bf16[2,256,1024]{2,1,0:T(8,128)(2,1)S(1)}, bf16[2,256,1024]{2,1,0:T(8,128)(2,1)S(1)}, u32[]{:S(2)}, u32[]{:S(2)}) collective-permute-start(bf16[2,256,1024]{2,1,0:T(8,128)(2,1)S(1)} %copy-done.30), channel_id=1, source_target_pairs={{6,4},{4,2},{2,0},{7,5},{5,3},{3,1},{14,12},{12,10},{10,8},{15,13}... | collective-permute-start | bytes 3145736 | tf_op jit(solution)/shard_map/ppermute | solution.py:336
  446.2 27.1 %collective-permute-start.46 = (bf16[2,256,1024]{2,1,0:T(8,128)(2,1)}, bf16[2,256,1024]{2,1,0:T(8,128)(2,1)}, u32[]{:S(2)}, u32[]{:S(2)}) collective-permute-start(bf16[2,256,1024]{2,1,0:T(8,128)(2,1)} %get-tuple-element.326), channel_id=1, source_target_pairs={{0,2},{2,4},{1,3},{3,5},{8,10},{10,12},{9,11},{11,13},{16,18},{18,... | collective-permute-start | bytes 3145736 | tf_op jit(solution)/shard_map/ppermute | solution.py:335
  456.8 30.4 %collective-permute-start.41 = (bf16[2,512,512]{2,1,0:T(8,128)(2,1)}, bf16[2,512,512]{2,1,0:T(8,128)(2,1)}, u32[]{:S(2)}, u32[]{:S(2)}) collective-permute-start(bf16[2,512,512]{2,1,0:T(8,128)(2,1)} %dynamic-slice_bitcast_fusion.1), channel_id=1, source_target_pairs={{0,16},{16,0},{1,17},{17,1},{2,18},{18,2},{3,19},{19,3},{4,20},{20... | collective-permute-start | bytes 3145736 | tf_op jit(solution)/shard_map/ppermute | solution.py:423
  459.2 28.0 %collective-permute-start.42 = (bf16[2,512,512]{2,1,0:T(8,128)(2,1)}, bf16[2,512,512]{2,1,0:T(8,128)(2,1)S(1)}, u32[]{:S(2)}, u32[]{:S(2)}) collective-permute-start(bf16[2,512,512]{2,1,0:T(8,128)(2,1)} %dynamic-slice_bitcast_fusion), channel_id=1, source_target_pairs={{0,8},{8,0},{1,9},{9,1},{2,10},{10,2},{3,11},{11,3},{4,12},{12,4},... | collective-permute-start | bytes 3145736 | tf_op jit(solution)/shard_map/ppermute | solution.py:423
  464.0 43.2 %all-to-all-start.1 = ((bf16[4,128,1024]{2,1,0:T(8,128)(2,1)}), bf16[4,128,1024]{2,1,0:T(8,128)(2,1)S(1)}, u32[]{:S(2)}, u32[]{:S(2)}) async-start(bf16[4,128,1024]{2,1,0:T(8,128)(2,1)} %bitcast.36), calls=%async_computation.1 | async-start | bytes 2097152 | tf_op jit(solution)/shard_map/all_to_all | solution.py:620
  495.2 25.6 %collective-permute-start.54 = (bf16[2,256,1024]{2,1,0:T(8,128)(2,1)}, bf16[2,256,1024]{2,1,0:T(8,128)(2,1)}, u32[]{:S(2)}, u32[]{:S(2)}) collective-permute-start(bf16[2,256,1024]{2,1,0:T(8,128)(2,1)} %get-tuple-element.346), channel_id=1, source_target_pairs={{6,4},{4,2},{2,0},{7,5},{5,3},{3,1},{14,12},{12,10},{10,8},{15,13}... | collective-permute-start | bytes 3145736 | tf_op jit(solution)/shard_map/ppermute | solution.py:336
  496.4 25.5 %collective-permute-start.53 = (bf16[2,256,1024]{2,1,0:T(8,128)(2,1)}, bf16[2,256,1024]{2,1,0:T(8,128)(2,1)}, u32[]{:S(2)}, u32[]{:S(2)}) collective-permute-start(bf16[2,256,1024]{2,1,0:T(8,128)(2,1)} %get-tuple-element.347), channel_id=1, source_target_pairs={{0,2},{2,4},{4,6},{1,3},{3,5},{5,7},{8,10},{10,12},{12,14},{9,11},... | collective-permute-start | bytes 3145736 | tf_op jit(solution)/shard_map/ppermute | solution.py:335
  (70 other events, 1050.8 us)
Sparse Core Ops, SparseCore 0:
  11.8 70.6 all-gather.2
  84.0 32.2 all-gather.4
  414.8 55.5 reduce-scatter.3
